TPU v7x, 32 devices: a whole 2x2x4 slice. The times are simulated.
32 devices in a mesh: dp: 16 (over z, y, x), mp: 2 (over core).
Axes of the slice: x: 2, y: 2, z: 4, core: 2. Of those that a mesh axis runs over, the one named last changes fastest.
Arguments:
- tokens_in: bfloat16 [2048, 8192], P('dp', 'mp'), may hold values from -6 to 6
- gate_pre: bfloat16 [2048, 28672], P('dp', 'mp'), may hold values from -8 to 8
- up_pre: bfloat16 [2048, 28672], P('dp', 'mp'), may hold values from -6 to 6
- hidden_grad: bfloat16 [2048, 28672], P('dp', 'mp'), may hold values from -160 to 160
- out_grad: bfloat16 [2048, 8192], P('dp', 'mp'), may hold values from -160 to 160
- proj_model: bfloat16 [8192, 128], P('mp'), may hold values from -0.0625 to 0.0625
- proj_hidden: bfloat16 [28672, 128], P('mp'), may hold values from -0.03125 to 0.03125
Outputs:
- whitened: float32 [16, 128, 64], P('dp', 'mp')
All inputs are finite; a program needn't handle non-finite values.
Results may differ from a plain program's by a relative error of at most 0.003.
Values sent between devices are 32-bit elements; how exact they have to be, the bound alone decides.
No kernel may reach another device: no remote copies, remote signals or barrier semaphores. Data moves between devices by JAX's collectives and lax.ppermute only.
A program may use at most 64 MiB of HBM per device.

v0:
```python
import math

import jax
import jax.numpy as jnp
from jax import lax
from jax.sharding import PartitionSpec as P

RANK = 64
LEN = 128


highest = lax.Precision.HIGHEST


def partner_2(value, axis, apart):
    mask = 2**apart
    pairs = [(source, source ^ mask) for source in range(lax.axis_size(axis))]
    return lax.ppermute(value, axis, pairs)


def gradient_blocks(projected):
    columns_each = projected.shape[-1] // 4
    input_side = projected[..., :columns_each]
    output_side = projected[..., columns_each : 2 * columns_each]
    upward = projected[..., 2 * columns_each : 3 * columns_each]
    hidden_side = projected[..., 3 * columns_each :]
    up_block = jnp.einsum("elr,els->ers", input_side, upward, precision=highest)
    down_block = jnp.einsum("elr,els->ers", hidden_side, output_side, precision=highest)
    return jnp.concatenate([up_block, down_block], axis=1)


def gram_of(rows):
    flat_rows = rows.reshape(-1, rows.shape[-1])
    return jnp.dot(flat_rows.T, flat_rows, precision=highest, preferred_element_type=jnp.float32)


def shards(tokens_in, gate_pre, up_pre, hidden_grad, out_grad, proj_model, proj_hidden):
    gate_act = jax.nn.silu(gate_pre.astype(jnp.float32))
    up_grad = (hidden_grad.astype(jnp.float32) * gate_act).astype(jnp.bfloat16)
    hidden = (gate_act * up_pre.astype(jnp.float32)).astype(jnp.bfloat16)
    local_sums = jnp.concatenate(
        [
            jnp.dot(tokens_in, proj_model[:, :RANK], preferred_element_type=jnp.float32),
            jnp.dot(out_grad, proj_model[:, RANK:], preferred_element_type=jnp.float32),
            jnp.dot(up_grad, proj_hidden[:, :RANK], preferred_element_type=jnp.float32),
            jnp.dot(hidden, proj_hidden[:, RANK:], preferred_element_type=jnp.float32),
        ],
        axis=1,
    )
    local_examples = tokens_in.shape[0] // LEN
    shaped = local_sums.reshape(local_examples, LEN, 4 * RANK)
    model_shards = lax.axis_size("mp")
    rows_each = 2 * RANK // model_shards
    summed = lax.psum(shaped, "mp")
    blocks = gradient_blocks(summed)
    mine = lax.dynamic_slice_in_dim(blocks, lax.axis_index("mp") * rows_each, rows_each, 1)
    group_gram = gram_of(blocks)
    flat_mine = mine.reshape(local_examples * rows_each, RANK)
    lower = jnp.linalg.cholesky(group_gram)
    for level in range(lax.axis_size("dp").bit_length() - 1):
        partner = partner_2(lower, "dp", level)
        combined = jnp.dot(
            lower, lower.T, precision=highest, preferred_element_type=jnp.float32
        ) + jnp.dot(partner, partner.T, precision=highest, preferred_element_type=jnp.float32)
        lower = jnp.linalg.cholesky(combined)
    solved = jax.scipy.linalg.solve_triangular(lower, flat_mine.T, lower=True)
    factor = math.sqrt(local_examples * lax.axis_size("dp") * 2 * RANK)
    return (solved.T * factor).reshape(local_examples, rows_each, RANK)


def solution(mesh):
    in_specs = (
        P("dp", "mp"),
        P("dp", "mp"),
        P("dp", "mp"),
        P("dp", "mp"),
        P("dp", "mp"),
        P("mp", None),
        P("mp", None),
    )
    out_specs = P("dp", "mp", None)
    return jax.shard_map(shards, mesh=mesh, in_specs=in_specs, out_specs=out_specs, check_vma=False)
```

profile of v0, /device:TPU:0, one launch (start us, length us, event | category | flops | bytes accessed | tf_op | source)
XLA Modules:
  0.0 109.5 jit_solution(18162307442310419931)
XLA Ops:
  6.5 0.0 copy-start
  6.5 0.0 all-reduce.2.cloned.1.call-start
  6.5 0.0 copy-start.3
  6.5 0.0 copy-start.4
  6.5 0.0 copy-start.5
  6.6 7.1 %fusion.3 = f32[128,64]{0,1:T(8,128)S(1)} fusion(bf16[128,14336]{1,0:T(8,128)(2,1)} %param.11, bf16[14336,128]{1,0:T(8,128)(2,1)} %param.14, bf16[128,14336]{1,0:T(8,128)(2,1)} %param.9), kind=kOutput, calls=%fused_computation.7 | convolution fusion | flops 249561088 | bytes 11042816 | tf_op jit(solution)/shard_map/dot_general | solution.py:45
  13.7 0.0 copy-done.3
  13.7 0.0 copy-done.4
  13.7 0.3 copy-done.5
  14.0 0.0 copy-start.1
  14.0 0.0 copy-start.2
  14.0 3.5 %fusion.4 = f32[128,64]{0,1:T(8,128)S(1)} fusion(bf16[128,14336]{1,0:T(8,128)(2,1)S(1)} %copy-done.3, bf16[14336,128]{1,0:T(8,128)(2,1)S(1)} %copy-done.4, bf16[128,14336]{1,0:T(8,128)(2,1)S(1)} %copy-done.5), kind=kOutput, calls=%fused_computation.8 | convolution fusion | flops 249561088 | bytes 11042816 | tf_op jit(solution)/shard_map/dot_general | solution.py:46
  17.6 0.0 copy-done
  17.6 0.0 copy-done.1
  17.6 0.6 fusion.10
  18.2 0.0 copy-done.2
  18.2 1.0 fusion.8
  19.2 0.7 maximum_bitcast_fusion
  19.9 0.0 all-reduce.2.cloned.1.call-update
  19.9 20.7 %all-reduce.2.cloned.1.call-done = f32[1,128,256]{1,2,0:T(8,128)} async-done(((f32[1,128,256]{1,2,0:T(8,128)}), f32[1,128,256]{1,2,0:T(8,128)}) %all-reduce.2.cloned.1.call-update) | async-done | bytes 131088 | tf_op jit(solution)/shard_map/psum | solution.py:54
  40.6 1.0 convolution_bitcast_fusion
  41.6 1.0 convolution_bitcast_fusion.1
  42.6 0.3 fusion.15
  42.8 0.1 copy.8
  42.9 5.8 %cholesky.89 = f32[64,64]{1,0:T(8,128)S(1)} custom-call(f32[64,64]{1,0:T(8,128)S(1)} %fusion.21), custom_call_target="Cholesky" | custom-call | tf_op jit(solution)/shard_map/jit(cholesky)/cholesky | solution.py:59
  48.8 0.6 compare_reduce_fusion.4
  49.5 0.7 select_select_fusion.4
  50.1 1.8 %collective-permute-start = (f32[64,64]{1,0:T(8,128)S(1)}, f32[64,64]{1,0:T(8,128)S(1)}, u32[]{:S(2)}, u32[]{:S(2)}) collective-permute-start(f32[64,64]{1,0:T(8,128)S(1)} %select_select_fusion.4), channel_id=1, source_target_pairs={{0,2},{2,0},{4,6},{6,4},{8,10},{10,8},{12,14},{14,12},{16,18},{18,... | collective-permute-start | bytes 49160 | tf_op jit(solution)/shard_map/ppermute | solution.py:18
  51.9 0.2 fusion.39
  52.1 2.0 %collective-permute-done = f32[64,64]{1,0:T(8,128)S(1)} collective-permute-done((f32[64,64]{1,0:T(8,128)S(1)}, f32[64,64]{1,0:T(8,128)S(1)}, u32[]{:S(2)}, u32[]{:S(2)}) %collective-permute-start) | collective-permute-done | bytes 16416 | tf_op jit(solution)/shard_map/ppermute | solution.py:18
  54.1 0.2 convolution_add_fusion.3
  54.3 0.1 copy.11
  54.4 5.8 %cholesky.100 = f32[64,64]{1,0:T(8,128)S(1)} custom-call(f32[64,64]{1,0:T(8,128)S(1)} %fusion.20), custom_call_target="Cholesky" | custom-call | tf_op jit(solution)/shard_map/jit(cholesky)/cholesky | solution.py:65
  60.3 0.6 compare_reduce_fusion.3
  60.9 0.7 select_select_fusion.3
  61.6 1.8 %collective-permute-start.1 = (f32[64,64]{1,0:T(8,128)S(1)}, f32[64,64]{1,0:T(8,128)S(1)}, u32[]{:S(2)}, u32[]{:S(2)}) collective-permute-start(f32[64,64]{1,0:T(8,128)S(1)} %select_select_fusion.3), channel_id=1, source_target_pairs={{0,4},{2,6},{4,0},{6,2},{8,12},{10,14},{12,8},{14,10},{16,20},{18,... | collective-permute-start | bytes 49160 | tf_op jit(solution)/shard_map/ppermute | solution.py:18
  63.4 0.2 fusion.40
  63.6 2.0 %collective-permute-done.1 = f32[64,64]{1,0:T(8,128)S(1)} collective-permute-done((f32[64,64]{1,0:T(8,128)S(1)}, f32[64,64]{1,0:T(8,128)S(1)}, u32[]{:S(2)}, u32[]{:S(2)}) %collective-permute-start.1) | collective-permute-done | bytes 16416 | tf_op jit(solution)/shard_map/ppermute | solution.py:18
  65.5 0.2 convolution_add_fusion.2
  65.7 0.1 copy.14
  65.8 5.8 %cholesky.111 = f32[64,64]{1,0:T(8,128)S(1)} custom-call(f32[64,64]{1,0:T(8,128)S(1)} %fusion.19), custom_call_target="Cholesky" | custom-call | tf_op jit(solution)/shard_map/jit(cholesky)/cholesky | solution.py:65
  71.7 0.6 compare_reduce_fusion.2
  72.4 0.7 select_select_fusion.2
  73.0 1.8 %collective-permute-start.2 = (f32[64,64]{1,0:T(8,128)S(1)}, f32[64,64]{1,0:T(8,128)S(1)}, u32[]{:S(2)}, u32[]{:S(2)}) collective-permute-start(f32[64,64]{1,0:T(8,128)S(1)} %select_select_fusion.2), channel_id=1, source_target_pairs={{0,8},{2,10},{4,12},{6,14},{8,0},{10,2},{12,4},{14,6},{16,24},{18,... | collective-permute-start | bytes 49160 | tf_op jit(solution)/shard_map/ppermute | solution.py:18
  74.8 0.2 fusion.41
  75.0 2.0 %collective-permute-done.2 = f32[64,64]{1,0:T(8,128)S(1)} collective-permute-done((f32[64,64]{1,0:T(8,128)S(1)}, f32[64,64]{1,0:T(8,128)S(1)}, u32[]{:S(2)}, u32[]{:S(2)}) %collective-permute-start.2) | collective-permute-done | bytes 16416 | tf_op jit(solution)/shard_map/ppermute | solution.py:18
  77.0 0.2 convolution_add_fusion.1
  77.2 0.1 copy.17
  77.3 5.8 %cholesky.122 = f32[64,64]{1,0:T(8,128)S(1)} custom-call(f32[64,64]{1,0:T(8,128)S(1)} %fusion.18), custom_call_target="Cholesky" | custom-call | tf_op jit(solution)/shard_map/jit(cholesky)/cholesky | solution.py:65
  83.2 0.6 compare_reduce_fusion.1
  83.8 0.7 select_select_fusion.1
  84.5 2.7 %collective-permute-start.3 = (f32[64,64]{1,0:T(8,128)S(1)}, f32[64,64]{1,0:T(8,128)S(1)}, u32[]{:S(2)}, u32[]{:S(2)}) collective-permute-start(f32[64,64]{1,0:T(8,128)S(1)} %select_select_fusion.1), channel_id=1, source_target_pairs={{0,16},{2,18},{4,20},{6,22},{8,24},{10,26},{12,28},{14,30},{16,0},... | collective-permute-start | bytes 49160 | tf_op jit(solution)/shard_map/ppermute | solution.py:18
  87.2 0.2 fusion.42
  87.4 2.0 %collective-permute-done.3 = f32[64,64]{1,0:T(8,128)S(1)} collective-permute-done((f32[64,64]{1,0:T(8,128)S(1)}, f32[64,64]{1,0:T(8,128)S(1)}, u32[]{:S(2)}, u32[]{:S(2)}) %collective-permute-start.3) | collective-permute-done | bytes 16416 | tf_op jit(solution)/shard_map/ppermute | solution.py:18
  89.4 0.2 convolution_add_fusion
  89.5 0.1 copy.20
  89.6 5.8 %cholesky.133 = f32[64,64]{1,0:T(8,128)S(1)} custom-call(f32[64,64]{1,0:T(8,128)S(1)} %fusion.17), custom_call_target="Cholesky" | custom-call | tf_op jit(solution)/shard_map/jit(cholesky)/cholesky | solution.py:65
  95.5 0.6 compare_reduce_fusion
  96.2 0.7 fusion.12
  96.8 4.9 %custom-call.6 = f32[1,64,64]{1,2,0:T(8,128)S(1)} custom-call(f32[1,64,64]{2,1,0:T(8,128)S(1)} %fusion.12), custom_call_target="InvertDiagBlocksLowerTriangular" | custom-call | tf_op jit(solution)/shard_map/jit(_solve_triangular)/triangular_solve | solution.py:66
  101.7 0.9 fusion.7
  (10 shorter events, 0.2 us)
Async XLA Ops:
  6.5 11.0 %copy-start = (bf16[128,4096]{1,0:T(8,128)(2,1)S(1)}, bf16[128,4096]{1,0:T(8,128)(2,1)}, u32[]{:S(2)}) copy-start(bf16[128,4096]{1,0:T(8,128)(2,1)} %param.8) | copy-start | bytes 3145732
  6.5 34.1 %all-reduce.2.cloned.1.call-start = ((), (), s32[]{:S(2)}) async-start(), calls=%async_computation | async-start | bytes 262144 | tf_op jit(solution)/shard_map/psum | solution.py:54
  6.5 7.1 %copy-start.3 = (bf16[128,14336]{1,0:T(8,128)(2,1)S(1)}, bf16[128,14336]{1,0:T(8,128)(2,1)}, u32[]{:S(2)}) copy-start(bf16[128,14336]{1,0:T(8,128)(2,1)} %param.10) | copy-start | bytes 11010052
  6.5 7.1 %copy-start.4 = (bf16[14336,128]{1,0:T(8,128)(2,1)S(1)}, bf16[14336,128]{1,0:T(8,128)(2,1)}, u32[]{:S(2)}) copy-start(bf16[14336,128]{1,0:T(8,128)(2,1)} %param.14) | copy-start | bytes 11010052
  6.5 7.5 %copy-start.5 = (bf16[128,14336]{1,0:T(8,128)(2,1)S(1)}, bf16[128,14336]{1,0:T(8,128)(2,1)}, u32[]{:S(2)}) copy-start(bf16[128,14336]{1,0:T(8,128)(2,1)} %param.9) | copy-start | bytes 11010052
  14.0 3.6 %copy-start.1 = (bf16[4096,128]{1,0:T(8,128)(2,1)S(1)}, bf16[4096,128]{1,0:T(8,128)(2,1)}, u32[]{:S(2)}) copy-start(bf16[4096,128]{1,0:T(8,128)(2,1)} %param.13) | copy-start | bytes 3145732
  14.0 4.2 %copy-start.2 = (bf16[128,4096]{1,0:T(8,128)(2,1)S(1)}, bf16[128,4096]{1,0:T(8,128)(2,1)}, u32[]{:S(2)}) copy-start(bf16[128,4096]{1,0:T(8,128)(2,1)} %param.12) | copy-start | bytes 3145732
  50.1 4.0 %collective-permute-start = (f32[64,64]{1,0:T(8,128)S(1)}, f32[64,64]{1,0:T(8,128)S(1)}, u32[]{:S(2)}, u32[]{:S(2)}) collective-permute-start(f32[64,64]{1,0:T(8,128)S(1)} %select_select_fusion.4), channel_id=1, source_target_pairs={{0,2},{2,0},{4,6},{6,4},{8,10},{10,8},{12,14},{14,12},{16,18},{18,... | collective-permute-start | bytes 49160 | tf_op jit(solution)/shard_map/ppermute | solution.py:18
  61.6 4.0 %collective-permute-start.1 = (f32[64,64]{1,0:T(8,128)S(1)}, f32[64,64]{1,0:T(8,128)S(1)}, u32[]{:S(2)}, u32[]{:S(2)}) collective-permute-start(f32[64,64]{1,0:T(8,128)S(1)} %select_select_fusion.3), channel_id=1, source_target_pairs={{0,4},{2,6},{4,0},{6,2},{8,12},{10,14},{12,8},{14,10},{16,20},{18,... | collective-permute-start | bytes 49160 | tf_op jit(solution)/shard_map/ppermute | solution.py:18
  73.0 4.0 %collective-permute-start.2 = (f32[64,64]{1,0:T(8,128)S(1)}, f32[64,64]{1,0:T(8,128)S(1)}, u32[]{:S(2)}, u32[]{:S(2)}) collective-permute-start(f32[64,64]{1,0:T(8,128)S(1)} %select_select_fusion.2), channel_id=1, source_target_pairs={{0,8},{2,10},{4,12},{6,14},{8,0},{10,2},{12,4},{14,6},{16,24},{18,... | collective-permute-start | bytes 49160 | tf_op jit(solution)/shard_map/ppermute | solution.py:18
  84.5 4.9 %collective-permute-start.3 = (f32[64,64]{1,0:T(8,128)S(1)}, f32[64,64]{1,0:T(8,128)S(1)}, u32[]{:S(2)}, u32[]{:S(2)}) collective-permute-start(f32[64,64]{1,0:T(8,128)S(1)} %select_select_fusion.1), channel_id=1, source_target_pairs={{0,16},{2,18},{4,20},{6,22},{8,24},{10,26},{12,28},{14,30},{16,0},... | collective-permute-start | bytes 49160 | tf_op jit(solution)/shard_map/ppermute | solution.py:18
Sparse Core Ops, SparseCore 0:
  20.0 20.5 all-reduce.1
where the time goes:
time: 110 us
  other arithmetic  41.5 us (38%)
  waiting for transfers between devices  28.7 us (26%)
  matrix products  16.8 us (15%)
  between operations  13.7 us (12%)
  starting transfers between devices  8.12 us (7%)
    another operation x12, other arithmetic, shards(): lower = jnp.linalg.cholesky(combined)  26.1 us
    psum x1, waiting for transfers between devices, shards(): summed = lax.psum(shaped, 'mp')  20.7 us
    ppermute x4, starting transfers between devices, partner_2(): return lax.ppermute(value, axis, pairs)  8.12 us
    ppermute x4, waiting for transfers between devices, partner_2(): return lax.ppermute(value, axis, pairs)  7.93 us
    dot_general x1, matrix products, shards(): jnp.dot(up_grad, proj_hidden[:, :RANK], preferred_element_type=jnp.float32)  7.11 us
    another operation x3, other arithmetic, shards(): lower = jnp.linalg.cholesky(group_gram)  6.52 us
    another operation x2, other arithmetic, shards(): solved = jax.scipy.linalg.solve_triangular(lower, flat_mine.T, lower=True)  5.55 us
    dot_general x1, matrix products, shards(): jnp.dot(hidden, proj_hidden[:, RANK:], preferred_element_type=jnp.float32)  3.53 us
  transfers between devices with their start and end apart: 5, of which 5 were waited for; matrix products, arithmetic and copies ran while one was open for 1% of the time, Pallas kernels for 0%

commit v1 on v0

v1 whole, which is shorter than its diff:
```python
import functools
import math

import jax
import jax.numpy as jnp
from jax import lax
from jax.experimental import pallas as pl
from jax.experimental.pallas import tpu as pltpu
from jax.sharding import PartitionSpec as P

RANK = 64
LEN = 128
WIDE = 2 * RANK

highest = lax.Precision.HIGHEST
whole_vmem = pl.BlockSpec(memory_space=pltpu.VMEM)
left_in_hbm = pl.BlockSpec(memory_space=pl.ANY)


def pieces_of(width, most):
    count = most
    while width % (count * 128):
        count //= 2
    return count, width // count


def lanes_of(shape):
    return lax.broadcasted_iota(jnp.int32, shape, len(shape) - 1)


def project_kernel(
    shards, place, gate, up, grad, proj_hidden, tokens, outer, proj_model, *rest
):
    outs = rest[:shards]
    gate_v, up_v, grad_v, hidden_w, tokens_v, outer_v, model_w, sems, model_sems = rest[shards:]
    rows, hidden_width = gate.shape
    model_width = tokens.shape[1]
    hidden_count, hidden_each = pieces_of(hidden_width, 8)
    model_count, model_each = pieces_of(model_width, 4)

    hidden_copies = []
    for piece in range(hidden_count):
        cut = pl.ds(piece * hidden_each, hidden_each)
        hidden_copies.append(
            [
                pltpu.make_async_copy(gate.at[:, cut], gate_v.at[:, cut], sems.at[piece, 0]),
                pltpu.make_async_copy(grad.at[:, cut], grad_v.at[:, cut], sems.at[piece, 1]),
                pltpu.make_async_copy(up.at[:, cut], up_v.at[:, cut], sems.at[piece, 2]),
                pltpu.make_async_copy(
                    proj_hidden.at[cut, :], hidden_w.at[cut, :], sems.at[piece, 3]
                ),
            ]
        )
    model_copies = []
    for piece in range(model_count):
        cut = pl.ds(piece * model_each, model_each)
        model_copies.append(
            [
                pltpu.make_async_copy(
                    tokens.at[:, cut], tokens_v.at[:, cut], model_sems.at[piece, 0]
                ),
                pltpu.make_async_copy(
                    outer.at[:, cut], outer_v.at[:, cut], model_sems.at[piece, 1]
                ),
                pltpu.make_async_copy(
                    proj_model.at[cut, :], model_w.at[cut, :], model_sems.at[piece, 2]
                ),
            ]
        )
    for group in hidden_copies + model_copies:
        for copy in group:
            copy.start()

    step = 256 if hidden_each % 256 == 0 else 128
    hidden_sum = jnp.zeros((2 * rows, WIDE), jnp.float32)
    for piece in range(hidden_count):
        for copy in hidden_copies[piece]:
            copy.wait()
        for first in range(piece * hidden_each, (piece + 1) * hidden_each, step):
            cut = slice(first, first + step)
            half = gate_v[:, cut].astype(jnp.float32) * 0.5
            act = half + half * jnp.tanh(half)
            up_grad = (grad_v[:, cut].astype(jnp.float32) * act).astype(jnp.bfloat16)
            hidden = (act * up_v[:, cut].astype(jnp.float32)).astype(jnp.bfloat16)
            both = jnp.concatenate([up_grad, hidden], axis=0)
            hidden_sum += jnp.dot(both, hidden_w[cut, :], preferred_element_type=jnp.float32)
    model_sum = jnp.zeros((2 * rows, WIDE), jnp.float32)
    for piece in range(model_count):
        for copy in model_copies[piece]:
            copy.wait()
        cut = slice(piece * model_each, (piece + 1) * model_each)
        both = jnp.concatenate([tokens_v[:, cut], outer_v[:, cut]], axis=0)
        model_sum += jnp.dot(both, model_w[cut, :], preferred_element_type=jnp.float32)

    upward = hidden_sum[:rows]
    hidden_side = hidden_sum[rows:]
    input_side = model_sum[:rows]
    output_side = model_sum[rows:]
    lane = lanes_of((rows, WIDE))
    rows_each = WIDE // shards
    me = place[0]
    for shard in range(shards):
        at = shard * rows_each
        if at < RANK:
            left = input_side if at == 0 else pltpu.roll(input_side, WIDE - at, 1)
            right = pltpu.roll(upward, RANK, 1)
        else:
            left = pltpu.roll(hidden_side, WIDE - at, 1)
            right = output_side
        if rows_each < RANK:
            left = jnp.where(lane < rows_each, left, 0.0)
        block = jnp.where(lane < RANK, left, right)
        for away in range(shards):

            @pl.when(me == (shard - away) % shards)
            def _(block=block, away=away):
                outs[away][...] = block


def project(place, gate_pre, up_pre, hidden_grad, proj_hidden, tokens_in, out_grad, proj_model):
    shards = lax.axis_size("mp")
    rows, hidden_width = gate_pre.shape
    model_width = tokens_in.shape[1]
    hidden_count, _ = pieces_of(hidden_width, 8)
    model_count, _ = pieces_of(model_width, 4)
    held = jnp.bfloat16
    return pl.pallas_call(
        functools.partial(project_kernel, shards),
        out_shape=[jax.ShapeDtypeStruct((rows, WIDE), jnp.float32)] * shards,
        in_specs=[pl.BlockSpec(memory_space=pltpu.SMEM)] + [left_in_hbm] * 7,
        out_specs=[whole_vmem] * shards,
        scratch_shapes=[
            pltpu.VMEM((rows, hidden_width), held),
            pltpu.VMEM((rows, hidden_width), held),
            pltpu.VMEM((rows, hidden_width), held),
            pltpu.VMEM((hidden_width, WIDE), held),
            pltpu.VMEM((rows, model_width), held),
            pltpu.VMEM((rows, model_width), held),
            pltpu.VMEM((model_width, WIDE), held),
            pltpu.SemaphoreType.DMA((hidden_count, 4)),
            pltpu.SemaphoreType.DMA((model_count, 3)),
        ],
        compiler_params=pltpu.CompilerParams(vmem_limit_bytes=40 * 2**20),
        name="project",
    )(place, gate_pre, up_pre, hidden_grad, proj_hidden, tokens_in, out_grad, proj_model)


def gram_kernel(count, *refs):
    parts, (rows_ref, gram_ref) = refs[:count], refs[count:]
    total = parts[0][...]
    for part in parts[1:]:
        total += part[...]
    row = lax.broadcasted_iota(jnp.int32, (WIDE, WIDE), 0)
    lane = lanes_of((WIDE, WIDE))
    gram = jnp.zeros((RANK, WIDE), jnp.float32)
    for example in range(total.shape[0] // LEN):
        sides = total[example * LEN : (example + 1) * LEN]
        crossed = jnp.dot(
            sides.T, sides, precision=highest, preferred_element_type=jnp.float32
        )
        mixed = jnp.where((row < RANK) != (lane < RANK), crossed, 0.0)
        mine = mixed[RANK:]
        rows_ref[example] = mine
        gram += jnp.dot(mine, mixed, precision=highest, preferred_element_type=jnp.float32)
    top, bottom = gram[: RANK // 2], gram[RANK // 2 :]
    gram_ref[...] = jnp.where(
        lanes_of(top.shape) < RANK, pltpu.roll(top, RANK, 1), bottom
    )


def gram_of(parts):
    examples = parts[0].shape[0] // LEN
    return pl.pallas_call(
        functools.partial(gram_kernel, len(parts)),
        out_shape=[
            jax.ShapeDtypeStruct((examples, RANK, WIDE), jnp.float32),
            jax.ShapeDtypeStruct((RANK // 2, WIDE), jnp.float32),
        ],
        in_specs=[whole_vmem] * len(parts),
        out_specs=[whole_vmem] * 2,
        name="gram",
    )(*parts)


def whiten_kernel(factor, rows_each, rows_ref, gram_ref, out_ref):
    packed = gram_ref[...]
    gram = jnp.concatenate([pltpu.roll(packed, RANK, 1), packed], axis=0)
    height = 8
    lane = lanes_of((height, WIDE))
    sub = lax.broadcasted_iota(jnp.int32, (height, WIDE), 0)
    for example in range(rows_ref.shape[0]):
        joined = jnp.where(lanes_of((RANK, WIDE)) < RANK, rows_ref[example], gram)
        state = [joined[at : at + height] for at in range(0, RANK, height)]
        for pivot in range(RANK):
            held, inner = divmod(pivot, height)
            spot = RANK + pivot
            row = state[held][inner : inner + 1, :]
            scaled = row * (1.0 / row[:, spot : spot + 1])
            for other in range(held, RANK // height):
                column = state[other][:, spot : spot + 1]
                taken = column * scaled
                if other == held:
                    taken = jnp.where(sub > inner, taken, 0.0)
                state[other] = state[other] - taken
        done = []
        for held, block in enumerate(state):
            diagonal = jnp.sum(
                jnp.where(lane == RANK + held * height + sub, block, 0.0), axis=1, keepdims=True
            )
            done.append(block * (lax.rsqrt(diagonal) * factor))
        solved = jnp.concatenate(done, axis=0).T
        out_ref[example] = solved[:rows_each, :]


def whiten(rows, gram, rows_each, factor):
    return pl.pallas_call(
        functools.partial(whiten_kernel, factor, rows_each),
        out_shape=jax.ShapeDtypeStruct((rows.shape[0], rows_each, RANK), jnp.float32),
        in_specs=[whole_vmem] * 2,
        out_specs=whole_vmem,
        name="whiten",
    )(rows, gram)


def summed_everywhere(value):
    axes = ("dp", "mp")
    devices = lax.axis_size("dp") * lax.axis_size("mp")
    pieces = value.reshape(devices, -1)
    received = lax.all_to_all(pieces, axes, 0, 0, tiled=True)
    total = jnp.sum(received, axis=0, keepdims=True)
    gathered = lax.all_to_all(jnp.broadcast_to(total, pieces.shape), axes, 0, 0, tiled=True)
    return gathered.reshape(value.shape)


def shards(tokens_in, gate_pre, up_pre, hidden_grad, out_grad, proj_model, proj_hidden):
    model_shards = lax.axis_size("mp")
    rows_each = WIDE // model_shards
    local_examples = tokens_in.shape[0] // LEN
    place = lax.axis_index("mp").astype(jnp.int32).reshape(1)
    parts = project(
        place, gate_pre, up_pre, hidden_grad, proj_hidden, tokens_in, out_grad, proj_model
    )
    received = [parts[0]]
    for away in range(1, model_shards):
        pairs = [(source, (source + away) % model_shards) for source in range(model_shards)]
        received.append(lax.ppermute(parts[away], "mp", pairs))
    rows, gram = gram_of(received)
    gram = summed_everywhere(gram)
    factor = math.sqrt(local_examples * lax.axis_size("dp") * 2 * RANK)
    return whiten(rows, gram, rows_each, factor)


def solution(mesh):
    in_specs = (
        P("dp", "mp"),
        P("dp", "mp"),
        P("dp", "mp"),
        P("dp", "mp"),
        P("dp", "mp"),
        P("mp", None),
        P("mp", None),
    )
    out_specs = P("dp", "mp", None)
    return jax.shard_map(shards, mesh=mesh, in_specs=in_specs, out_specs=out_specs, check_vma=False)
```

time: 110 us -> 53.1 us (0.48)
  other arithmetic: 41.5 us -> 0.05 us
  waiting for transfers between devices: 28.7 us -> 0.9 us
  blocking collectives: 0 us -> 23.6 us
  matrix products: 16.8 us -> 0 us
  Pallas kernels: 0 us -> 16.4 us
  between operations: 13.7 us -> 0.03 us
  local copies, waits for them, and re-layouts: 0.71 us -> 11.1 us
  starting transfers between devices: 8.12 us -> 0.46 us
    another operation x17 -> x0, other arithmetic: 38.1 us -> none  [the longest x12 26.1 us: shards(): lower = jnp.linalg.cholesky(combined)]
    all_to_all x0 -> x2, blocking collectives: none -> 23.6 us  [the longest x1 14.3 us: summed_everywhere(): received = lax.all_to_all(pieces, axes, 0, 0, tiled=True)]
    psum x1 -> x0, waiting for transfers between devices: 20.7 us -> none  [shards(): summed = lax.psum(shaped, 'mp')]
    pallas_call x0 -> x3, Pallas kernels: none -> 16.4 us  [the longest x1 7.48 us: project(): pl.pallas_call(functools.partial(project_kernel, shards), out_shape=[jax....]
    dot_general x15 -> x0, matrix products: 15.9 us -> none  [the longest x1 7.11 us: shards(): jnp.dot(up_grad, proj_hidden[:, :RANK], preferred_element_type=jnp.float32)]
    unnamed x12 -> x16, local copies, waits for them, and re-layouts: 0.33 us -> 11 us
    ppermute x4 -> x1, starting transfers between devices: 8.12 us -> 0.46 us  [shards(): received.append(lax.ppermute(parts[away], 'mp', pairs))]
    ppermute x4 -> x1, waiting for transfers between devices: 7.93 us -> 0.9 us  [shards(): received.append(lax.ppermute(parts[away], 'mp', pairs))]
  transfers between devices with their start and end apart: 5 -> 1, of which waited for: 5 -> 1; matrix products, arithmetic and copies ran while one was open for 1% -> 0% of each run, Pallas kernels for 0% -> 0%
where the time goes in v1:
time: 53.1 us; the launch traced here: 52.6 us
  blocking collectives  23.6 us (44%)
  Pallas kernels  16.4 us (31%)
  local copies, waits for them, and re-layouts  11.1 us (21%)
  waiting for transfers between devices  0.9 us (2%)
    all_to_all x1, blocking collectives, summed_everywhere(): received = lax.all_to_all(pieces, axes, 0, 0, tiled=True)  14.3 us
    unnamed x16, local copies, waits for them, and re-layouts  11 us
    all_to_all x1, blocking collectives, summed_everywhere(): lax.all_to_all(jnp.broadcast_to(total, pieces.shape), axes, 0, 0, tiled=T...  9.37 us
    pallas_call x1, Pallas kernels, project(): pl.pallas_call(functools.partial(project_kernel, shards), out_shape=[jax....  7.48 us
    pallas_call x1, Pallas kernels, whiten(): pl.pallas_call(functools.partial(whiten_kernel, factor, rows_each), out_s...  6.9 us
    pallas_call x1, Pallas kernels, gram_of(): pl.pallas_call(functools.partial(gram_kernel, len(parts)), out_shape=[jax...  2.06 us
  transfers between devices with their start and end apart: 1, of which 1 were waited for; matrix products, arithmetic and copies ran while one was open for 0% of the time, Pallas kernels for 0%

profile of v1, /device:TPU:0, one launch (start us, length us, event | category | flops | bytes accessed | tf_op | source)
XLA Modules:
  0.0 52.6 jit_solution(14492096903729696219)
XLA Ops:
  0.0 0.0 copy-start
  0.0 2.0 %copy-done = bf16[128,14336]{1,0:T(8,128)(2,1)S(1)} copy-done((bf16[128,14336]{1,0:T(8,128)(2,1)S(1)}, bf16[128,14336]{1,0:T(8,128)(2,1)}, u32[]{:S(2)}) %copy-start) | copy-done | bytes 3670040
  2.0 0.0 copy-start.1
  2.0 2.0 %copy-done.1 = bf16[128,14336]{1,0:T(8,128)(2,1)S(1)} copy-done((bf16[128,14336]{1,0:T(8,128)(2,1)S(1)}, bf16[128,14336]{1,0:T(8,128)(2,1)}, u32[]{:S(2)}) %copy-start.1) | copy-done | bytes 3670040
  4.1 0.0 copy-start.2
  4.1 2.0 %copy-done.2 = bf16[128,14336]{1,0:T(8,128)(2,1)S(1)} copy-done((bf16[128,14336]{1,0:T(8,128)(2,1)S(1)}, bf16[128,14336]{1,0:T(8,128)(2,1)}, u32[]{:S(2)}) %copy-start.2) | copy-done | bytes 3670040
  6.1 0.0 copy-start.3
  6.1 1.2 %copy-done.3 = bf16[128,4096]{1,0:T(8,128)(2,1)S(1)} copy-done((bf16[128,4096]{1,0:T(8,128)(2,1)S(1)}, bf16[128,4096]{1,0:T(8,128)(2,1)}, u32[]{:S(2)}) %copy-start.3) | copy-done | bytes 1048600
  7.3 0.0 copy-start.4
  7.3 1.2 %copy-done.4 = bf16[128,4096]{1,0:T(8,128)(2,1)S(1)} copy-done((bf16[128,4096]{1,0:T(8,128)(2,1)S(1)}, bf16[128,4096]{1,0:T(8,128)(2,1)}, u32[]{:S(2)}) %copy-start.4) | copy-done | bytes 1048600
  8.6 0.0 copy-start.5
  8.6 1.2 %copy-done.5 = bf16[4096,128]{1,0:T(8,128)(2,1)S(1)} copy-done((bf16[4096,128]{1,0:T(8,128)(2,1)S(1)}, bf16[4096,128]{1,0:T(8,128)(2,1)}, u32[]{:S(2)}) %copy-start.5) | copy-done | bytes 1048600
  9.8 7.5 %project.1 = (f32[128,128]{1,0:T(8,128)S(1)}, f32[128,128]{1,0:T(8,128)S(1)}) custom-call(s32[1]{0:T(128)} %bitcast.place, bf16[128,14336]{1,0:T(8,128)(2,1)S(1)} %copy-done, bf16[128,14336]{1,0:T(8,128)(2,1)S(1)} %copy-done.1, bf16[128,14336]{1,0:T(8,128)(2,1)S(1)} %copy-done.2, bf16[14336,128]{1,0:T(8,128)(2,1)} %proj_hidden.1, ...), custom_call_target="tpu_custom_call" | custom-call | tf_op jit(solution)/shard_map/project/pallas_call | solution.py:127
  17.3 0.0 copy-start.6
  17.3 0.6 %copy-done.6 = f32[128,128]{1,0:T(8,128)} copy-done((f32[128,128]{1,0:T(8,128)}, f32[128,128]{1,0:T(8,128)S(1)}, u32[]{:S(2)}) %copy-start.6) | copy-done | bytes 65560
  17.9 0.5 collective-permute-start
  18.4 0.9 %collective-permute-done.refs_1_ = f32[128,128]{1,0:T(8,128)S(1)} collective-permute-done((f32[128,128]{1,0:T(8,128)S(1)}, f32[128,128]{1,0:T(8,128)S(1)}, u32[]{:S(2)}, u32[]{:S(2)}) %collective-permute-start) | collective-permute-done | bytes 65568 | tf_op jit(solution)/shard_map/ppermute | solution.py:246
  19.3 0.0 copy-start.7
  19.3 0.6 %copy-done.7 = f32[128,128]{1,0:T(8,128)} copy-done((f32[128,128]{1,0:T(8,128)}, f32[128,128]{1,0:T(8,128)S(1)}, u32[]{:S(2)}) %copy-start.7) | copy-done | bytes 65560
  19.9 2.1 %gram.1 = (f32[1,64,128]{2,1,0:T(8,128)}, f32[32,128]{1,0:T(8,128)}) custom-call(f32[128,128]{1,0:T(8,128)} %copy-done.6, f32[128,128]{1,0:T(8,128)} %copy-done.7), custom_call_target="tpu_custom_call" | custom-call | tf_op jit(solution)/shard_map/gram/pallas_call | solution.py:173
  22.0 14.3 %all_to_all.17 = f32[32,1,128]{2,1,0:T(1,128)S(1)} all-to-all(f32[32,1,128]{2,1,0:T(1,128)} %bitcast.6), channel_id=1, replica_groups=mesh['dp'=16,'mp'=2] {'dp','mp'}, dimensions={0} | all-to-all | bytes 32768 | tf_op jit(solution)/shard_map/all_to_all | solution.py:229
  36.2 0.1 reduce_sum.9
  36.3 9.4 %all_to_all.18 = f32[32,1,128]{2,1,0:T(1,128)} all-to-all(f32[32,1,128]{2,1,0:T(1,128)S(1)} %broadcast_in_dim.2), channel_id=1, replica_groups=mesh['dp'=16,'mp'=2] {'dp','mp'}, dimensions={0} | all-to-all | bytes 32768 | tf_op jit(solution)/shard_map/all_to_all | solution.py:231
  45.7 6.9 %whiten.1 = f32[1,64,64]{2,1,0:T(8,128)} custom-call(f32[1,64,128]{2,1,0:T(8,128)} %get-tuple-element.11.rows_ref, f32[32,128]{1,0:T(8,128)} %bitcast.5), custom_call_target="tpu_custom_call" | custom-call | tf_op jit(solution)/shard_map/whiten/pallas_call | solution.py:216
  (1 shorter events, 0.0 us)
Async XLA Ops:
  0.0 2.0 %copy-start = (bf16[128,14336]{1,0:T(8,128)(2,1)S(1)}, bf16[128,14336]{1,0:T(8,128)(2,1)}, u32[]{:S(2)}) copy-start(bf16[128,14336]{1,0:T(8,128)(2,1)} %gate.1) | copy-start | bytes 11010052
  2.0 2.0 %copy-start.1 = (bf16[128,14336]{1,0:T(8,128)(2,1)S(1)}, bf16[128,14336]{1,0:T(8,128)(2,1)}, u32[]{:S(2)}) copy-start(bf16[128,14336]{1,0:T(8,128)(2,1)} %up.1) | copy-start | bytes 11010052
  4.1 2.0 %copy-start.2 = (bf16[128,14336]{1,0:T(8,128)(2,1)S(1)}, bf16[128,14336]{1,0:T(8,128)(2,1)}, u32[]{:S(2)}) copy-start(bf16[128,14336]{1,0:T(8,128)(2,1)} %grad.1) | copy-start | bytes 11010052
  6.1 1.2 %copy-start.3 = (bf16[128,4096]{1,0:T(8,128)(2,1)S(1)}, bf16[128,4096]{1,0:T(8,128)(2,1)}, u32[]{:S(2)}) copy-start(bf16[128,4096]{1,0:T(8,128)(2,1)} %tokens.1) | copy-start | bytes 3145732
  7.3 1.2 %copy-start.4 = (bf16[128,4096]{1,0:T(8,128)(2,1)S(1)}, bf16[128,4096]{1,0:T(8,128)(2,1)}, u32[]{:S(2)}) copy-start(bf16[128,4096]{1,0:T(8,128)(2,1)} %outer.1) | copy-start | bytes 3145732
  8.6 1.2 %copy-start.5 = (bf16[4096,128]{1,0:T(8,128)(2,1)S(1)}, bf16[4096,128]{1,0:T(8,128)(2,1)}, u32[]{:S(2)}) copy-start(bf16[4096,128]{1,0:T(8,128)(2,1)} %proj_model.1) | copy-start | bytes 3145732
  17.3 0.6 %copy-start.6 = (f32[128,128]{1,0:T(8,128)}, f32[128,128]{1,0:T(8,128)S(1)}, u32[]{:S(2)}) copy-start(f32[128,128]{1,0:T(8,128)S(1)} %get-tuple-element.9.refs_0_) | copy-start | bytes 196612
  17.9 1.4 %collective-permute-start = (f32[128,128]{1,0:T(8,128)S(1)}, f32[128,128]{1,0:T(8,128)S(1)}, u32[]{:S(2)}, u32[]{:S(2)}) collective-permute-start(f32[128,128]{1,0:T(8,128)S(1)} %get-tuple-element.10), channel_id=1, source_target_pairs={{0,1},{1,0},{2,3},{3,2},{4,5},{5,4},{6,7},{7,6},{8,9},{9,8},{10,11... | collective-permute-start | bytes 196616 | tf_op jit(solution)/shard_map/ppermute | solution.py:246
  19.3 0.6 %copy-start.7 = (f32[128,128]{1,0:T(8,128)}, f32[128,128]{1,0:T(8,128)S(1)}, u32[]{:S(2)}) copy-start(f32[128,128]{1,0:T(8,128)S(1)} %collective-permute-done.refs_1_) | copy-start | bytes 196612

commit v2 on v1

v2 whole, which is shorter than its diff:
```python
import functools
import math

import jax
import jax.numpy as jnp
from jax import lax
from jax.experimental import pallas as pl
from jax.experimental.pallas import tpu as pltpu
from jax.sharding import PartitionSpec as P

RANK = 64
LEN = 128
WIDE = 2 * RANK

highest = lax.Precision.HIGHEST
whole_vmem = pl.BlockSpec(memory_space=pltpu.VMEM)
left_in_hbm = pl.BlockSpec(memory_space=pl.ANY)
small = pltpu.CompilerParams(vmem_limit_bytes=8 * 2**20)


def pieces_of(width, most):
    count = most
    while width % (count * 128):
        count //= 2
    return count, width // count


def lanes_of(shape):
    return lax.broadcasted_iota(jnp.int32, shape, len(shape) - 1)


def project_kernel(gate, up, grad, proj_hidden, tokens, outer, proj_model, out, *rest):
    gate_v, up_v, grad_v, hidden_w, tokens_v, outer_v, model_w, sems, model_sems = rest
    rows, hidden_width = gate.shape
    model_width = tokens.shape[1]
    hidden_count, hidden_each = pieces_of(hidden_width, 8)
    model_count, model_each = pieces_of(model_width, 4)

    hidden_copies = []
    for piece in range(hidden_count):
        cut = pl.ds(piece * hidden_each, hidden_each)
        hidden_copies.append(
            [
                pltpu.make_async_copy(gate.at[:, cut], gate_v.at[:, cut], sems.at[piece, 0]),
                pltpu.make_async_copy(grad.at[:, cut], grad_v.at[:, cut], sems.at[piece, 1]),
                pltpu.make_async_copy(up.at[:, cut], up_v.at[:, cut], sems.at[piece, 2]),
                pltpu.make_async_copy(
                    proj_hidden.at[cut, :], hidden_w.at[cut, :], sems.at[piece, 3]
                ),
            ]
        )
    model_copies = []
    for piece in range(model_count):
        cut = pl.ds(piece * model_each, model_each)
        model_copies.append(
            [
                pltpu.make_async_copy(
                    tokens.at[:, cut], tokens_v.at[:, cut], model_sems.at[piece, 0]
                ),
                pltpu.make_async_copy(
                    outer.at[:, cut], outer_v.at[:, cut], model_sems.at[piece, 1]
                ),
                pltpu.make_async_copy(
                    proj_model.at[cut, :], model_w.at[cut, :], model_sems.at[piece, 2]
                ),
            ]
        )
    for group in hidden_copies + model_copies:
        for copy in group:
            copy.start()

    step = 256 if hidden_each % 256 == 0 else 128
    hidden_sum = jnp.zeros((2 * rows, WIDE), jnp.float32)
    for piece in range(hidden_count):
        for copy in hidden_copies[piece]:
            copy.wait()
        for first in range(piece * hidden_each, (piece + 1) * hidden_each, step):
            cut = slice(first, first + step)
            half = gate_v[:, cut].astype(jnp.float32) * 0.5
            act = half + half * jnp.tanh(half)
            up_grad = (grad_v[:, cut].astype(jnp.float32) * act).astype(jnp.bfloat16)
            hidden = (act * up_v[:, cut].astype(jnp.float32)).astype(jnp.bfloat16)
            both = jnp.concatenate([up_grad, hidden], axis=0)
            hidden_sum += jnp.dot(both, hidden_w[cut, :], preferred_element_type=jnp.float32)
    model_sum = jnp.zeros((2 * rows, WIDE), jnp.float32)
    for piece in range(model_count):
        for copy in model_copies[piece]:
            copy.wait()
        cut = slice(piece * model_each, (piece + 1) * model_each)
        both = jnp.concatenate([tokens_v[:, cut], outer_v[:, cut]], axis=0)
        model_sum += jnp.dot(both, model_w[cut, :], preferred_element_type=jnp.float32)

    low = lanes_of((rows, WIDE)) < RANK
    upward = pltpu.roll(hidden_sum[:rows], RANK, 1)
    hidden_side = pltpu.roll(hidden_sum[rows:], RANK, 1)
    out[:, :WIDE] = jnp.where(low, model_sum[:rows], upward)
    out[:, WIDE:] = jnp.where(low, hidden_side, model_sum[rows:])


def project(gate_pre, up_pre, hidden_grad, proj_hidden, tokens_in, out_grad, proj_model):
    rows, hidden_width = gate_pre.shape
    model_width = tokens_in.shape[1]
    hidden_count, _ = pieces_of(hidden_width, 8)
    model_count, _ = pieces_of(model_width, 4)
    held = jnp.bfloat16
    return pl.pallas_call(
        project_kernel,
        out_shape=jax.ShapeDtypeStruct((rows, 2 * WIDE), jnp.float32),
        in_specs=[left_in_hbm] * 7,
        out_specs=whole_vmem,
        scratch_shapes=[
            pltpu.VMEM((rows, hidden_width), held),
            pltpu.VMEM((rows, hidden_width), held),
            pltpu.VMEM((rows, hidden_width), held),
            pltpu.VMEM((hidden_width, WIDE), held),
            pltpu.VMEM((rows, model_width), held),
            pltpu.VMEM((rows, model_width), held),
            pltpu.VMEM((model_width, WIDE), held),
            pltpu.SemaphoreType.DMA((hidden_count, 4)),
            pltpu.SemaphoreType.DMA((model_count, 3)),
        ],
        compiler_params=pltpu.CompilerParams(vmem_limit_bytes=60 * 2**20),
        name="project",
    )(gate_pre, up_pre, hidden_grad, proj_hidden, tokens_in, out_grad, proj_model)


def gram_kernel(rows_each, count, *refs):
    place, parts, (rows_ref, gram_ref) = refs[0], refs[1 : 1 + count], refs[1 + count :]
    total = parts[0][...]
    for part in parts[1:]:
        total += part[...]
    row = lax.broadcasted_iota(jnp.int32, (WIDE, WIDE), 0)
    lane = lanes_of((WIDE, WIDE))
    low = lanes_of((RANK, WIDE)) < RANK
    gram = jnp.zeros((RANK, WIDE), jnp.float32)
    shift = lax.rem(WIDE - place[0] * rows_each, WIDE)
    for example in range(total.shape[0] // LEN):
        mixed = []
        for at in (0, WIDE):
            sides = total[example * LEN : (example + 1) * LEN, at : at + WIDE]
            crossed = jnp.dot(
                sides.T, sides, precision=highest, preferred_element_type=jnp.float32
            )
            mixed.append(jnp.where((row < RANK) != (lane < RANK), crossed, 0.0))
        up_block, down_block = mixed[0][RANK:], mixed[1][RANK:]
        across = jnp.where(low, up_block, pltpu.roll(down_block, RANK, 1))
        rows_ref[example] = jnp.where(low, pltpu.roll(across, shift, 1), 0.0)
        gram += jnp.dot(
            jnp.concatenate([up_block, down_block], axis=1),
            jnp.concatenate(mixed, axis=0),
            precision=highest,
            preferred_element_type=jnp.float32,
        )
    top, bottom = gram[: RANK // 2], gram[RANK // 2 :]
    gram_ref[...] = jnp.where(
        lanes_of(top.shape) < RANK, pltpu.roll(top, RANK, 1), bottom
    )


def gram_of(place, parts, rows_each):
    examples = parts[0].shape[0] // LEN
    return pl.pallas_call(
        functools.partial(gram_kernel, rows_each, len(parts)),
        out_shape=[
            jax.ShapeDtypeStruct((examples, RANK, WIDE), jnp.float32),
            jax.ShapeDtypeStruct((RANK // 2, WIDE), jnp.float32),
        ],
        in_specs=[pl.BlockSpec(memory_space=pltpu.SMEM)] + [whole_vmem] * len(parts),
        out_specs=[whole_vmem] * 2,
        compiler_params=small,
        name="gram",
    )(place, *parts)


def eliminated(state):
    height = 8
    blocks = len(state)
    state = list(state)
    sub = lax.broadcasted_iota(jnp.int32, state[0].shape, 0)

    def across(block, at):
        return jnp.broadcast_to(block[:, at : at + 1], block.shape)

    def down(block, at):
        return jnp.broadcast_to(block[at : at + 1, :], block.shape)

    done = []
    for held in range(blocks):
        base = RANK + held * height
        own = state[held]
        columns = [across(own, base + k) for k in range(height)]
        corner = {
            (k, m): down(columns[m], k) for k in range(height) for m in range(k, height)
        }
        rows = [down(own, k) for k in range(height)]
        ahead = None
        if held + 1 < blocks:
            ahead = [across(state[held + 1], base + k) for k in range(height)]
        factors = {}
        inverses = []
        for k in range(height):
            inverse = 1.0 / corner[k, k]
            inverses.append(inverse)
            for m in range(k + 1, height):
                factor = corner[k, m] * inverse
                factors[k, m] = factor
                for n in range(m, height):
                    corner[m, n] = corner[m, n] - factor * corner[k, n]
                rows[m] = rows[m] - factor * rows[k]
                if ahead is not None:
                    ahead[m] = ahead[m] - factor * ahead[k]
        if ahead is not None:
            taken = [ahead[k] * (inverses[k] * rows[k]) for k in range(height)]
            while len(taken) > 1:
                taken = [left + right for left, right in zip(taken[::2], taken[1::2])]
            state[held + 1] = state[held + 1] - taken[0]
        if held + 2 < blocks:
            back = [inverses[k] * rows[k] for k in range(height)]
            for k in reversed(range(height)):
                for m in range(k):
                    back[m] = back[m] - factors[m, k] * back[k]
            for other in range(held + 2, blocks):
                for k in range(height):
                    state[other] = state[other] - across(state[other], base + k) * back[k]
        block = rows[0] * lax.rsqrt(corner[0, 0])
        for k in range(1, height):
            block = jnp.where(sub == k, rows[k] * lax.rsqrt(corner[k, k]), block)
        done.append(block)
    return done


def whiten_kernel(factor, rows_each, rows_ref, gram_ref, out_ref):
    packed = gram_ref[...]
    gram = jnp.concatenate([pltpu.roll(packed, RANK, 1), packed], axis=0)
    low = lanes_of((RANK, WIDE)) < RANK
    for example in range(rows_ref.shape[0]):
        joined = jnp.where(low, rows_ref[example], gram)
        done = eliminated([joined[at : at + 8] for at in range(0, RANK, 8)])
        solved = (jnp.concatenate(done, axis=0) * factor).T
        out_ref[example] = solved[:rows_each, :]


def whiten(rows, gram, rows_each, factor):
    return pl.pallas_call(
        functools.partial(whiten_kernel, factor, rows_each),
        out_shape=jax.ShapeDtypeStruct((rows.shape[0], rows_each, RANK), jnp.float32),
        in_specs=[whole_vmem] * 2,
        out_specs=whole_vmem,
        compiler_params=small,
        name="whiten",
    )(rows, gram)


def summed_over_groups(value):
    groups = lax.axis_size("dp")
    for level in range(groups.bit_length() - 1):
        pairs = [(source, source ^ 2**level) for source in range(groups)]
        value = value + lax.ppermute(value, "dp", pairs)
    return value


def shards(tokens_in, gate_pre, up_pre, hidden_grad, out_grad, proj_model, proj_hidden):
    model_shards = lax.axis_size("mp")
    rows_each = WIDE // model_shards
    local_examples = tokens_in.shape[0] // LEN
    place = lax.axis_index("mp").astype(jnp.int32).reshape(1)
    part = project(
        gate_pre, up_pre, hidden_grad, proj_hidden, tokens_in, out_grad, proj_model
    )
    parts = [part]
    for away in range(1, model_shards):
        pairs = [(source, (source + away) % model_shards) for source in range(model_shards)]
        parts.append(lax.ppermute(part, "mp", pairs))
    rows, gram = gram_of(place, parts, rows_each)
    gram = summed_over_groups(gram)
    factor = math.sqrt(local_examples * lax.axis_size("dp") * 2 * RANK)
    return whiten(rows, gram, rows_each, factor)


def solution(mesh):
    in_specs = (
        P("dp", "mp"),
        P("dp", "mp"),
        P("dp", "mp"),
        P("dp", "mp"),
        P("dp", "mp"),
        P("mp", None),
        P("mp", None),
    )
    out_specs = P("dp", "mp", None)
    return jax.shard_map(shards, mesh=mesh, in_specs=in_specs, out_specs=out_specs, check_vma=False)
```

time: 53.1 us -> 33.8 us (0.64)
  blocking collectives: 23.6 us -> 0 us
  local copies, waits for them, and re-layouts: 11.1 us -> 0.9 us
  starting transfers between devices: 0.46 us -> 10.5 us
  waiting for transfers between devices: 0.9 us -> 8.06 us
  Pallas kernels: 16.4 us -> 14.1 us
    all_to_all x2 -> x0, blocking collectives: 23.6 us -> none  [the longest x1 14.3 us: summed_everywhere(): received = lax.all_to_all(pieces, axes, 0, 0, tiled=True)]
    unnamed x16 -> x2, local copies, waits for them, and re-layouts: 11 us -> 0.9 us
    ppermute x1 -> x5, starting transfers between devices: 0.46 us -> 10.5 us  [the longest x4 10 us: summed_over_groups(): value = value + lax.ppermute(value, 'dp', pairs)]
    ppermute x1 -> x5, waiting for transfers between devices: 0.9 us -> 8.06 us  [the longest x4 6.87 us: summed_over_groups(): value = value + lax.ppermute(value, 'dp', pairs)]
    pallas_call x1, Pallas kernels: 6.9 us -> 4.61 us  [whiten(): pl.pallas_call(functools.partial(whiten_kernel, factor, rows_each), out_s...]
  transfers between devices with their start and end apart: 1 -> 5, of which waited for: 1 -> 5; matrix products, arithmetic and copies ran while one was open for 0% -> 0% of each run, Pallas kernels for 0% -> 0%
where the time goes in v2:
time: 33.8 us; the launch traced here: 33.6 us
  Pallas kernels  14.1 us (42%)
  starting transfers between devices  10.5 us (31%)
  waiting for transfers between devices  8.06 us (24%)
  local copies, waits for them, and re-layouts  0.9 us (3%)
    ppermute x4, starting transfers between devices, summed_over_groups(): value = value + lax.ppermute(value, 'dp', pairs)  10 us
    pallas_call x1, Pallas kernels, project(): pl.pallas_call(project_kernel, out_shape=jax.ShapeDtypeStruct((rows, 2 *...  8.9 us
    ppermute x4, waiting for transfers between devices, summed_over_groups(): value = value + lax.ppermute(value, 'dp', pairs)  6.87 us
    pallas_call x1, Pallas kernels, whiten(): pl.pallas_call(functools.partial(whiten_kernel, factor, rows_each), out_s...  4.61 us
    ppermute x1, waiting for transfers between devices, shards(): parts.append(lax.ppermute(part, 'mp', pairs))  1.2 us
    unnamed x2, local copies, waits for them, and re-layouts  0.9 us
  transfers between devices with their start and end apart: 5, of which 5 were waited for; matrix products, arithmetic and copies ran while one was open for 0% of the time, Pallas kernels for 0%

profile of v2, /device:TPU:0, one launch (start us, length us, event | category | flops | bytes accessed | tf_op | source)
XLA Modules:
  0.0 33.6 jit_solution(17976051572136938168)
XLA Ops:
  0.0 8.9 %project.1.refs_1_ = f32[128,256]{1,0:T(8,128)} custom-call(bf16[128,14336]{1,0:T(8,128)(2,1)} %gate.1, bf16[128,14336]{1,0:T(8,128)(2,1)} %up.1, bf16[128,14336]{1,0:T(8,128)(2,1)} %grad.1, bf16[14336,128]{1,0:T(8,128)(2,1)} %proj_hidden.1, bf16[128,4096]{1,0:T(8,128)(2,1)} %tokens.1, bf16[128,4096]{1,0:T(8,128)(2,1)} %outer.1, bf16[4096,128]{1,0:T(8,128)(2,1)} %proj_model.1), custom_call_target="tpu_custom_call" | custom-call | tf_op jit(solution)/shard_map/project/pallas_call | solution.py:106
  8.9 0.5 %collective-permute-start = (f32[128,256]{1,0:T(8,128)}, f32[128,256]{1,0:T(8,128)S(1)}, u32[]{:S(2)}, u32[]{:S(2)}) collective-permute-start(f32[128,256]{1,0:T(8,128)} %project.1.refs_1_), channel_id=1, source_target_pairs={{0,1},{1,0},{2,3},{3,2},{4,5},{5,4},{6,7},{7,6},{8,9},{9,8},{10,11... | collective-permute-start | bytes 393224 | tf_op jit(solution)/shard_map/ppermute | solution.py:273
  9.4 1.2 %collective-permute-done.refs_2_ = f32[128,256]{1,0:T(8,128)S(1)} collective-permute-done((f32[128,256]{1,0:T(8,128)}, f32[128,256]{1,0:T(8,128)S(1)}, u32[]{:S(2)}, u32[]{:S(2)}) %collective-permute-start) | collective-permute-done | bytes 131104 | tf_op jit(solution)/shard_map/ppermute | solution.py:273
  10.6 0.0 copy-start
  10.6 0.9 %copy-done = f32[128,256]{1,0:T(8,128)S(1)} copy-done((f32[128,256]{1,0:T(8,128)S(1)}, f32[128,256]{1,0:T(8,128)}, u32[]{:S(2)}) %copy-start) | copy-done | bytes 131096
  11.5 0.6 %gram.1 = (f32[1,64,128]{2,1,0:T(8,128)S(1)}, f32[32,128]{1,0:T(8,128)S(1)}) custom-call(s32[1]{0:T(128)} %bitcast.refs_0_, f32[128,256]{1,0:T(8,128)S(1)} %copy-done, f32[128,256]{1,0:T(8,128)S(1)} %collective-permute-done.refs_2_), custom_call_target="tpu_custom_call" | custom-call | tf_op jit(solution)/shard_map/gram/pallas_call | solution.py:162
  12.1 2.9 %collective-permute-start.1 = (f32[32,128]{1,0:T(8,128)S(1)}, f32[32,128]{1,0:T(8,128)S(1)}, u32[]{:S(2)}, u32[]{:S(2)}) collective-permute-start(f32[32,128]{1,0:T(8,128)S(1)} %get-tuple-element.8), channel_id=1, source_target_pairs={{0,2},{2,0},{4,6},{6,4},{8,10},{10,8},{12,14},{14,12},{16,18},{18,... | collective-permute-start | bytes 49160 | tf_op jit(solution)/shard_map/ppermute | solution.py:258
  15.0 1.7 %collective-permute-done.1 = f32[32,128]{1,0:T(8,128)S(1)} collective-permute-done((f32[32,128]{1,0:T(8,128)S(1)}, f32[32,128]{1,0:T(8,128)S(1)}, u32[]{:S(2)}, u32[]{:S(2)}) %collective-permute-start.1) | collective-permute-done | bytes 16416 | tf_op jit(solution)/shard_map/ppermute | solution.py:258
  16.7 2.0 %collective-permute-start.2 = (f32[32,128]{1,0:T(8,128)S(1)}, f32[32,128]{1,0:T(8,128)S(1)}, u32[]{:S(2)}, u32[]{:S(2)}) collective-permute-start(f32[32,128]{1,0:T(8,128)S(1)} %add.12), channel_id=1, source_target_pairs={{0,4},{2,6},{4,0},{6,2},{8,12},{10,14},{12,8},{14,10},{16,20},{18,... | collective-permute-start | bytes 49160 | tf_op jit(solution)/shard_map/ppermute | solution.py:258
  18.7 1.7 %collective-permute-done.2 = f32[32,128]{1,0:T(8,128)S(1)} collective-permute-done((f32[32,128]{1,0:T(8,128)S(1)}, f32[32,128]{1,0:T(8,128)S(1)}, u32[]{:S(2)}, u32[]{:S(2)}) %collective-permute-start.2) | collective-permute-done | bytes 16416 | tf_op jit(solution)/shard_map/ppermute | solution.py:258
  20.5 2.1 %collective-permute-start.3 = (f32[32,128]{1,0:T(8,128)S(1)}, f32[32,128]{1,0:T(8,128)S(1)}, u32[]{:S(2)}, u32[]{:S(2)}) collective-permute-start(f32[32,128]{1,0:T(8,128)S(1)} %add.13), channel_id=1, source_target_pairs={{0,8},{2,10},{4,12},{6,14},{8,0},{10,2},{12,4},{14,6},{16,24},{18,... | collective-permute-start | bytes 49160 | tf_op jit(solution)/shard_map/ppermute | solution.py:258
  22.5 1.7 %collective-permute-done.3 = f32[32,128]{1,0:T(8,128)S(1)} collective-permute-done((f32[32,128]{1,0:T(8,128)S(1)}, f32[32,128]{1,0:T(8,128)S(1)}, u32[]{:S(2)}, u32[]{:S(2)}) %collective-permute-start.3) | collective-permute-done | bytes 16416 | tf_op jit(solution)/shard_map/ppermute | solution.py:258
  24.3 3.0 %collective-permute-start.4 = (f32[32,128]{1,0:T(8,128)S(1)}, f32[32,128]{1,0:T(8,128)S(1)}, u32[]{:S(2)}, u32[]{:S(2)}) collective-permute-start(f32[32,128]{1,0:T(8,128)S(1)} %add.14), channel_id=1, source_target_pairs={{0,16},{2,18},{4,20},{6,22},{8,24},{10,26},{12,28},{14,30},{16,0},... | collective-permute-start | bytes 49160 | tf_op jit(solution)/shard_map/ppermute | solution.py:258
  27.3 1.7 %collective-permute-done.4 = f32[32,128]{1,0:T(8,128)S(1)} collective-permute-done((f32[32,128]{1,0:T(8,128)S(1)}, f32[32,128]{1,0:T(8,128)S(1)}, u32[]{:S(2)}, u32[]{:S(2)}) %collective-permute-start.4) | collective-permute-done | bytes 16416 | tf_op jit(solution)/shard_map/ppermute | solution.py:258
  29.0 4.6 %whiten.1 = f32[1,64,64]{2,1,0:T(8,128)} custom-call(f32[1,64,128]{2,1,0:T(8,128)S(1)} %get-tuple-element.7.rows_ref, f32[32,128]{1,0:T(8,128)S(1)} %add.15.gram_ref), custom_call_target="tpu_custom_call" | custom-call | tf_op jit(solution)/shard_map/whiten/pallas_call | solution.py:244
  (4 shorter events, 0.0 us)
Async XLA Ops:
  8.9 1.7 %collective-permute-start = (f32[128,256]{1,0:T(8,128)}, f32[128,256]{1,0:T(8,128)S(1)}, u32[]{:S(2)}, u32[]{:S(2)}) collective-permute-start(f32[128,256]{1,0:T(8,128)} %project.1.refs_1_), channel_id=1, source_target_pairs={{0,1},{1,0},{2,3},{3,2},{4,5},{5,4},{6,7},{7,6},{8,9},{9,8},{10,11... | collective-permute-start | bytes 393224 | tf_op jit(solution)/shard_map/ppermute | solution.py:273
  10.6 0.9 %copy-start = (f32[128,256]{1,0:T(8,128)S(1)}, f32[128,256]{1,0:T(8,128)}, u32[]{:S(2)}) copy-start(f32[128,256]{1,0:T(8,128)} %project.1.refs_1_) | copy-start | bytes 393220
  12.1 4.6 %collective-permute-start.1 = (f32[32,128]{1,0:T(8,128)S(1)}, f32[32,128]{1,0:T(8,128)S(1)}, u32[]{:S(2)}, u32[]{:S(2)}) collective-permute-start(f32[32,128]{1,0:T(8,128)S(1)} %get-tuple-element.8), channel_id=1, source_target_pairs={{0,2},{2,0},{4,6},{6,4},{8,10},{10,8},{12,14},{14,12},{16,18},{18,... | collective-permute-start | bytes 49160 | tf_op jit(solution)/shard_map/ppermute | solution.py:258
  16.7 3.8 %collective-permute-start.2 = (f32[32,128]{1,0:T(8,128)S(1)}, f32[32,128]{1,0:T(8,128)S(1)}, u32[]{:S(2)}, u32[]{:S(2)}) collective-permute-start(f32[32,128]{1,0:T(8,128)S(1)} %add.12), channel_id=1, source_target_pairs={{0,4},{2,6},{4,0},{6,2},{8,12},{10,14},{12,8},{14,10},{16,20},{18,... | collective-permute-start | bytes 49160 | tf_op jit(solution)/shard_map/ppermute | solution.py:258
  20.5 3.8 %collective-permute-start.3 = (f32[32,128]{1,0:T(8,128)S(1)}, f32[32,128]{1,0:T(8,128)S(1)}, u32[]{:S(2)}, u32[]{:S(2)}) collective-permute-start(f32[32,128]{1,0:T(8,128)S(1)} %add.13), channel_id=1, source_target_pairs={{0,8},{2,10},{4,12},{6,14},{8,0},{10,2},{12,4},{14,6},{16,24},{18,... | collective-permute-start | bytes 49160 | tf_op jit(solution)/shard_map/ppermute | solution.py:258
  24.3 4.8 %collective-permute-start.4 = (f32[32,128]{1,0:T(8,128)S(1)}, f32[32,128]{1,0:T(8,128)S(1)}, u32[]{:S(2)}, u32[]{:S(2)}) collective-permute-start(f32[32,128]{1,0:T(8,128)S(1)} %add.14), channel_id=1, source_target_pairs={{0,16},{2,18},{4,20},{6,22},{8,24},{10,26},{12,28},{14,30},{16,0},... | collective-permute-start | bytes 49160 | tf_op jit(solution)/shard_map/ppermute | solution.py:258

commit v3 on v2

--- a/solution.py
+++ b/solution.py
@@ -11,6 +11,10 @@
 RANK = 64
 LEN = 128
 WIDE = 2 * RANK
+HIDDEN_PIECES = 16
+MODEL_PIECES = 4
+AHEAD = 4
+STRIP = 32
 
 highest = lax.Precision.HIGHEST
 whole_vmem = pl.BlockSpec(memory_space=pltpu.VMEM)
@@ -30,11 +34,11 @@
 
 
 def project_kernel(gate, up, grad, proj_hidden, tokens, outer, proj_model, out, *rest):
-    gate_v, up_v, grad_v, hidden_w, tokens_v, outer_v, model_w, sems, model_sems = rest
+    gate_v, up_v, grad_v, hidden_w, tokens_v, outer_v, model_w, acts, sems, model_sems = rest
     rows, hidden_width = gate.shape
     model_width = tokens.shape[1]
-    hidden_count, hidden_each = pieces_of(hidden_width, 8)
-    model_count, model_each = pieces_of(model_width, 4)
+    hidden_count, hidden_each = pieces_of(hidden_width, HIDDEN_PIECES)
+    model_count, model_each = pieces_of(model_width, MODEL_PIECES)
 
     hidden_copies = []
     for piece in range(hidden_count):
@@ -65,27 +69,40 @@
                 ),
             ]
         )
-    for group in hidden_copies + model_copies:
-        for copy in group:
-            copy.start()
-
-    step = 256 if hidden_each % 256 == 0 else 128
+    waiting = hidden_copies + model_copies
+
+    def start(which):
+        if which < len(waiting):
+            for copy in waiting[which]:
+                copy.start()
+
+    for which in range(AHEAD):
+        start(which)
     hidden_sum = jnp.zeros((2 * rows, WIDE), jnp.float32)
     for piece in range(hidden_count):
         for copy in hidden_copies[piece]:
             copy.wait()
-        for first in range(piece * hidden_each, (piece + 1) * hidden_each, step):
-            cut = slice(first, first + step)
-            half = gate_v[:, cut].astype(jnp.float32) * 0.5
-            act = half + half * jnp.tanh(half)
-            up_grad = (grad_v[:, cut].astype(jnp.float32) * act).astype(jnp.bfloat16)
-            hidden = (act * up_v[:, cut].astype(jnp.float32)).astype(jnp.bfloat16)
-            both = jnp.concatenate([up_grad, hidden], axis=0)
-            hidden_sum += jnp.dot(both, hidden_w[cut, :], preferred_element_type=jnp.float32)
+        start(piece + AHEAD)
+        slot = piece % 2
+        for strip in range(0, rows, STRIP):
+            for first in range(0, hidden_each, 128):
+                at = (slice(strip, strip + STRIP), pl.ds(piece * hidden_each + first, 128))
+                half = gate_v[at].astype(jnp.float32) * 0.5
+                act = half + half * jnp.tanh(half)
+                to = pl.ds(first, 128)
+                acts[slot, pl.ds(strip, STRIP), to] = (
+                    grad_v[at].astype(jnp.float32) * act
+                ).astype(jnp.bfloat16)
+                acts[slot, pl.ds(rows + strip, STRIP), to] = (
+                    act * up_v[at].astype(jnp.float32)
+                ).astype(jnp.bfloat16)
+        cut = slice(piece * hidden_each, (piece + 1) * hidden_each)
+        hidden_sum += jnp.dot(acts[slot], hidden_w[cut, :], preferred_element_type=jnp.float32)
     model_sum = jnp.zeros((2 * rows, WIDE), jnp.float32)
     for piece in range(model_count):
         for copy in model_copies[piece]:
             copy.wait()
+        start(hidden_count + piece + AHEAD)
         cut = slice(piece * model_each, (piece + 1) * model_each)
         both = jnp.concatenate([tokens_v[:, cut], outer_v[:, cut]], axis=0)
         model_sum += jnp.dot(both, model_w[cut, :], preferred_element_type=jnp.float32)
@@ -100,8 +117,8 @@
 def project(gate_pre, up_pre, hidden_grad, proj_hidden, tokens_in, out_grad, proj_model):
     rows, hidden_width = gate_pre.shape
     model_width = tokens_in.shape[1]
-    hidden_count, _ = pieces_of(hidden_width, 8)
-    model_count, _ = pieces_of(model_width, 4)
+    hidden_count, _ = pieces_of(hidden_width, HIDDEN_PIECES)
+    model_count, _ = pieces_of(model_width, MODEL_PIECES)
     held = jnp.bfloat16
     return pl.pallas_call(
         project_kernel,
@@ -116,10 +133,11 @@
             pltpu.VMEM((rows, model_width), held),
             pltpu.VMEM((rows, model_width), held),
             pltpu.VMEM((model_width, WIDE), held),
+            pltpu.VMEM((2, 2 * rows, hidden_width // hidden_count), held),
             pltpu.SemaphoreType.DMA((hidden_count, 4)),
             pltpu.SemaphoreType.DMA((model_count, 3)),
         ],
-        compiler_params=pltpu.CompilerParams(vmem_limit_bytes=60 * 2**20),
+        compiler_params=pltpu.CompilerParams(vmem_limit_bytes=56 * 10**6),
         name="project",
     )(gate_pre, up_pre, hidden_grad, proj_hidden, tokens_in, out_grad, proj_model)
 
@@ -252,11 +270,19 @@
 
 
 def summed_over_groups(value):
-    groups = lax.axis_size("dp")
+    groups, model_shards = lax.axis_size("dp"), lax.axis_size("mp")
+    last = model_shards - 1
     for level in range(groups.bit_length() - 1):
-        pairs = [(source, source ^ 2**level) for source in range(groups)]
-        value = value + lax.ppermute(value, "dp", pairs)
-    return value
+        pairs = [
+            (group * model_shards + last, (group ^ 2**level) * model_shards + last)
+            for group in range(groups)
+        ]
+        value = value + lax.ppermute(value, ("dp", "mp"), pairs)
+    result = value
+    for other in range(last):
+        received = lax.ppermute(value, "mp", [(last, other)])
+        result = jnp.where(lax.axis_index("mp") == other, received, result)
+    return result
 
 
 def shards(tokens_in, gate_pre, up_pre, hidden_grad, out_grad, proj_model, proj_hidden):

time: 33.8 us -> 38.2 us (1.13)
  waiting for transfers between devices: 8.06 us -> 19.1 us
  starting transfers between devices: 10.5 us -> 4.45 us
  local copies, waits for them, and re-layouts: 0.9 us -> 0 us
    ppermute x4 -> x5, waiting for transfers between devices: 6.87 us -> 18.1 us  [the longest x1 18.1 us: summed_over_groups(): received = lax.ppermute(value, 'mp', [(last, other)])]
    ppermute x4 -> x5, starting transfers between devices: 10 us -> 3.93 us  [the longest x4 2.64 us: summed_over_groups(): value = value + lax.ppermute(value, ('dp', 'mp'), pairs)]
    unnamed x2 -> x0, local copies, waits for them, and re-layouts: 0.9 us -> none
  transfers between devices with their start and end apart: 5 -> 6, of which waited for: 5 -> 2; matrix products, arithmetic and copies ran while one was open for 0% -> 0% of each run, Pallas kernels for 0% -> 0%
where the time goes in v3:
time: 38.2 us; the launch traced here: 37.9 us
  waiting for transfers between devices  19.1 us (50%)
  Pallas kernels  14.2 us (37%)
  starting transfers between devices  4.45 us (12%)
    ppermute x1, waiting for transfers between devices, summed_over_groups(): received = lax.ppermute(value, 'mp', [(last, other)])  18.1 us
    pallas_call x1, Pallas kernels, project(): pl.pallas_call(project_kernel, out_shape=jax.ShapeDtypeStruct((rows, 2 *...  9.03 us
    pallas_call x1, Pallas kernels, whiten(): pl.pallas_call(functools.partial(whiten_kernel, factor, rows_each), out_s...  4.61 us
    ppermute x4, starting transfers between devices, summed_over_groups(): value = value + lax.ppermute(value, ('dp', 'mp'), pairs)  2.64 us
    ppermute x1, starting transfers between devices, summed_over_groups(): received = lax.ppermute(value, 'mp', [(last, other)])  1.29 us
    ppermute x1, waiting for transfers between devices, shards(): parts.append(lax.ppermute(part, 'mp', pairs))  0.99 us
  transfers between devices with their start and end apart: 6, of which 2 were waited for; matrix products, arithmetic and copies ran while one was open for 0% of the time, Pallas kernels for 0%

profile of v3, /device:TPU:0, one launch (start us, length us, event | category | flops | bytes accessed | tf_op | source)
XLA Modules:
  0.0 37.9 jit_solution(15172061997910651830)
XLA Ops:
  0.0 9.0 %project.1.refs_1_ = f32[128,256]{1,0:T(8,128)S(1)} custom-call(bf16[128,14336]{1,0:T(8,128)(2,1)} %gate.1, bf16[128,14336]{1,0:T(8,128)(2,1)} %up.1, bf16[128,14336]{1,0:T(8,128)(2,1)} %grad.1, bf16[14336,128]{1,0:T(8,128)(2,1)} %proj_hidden.1, bf16[128,4096]{1,0:T(8,128)(2,1)} %tokens.1, bf16[128,4096]{1,0:T(8,128)(2,1)} %outer.1, bf16[4096,128]{1,0:T(8,128)(2,1)} %proj_model.1), custom_call_target="tpu_custom_call" | custom-call | tf_op jit(solution)/shard_map/project/pallas_call | solution.py:123
  9.0 0.5 %collective-permute-start = (f32[128,256]{1,0:T(8,128)S(1)}, f32[128,256]{1,0:T(8,128)S(1)}, u32[]{:S(2)}, u32[]{:S(2)}) collective-permute-start(f32[128,256]{1,0:T(8,128)S(1)} %project.1.refs_1_), channel_id=1, source_target_pairs={{0,1},{1,0},{2,3},{3,2},{4,5},{5,4},{6,7},{7,6},{8,9},{9,8},{10,11... | collective-permute-start | bytes 393224 | tf_op jit(solution)/shard_map/ppermute | solution.py:299
  9.6 1.0 %collective-permute-done.refs_2_ = f32[128,256]{1,0:T(8,128)S(1)} collective-permute-done((f32[128,256]{1,0:T(8,128)S(1)}, f32[128,256]{1,0:T(8,128)S(1)}, u32[]{:S(2)}, u32[]{:S(2)}) %collective-permute-start) | collective-permute-done | bytes 131104 | tf_op jit(solution)/shard_map/ppermute | solution.py:299
  10.5 0.6 %gram.1 = (f32[1,64,128]{2,1,0:T(8,128)S(1)}, f32[32,128]{1,0:T(8,128)S(1)}) custom-call(s32[1]{0:T(128)} %bitcast.refs_0_, f32[128,256]{1,0:T(8,128)S(1)} %project.1.refs_1_, f32[128,256]{1,0:T(8,128)S(1)} %collective-permute-done.refs_2_), custom_call_target="tpu_custom_call" | custom-call | tf_op jit(solution)/shard_map/gram/pallas_call | solution.py:180
  11.1 0.7 %collective-permute-start.1 = (f32[32,128]{1,0:T(8,128)S(1)}, f32[32,128]{1,0:T(8,128)S(1)}, u32[]{:S(2)}, u32[]{:S(2)}) collective-permute-start(f32[32,128]{1,0:T(8,128)S(1)} %get-tuple-element.8), channel_id=1, source_target_pairs={{1,3},{3,1},{5,7},{7,5},{9,11},{11,9},{13,15},{15,13},{17,19},{19,... | collective-permute-start | bytes 49160 | tf_op jit(solution)/shard_map/ppermute | solution.py:280
  11.8 0.0 collective-permute-done.1
  11.8 0.7 %collective-permute-start.2 = (f32[32,128]{1,0:T(8,128)S(1)}, f32[32,128]{1,0:T(8,128)S(1)}, u32[]{:S(2)}, u32[]{:S(2)}) collective-permute-start(f32[32,128]{1,0:T(8,128)S(1)} %add.12), channel_id=1, source_target_pairs={{1,5},{3,7},{5,1},{7,3},{9,13},{11,15},{13,9},{15,11},{17,21},{19,... | collective-permute-start | bytes 49160 | tf_op jit(solution)/shard_map/ppermute | solution.py:280
  12.5 0.0 collective-permute-done.2
  12.5 0.7 %collective-permute-start.3 = (f32[32,128]{1,0:T(8,128)S(1)}, f32[32,128]{1,0:T(8,128)S(1)}, u32[]{:S(2)}, u32[]{:S(2)}) collective-permute-start(f32[32,128]{1,0:T(8,128)S(1)} %add.13), channel_id=1, source_target_pairs={{1,9},{3,11},{5,13},{7,15},{9,1},{11,3},{13,5},{15,7},{17,25},{19,... | collective-permute-start | bytes 49160 | tf_op jit(solution)/shard_map/ppermute | solution.py:280
  13.2 0.0 collective-permute-done.3
  13.2 0.7 %collective-permute-start.4 = (f32[32,128]{1,0:T(8,128)S(1)}, f32[32,128]{1,0:T(8,128)S(1)}, u32[]{:S(2)}, u32[]{:S(2)}) collective-permute-start(f32[32,128]{1,0:T(8,128)S(1)} %add.14), channel_id=1, source_target_pairs={{1,17},{3,19},{5,21},{7,23},{9,25},{11,27},{13,29},{15,31},{17,1},... | collective-permute-start | bytes 49160 | tf_op jit(solution)/shard_map/ppermute | solution.py:280
  13.9 0.0 collective-permute-done.4
  13.9 1.3 %collective-permute-start.5 = (f32[32,128]{1,0:T(8,128)S(1)}, f32[32,128]{1,0:T(8,128)S(1)}, u32[]{:S(2)}, u32[]{:S(2)}) collective-permute-start(f32[32,128]{1,0:T(8,128)S(1)} %add.15), channel_id=1, source_target_pairs={{1,0},{3,2},{5,4},{7,6},{9,8},{11,10},{13,12},{15,14},{17,16},{19,... | collective-permute-start | bytes 49160 | tf_op jit(solution)/shard_map/ppermute | solution.py:283
  15.2 18.1 %collective-permute-done.5 = f32[32,128]{1,0:T(8,128)S(1)} collective-permute-done((f32[32,128]{1,0:T(8,128)S(1)}, f32[32,128]{1,0:T(8,128)S(1)}, u32[]{:S(2)}, u32[]{:S(2)}) %collective-permute-start.5) | collective-permute-done | bytes 16416 | tf_op jit(solution)/shard_map/ppermute | solution.py:283
  33.3 4.6 %whiten.1 = f32[1,64,64]{2,1,0:T(8,128)} custom-call(f32[1,64,128]{2,1,0:T(8,128)S(1)} %get-tuple-element.7.rows_ref, f32[32,128]{1,0:T(8,128)S(1)} %broadcast_select_fusion.gram_ref), custom_call_target="tpu_custom_call" | custom-call | tf_op jit(solution)/shard_map/whiten/pallas_call | solution.py:262
  (5 shorter events, 0.0 us)
Async XLA Ops:
  9.0 1.5 %collective-permute-start = (f32[128,256]{1,0:T(8,128)S(1)}, f32[128,256]{1,0:T(8,128)S(1)}, u32[]{:S(2)}, u32[]{:S(2)}) collective-permute-start(f32[128,256]{1,0:T(8,128)S(1)} %project.1.refs_1_), channel_id=1, source_target_pairs={{0,1},{1,0},{2,3},{3,2},{4,5},{5,4},{6,7},{7,6},{8,9},{9,8},{10,11... | collective-permute-start | bytes 393224 | tf_op jit(solution)/shard_map/ppermute | solution.py:299
  11.1 0.7 %collective-permute-start.1 = (f32[32,128]{1,0:T(8,128)S(1)}, f32[32,128]{1,0:T(8,128)S(1)}, u32[]{:S(2)}, u32[]{:S(2)}) collective-permute-start(f32[32,128]{1,0:T(8,128)S(1)} %get-tuple-element.8), channel_id=1, source_target_pairs={{1,3},{3,1},{5,7},{7,5},{9,11},{11,9},{13,15},{15,13},{17,19},{19,... | collective-permute-start | bytes 49160 | tf_op jit(solution)/shard_map/ppermute | solution.py:280
  11.8 0.7 %collective-permute-start.2 = (f32[32,128]{1,0:T(8,128)S(1)}, f32[32,128]{1,0:T(8,128)S(1)}, u32[]{:S(2)}, u32[]{:S(2)}) collective-permute-start(f32[32,128]{1,0:T(8,128)S(1)} %add.12), channel_id=1, source_target_pairs={{1,5},{3,7},{5,1},{7,3},{9,13},{11,15},{13,9},{15,11},{17,21},{19,... | collective-permute-start | bytes 49160 | tf_op jit(solution)/shard_map/ppermute | solution.py:280
  12.5 0.7 %collective-permute-start.3 = (f32[32,128]{1,0:T(8,128)S(1)}, f32[32,128]{1,0:T(8,128)S(1)}, u32[]{:S(2)}, u32[]{:S(2)}) collective-permute-start(f32[32,128]{1,0:T(8,128)S(1)} %add.13), channel_id=1, source_target_pairs={{1,9},{3,11},{5,13},{7,15},{9,1},{11,3},{13,5},{15,7},{17,25},{19,... | collective-permute-start | bytes 49160 | tf_op jit(solution)/shard_map/ppermute | solution.py:280
  13.2 0.7 %collective-permute-start.4 = (f32[32,128]{1,0:T(8,128)S(1)}, f32[32,128]{1,0:T(8,128)S(1)}, u32[]{:S(2)}, u32[]{:S(2)}) collective-permute-start(f32[32,128]{1,0:T(8,128)S(1)} %add.14), channel_id=1, source_target_pairs={{1,17},{3,19},{5,21},{7,23},{9,25},{11,27},{13,29},{15,31},{17,1},... | collective-permute-start | bytes 49160 | tf_op jit(solution)/shard_map/ppermute | solution.py:280
  13.9 19.4 %collective-permute-start.5 = (f32[32,128]{1,0:T(8,128)S(1)}, f32[32,128]{1,0:T(8,128)S(1)}, u32[]{:S(2)}, u32[]{:S(2)}) collective-permute-start(f32[32,128]{1,0:T(8,128)S(1)} %add.15), channel_id=1, source_target_pairs={{1,0},{3,2},{5,4},{7,6},{9,8},{11,10},{13,12},{15,14},{17,16},{19,... | collective-permute-start | bytes 49160 | tf_op jit(solution)/shard_map/ppermute | solution.py:283

commit v4 on v2

--- a/solution.py
+++ b/solution.py
@@ -11,6 +11,9 @@
 RANK = 64
 LEN = 128
 WIDE = 2 * RANK
+EACH = 1024
+STEP = 256
+AHEAD = 4
 
 highest = lax.Precision.HIGHEST
 whole_vmem = pl.BlockSpec(memory_space=pltpu.VMEM)
@@ -18,11 +21,8 @@
 small = pltpu.CompilerParams(vmem_limit_bytes=8 * 2**20)
 
 
-def pieces_of(width, most):
-    count = most
-    while width % (count * 128):
-        count //= 2
-    return count, width // count
+def cuts_of(width, each):
+    return [(first, min(each, width - first)) for first in range(0, width, each)]
 
 
 def lanes_of(shape):
@@ -33,49 +33,52 @@
     gate_v, up_v, grad_v, hidden_w, tokens_v, outer_v, model_w, sems, model_sems = rest
     rows, hidden_width = gate.shape
     model_width = tokens.shape[1]
-    hidden_count, hidden_each = pieces_of(hidden_width, 8)
-    model_count, model_each = pieces_of(model_width, 4)
-
-    hidden_copies = []
-    for piece in range(hidden_count):
-        cut = pl.ds(piece * hidden_each, hidden_each)
-        hidden_copies.append(
+    hidden_cuts, model_cuts = cuts_of(hidden_width, EACH), cuts_of(model_width, EACH)
+
+    copies = []
+    for piece, (first, size) in enumerate(hidden_cuts):
+        cut = pl.ds(first, size)
+        pairs = [
+            (gate.at[:, cut], gate_v.at[:, cut]),
+            (grad.at[:, cut], grad_v.at[:, cut]),
+            (up.at[:, cut], up_v.at[:, cut]),
+            (proj_hidden.at[cut, :], hidden_w.at[cut, :]),
+        ]
+        copies.append(
             [
-                pltpu.make_async_copy(gate.at[:, cut], gate_v.at[:, cut], sems.at[piece, 0]),
-                pltpu.make_async_copy(grad.at[:, cut], grad_v.at[:, cut], sems.at[piece, 1]),
-                pltpu.make_async_copy(up.at[:, cut], up_v.at[:, cut], sems.at[piece, 2]),
-                pltpu.make_async_copy(
-                    proj_hidden.at[cut, :], hidden_w.at[cut, :], sems.at[piece, 3]
-                ),
+                pltpu.make_async_copy(source, target, sems.at[piece, which])
+                for which, (source, target) in enumerate(pairs)
             ]
         )
-    model_copies = []
-    for piece in range(model_count):
-        cut = pl.ds(piece * model_each, model_each)
-        model_copies.append(
+    for piece, (first, size) in enumerate(model_cuts):
+        cut = pl.ds(first, size)
+        pairs = [
+            (tokens.at[:, cut], tokens_v.at[:, cut]),
+            (outer.at[:, cut], outer_v.at[:, cut]),
+            (proj_model.at[cut, :], model_w.at[cut, :]),
+        ]
+        copies.append(
             [
-                pltpu.make_async_copy(
-                    tokens.at[:, cut], tokens_v.at[:, cut], model_sems.at[piece, 0]
-                ),
-                pltpu.make_async_copy(
-                    outer.at[:, cut], outer_v.at[:, cut], model_sems.at[piece, 1]
-                ),
-                pltpu.make_async_copy(
-                    proj_model.at[cut, :], model_w.at[cut, :], model_sems.at[piece, 2]
-                ),
+                pltpu.make_async_copy(source, target, model_sems.at[piece, which])
+                for which, (source, target) in enumerate(pairs)
             ]
         )
-    for group in hidden_copies + model_copies:
+
+    def arrive(which):
+        for copy in copies[which]:
+            copy.wait()
+        if which + AHEAD < len(copies):
+            for copy in copies[which + AHEAD]:
+                copy.start()
+
+    for group in copies[:AHEAD]:
         for copy in group:
             copy.start()
-
-    step = 256 if hidden_each % 256 == 0 else 128
     hidden_sum = jnp.zeros((2 * rows, WIDE), jnp.float32)
-    for piece in range(hidden_count):
-        for copy in hidden_copies[piece]:
-            copy.wait()
-        for first in range(piece * hidden_each, (piece + 1) * hidden_each, step):
-            cut = slice(first, first + step)
+    for piece, (begin, size) in enumerate(hidden_cuts):
+        arrive(piece)
+        for first, step in cuts_of(size, STEP):
+            cut = slice(begin + first, begin + first + step)
             half = gate_v[:, cut].astype(jnp.float32) * 0.5
             act = half + half * jnp.tanh(half)
             up_grad = (grad_v[:, cut].astype(jnp.float32) * act).astype(jnp.bfloat16)
@@ -83,10 +86,9 @@
             both = jnp.concatenate([up_grad, hidden], axis=0)
             hidden_sum += jnp.dot(both, hidden_w[cut, :], preferred_element_type=jnp.float32)
     model_sum = jnp.zeros((2 * rows, WIDE), jnp.float32)
-    for piece in range(model_count):
-        for copy in model_copies[piece]:
-            copy.wait()
-        cut = slice(piece * model_each, (piece + 1) * model_each)
+    for piece, (begin, size) in enumerate(model_cuts):
+        arrive(len(hidden_cuts) + piece)
+        cut = slice(begin, begin + size)
         both = jnp.concatenate([tokens_v[:, cut], outer_v[:, cut]], axis=0)
         model_sum += jnp.dot(both, model_w[cut, :], preferred_element_type=jnp.float32)
 
@@ -100,8 +102,6 @@
 def project(gate_pre, up_pre, hidden_grad, proj_hidden, tokens_in, out_grad, proj_model):
     rows, hidden_width = gate_pre.shape
     model_width = tokens_in.shape[1]
-    hidden_count, _ = pieces_of(hidden_width, 8)
-    model_count, _ = pieces_of(model_width, 4)
     held = jnp.bfloat16
     return pl.pallas_call(
         project_kernel,
@@ -116,10 +116,10 @@
             pltpu.VMEM((rows, model_width), held),
             pltpu.VMEM((rows, model_width), held),
             pltpu.VMEM((model_width, WIDE), held),
-            pltpu.SemaphoreType.DMA((hidden_count, 4)),
-            pltpu.SemaphoreType.DMA((model_count, 3)),
+            pltpu.SemaphoreType.DMA((len(cuts_of(hidden_width, EACH)), 4)),
+            pltpu.SemaphoreType.DMA((len(cuts_of(model_width, EACH)), 3)),
         ],
-        compiler_params=pltpu.CompilerParams(vmem_limit_bytes=60 * 2**20),
+        compiler_params=pltpu.CompilerParams(vmem_limit_bytes=56 * 10**6),
         name="project",
     )(gate_pre, up_pre, hidden_grad, proj_hidden, tokens_in, out_grad, proj_model)
 
@@ -199,7 +199,7 @@
         factors = {}
         inverses = []
         for k in range(height):
-            inverse = 1.0 / corner[k, k]
+            inverse = pl.reciprocal(corner[k, k], approx=True)
             inverses.append(inverse)
             for m in range(k + 1, height):
                 factor = corner[k, m] * inverse
@@ -252,11 +252,24 @@
 
 
 def summed_over_groups(value):
-    groups = lax.axis_size("dp")
+    groups, model_shards = lax.axis_size("dp"), lax.axis_size("mp")
+    last = model_shards - 1
     for level in range(groups.bit_length() - 1):
-        pairs = [(source, source ^ 2**level) for source in range(groups)]
-        value = value + lax.ppermute(value, "dp", pairs)
-    return value
+        pairs = [
+            (
+                group * model_shards + shard,
+                (group ^ 2**level if shard == last else group) * model_shards + shard,
+            )
+            for group in range(groups)
+            for shard in range(model_shards)
+        ]
+        value = value + lax.ppermute(value, ("dp", "mp"), pairs)
+    result = value
+    for away in range(1, model_shards):
+        pairs = [(source, (source + away) % model_shards) for source in range(model_shards)]
+        received = lax.ppermute(value, "mp", pairs)
+        result = jnp.where(lax.axis_index("mp") == away - 1, received, result)
+    return result
 
 
 def shards(tokens_in, gate_pre, up_pre, hidden_grad, out_grad, proj_model, proj_hidden):

time: 33.8 us -> 36.2 us (1.071)
  starting transfers between devices: 10.5 us -> 20.7 us
  waiting for transfers between devices: 8.06 us -> 1.84 us
  local copies, waits for them, and re-layouts: 0.9 us -> 0 us
  Pallas kernels: 14.1 us -> 13.4 us
    ppermute x4 -> x5, starting transfers between devices: 10 us -> 20.1 us  [the longest x1 17.5 us: summed_over_groups(): received = lax.ppermute(value, 'mp', pairs)]
    ppermute x4 -> x5, waiting for transfers between devices: 6.87 us -> 0.85 us  [the longest x1 0.84 us: summed_over_groups(): received = lax.ppermute(value, 'mp', pairs)]
    unnamed x2 -> x0, local copies, waits for them, and re-layouts: 0.9 us -> none
    pallas_call x1, Pallas kernels: 8.9 us -> 8.18 us  [project(): pl.pallas_call(project_kernel, out_shape=jax.ShapeDtypeStruct((rows, 2 *...]
  transfers between devices with their start and end apart: 5 -> 6, of which waited for: 5 -> 2; matrix products, arithmetic and copies ran while one was open for 0% -> 0% of each run, Pallas kernels for 0% -> 0%
where the time goes in v4:
time: 36.2 us; the launch traced here: 36 us
  starting transfers between devices  20.7 us (57%)
  Pallas kernels  13.4 us (37%)
  waiting for transfers between devices  1.84 us (5%)
    ppermute x1, starting transfers between devices, summed_over_groups(): received = lax.ppermute(value, 'mp', pairs)  17.5 us
    pallas_call x1, Pallas kernels, project(): pl.pallas_call(project_kernel, out_shape=jax.ShapeDtypeStruct((rows, 2 *...  8.18 us
    pallas_call x1, Pallas kernels, whiten(): pl.pallas_call(functools.partial(whiten_kernel, factor, rows_each), out_s...  4.61 us
    ppermute x4, starting transfers between devices, summed_over_groups(): value = value + lax.ppermute(value, ('dp', 'mp'), pairs)  2.64 us
    ppermute x1, waiting for transfers between devices, shards(): parts.append(lax.ppermute(part, 'mp', pairs))  0.99 us
    ppermute x1, waiting for transfers between devices, summed_over_groups(): received = lax.ppermute(value, 'mp', pairs)  0.84 us
  transfers between devices with their start and end apart: 6, of which 2 were waited for; matrix products, arithmetic and copies ran while one was open for 0% of the time, Pallas kernels for 0%

profile of v4, /device:TPU:0, one launch (start us, length us, event | category | flops | bytes accessed | tf_op | source)
XLA Modules:
  0.0 36.0 jit_solution(11999262141570472111)
XLA Ops:
  0.0 8.2 %project.1.refs_1_ = f32[128,256]{1,0:T(8,128)S(1)} custom-call(bf16[128,14336]{1,0:T(8,128)(2,1)} %gate.1, bf16[128,14336]{1,0:T(8,128)(2,1)} %up.1, bf16[128,14336]{1,0:T(8,128)(2,1)} %grad.1, bf16[14336,128]{1,0:T(8,128)(2,1)} %proj_hidden.1, bf16[128,4096]{1,0:T(8,128)(2,1)} %tokens.1, bf16[128,4096]{1,0:T(8,128)(2,1)} %outer.1, bf16[4096,128]{1,0:T(8,128)(2,1)} %proj_model.1), custom_call_target="tpu_custom_call" | custom-call | tf_op jit(solution)/shard_map/project/pallas_call | solution.py:106
  8.2 0.5 %collective-permute-start = (f32[128,256]{1,0:T(8,128)S(1)}, f32[128,256]{1,0:T(8,128)S(1)}, u32[]{:S(2)}, u32[]{:S(2)}) collective-permute-start(f32[128,256]{1,0:T(8,128)S(1)} %project.1.refs_1_), channel_id=1, source_target_pairs={{0,1},{1,0},{2,3},{3,2},{4,5},{5,4},{6,7},{7,6},{8,9},{9,8},{10,11... | collective-permute-start | bytes 393224 | tf_op jit(solution)/shard_map/ppermute | solution.py:286
  8.7 1.0 %collective-permute-done.refs_2_ = f32[128,256]{1,0:T(8,128)S(1)} collective-permute-done((f32[128,256]{1,0:T(8,128)S(1)}, f32[128,256]{1,0:T(8,128)S(1)}, u32[]{:S(2)}, u32[]{:S(2)}) %collective-permute-start) | collective-permute-done | bytes 131104 | tf_op jit(solution)/shard_map/ppermute | solution.py:286
  9.7 0.6 %gram.1 = (f32[1,64,128]{2,1,0:T(8,128)S(1)}, f32[32,128]{1,0:T(8,128)S(1)}) custom-call(s32[1]{0:T(128)} %bitcast.refs_0_, f32[128,256]{1,0:T(8,128)S(1)} %project.1.refs_1_, f32[128,256]{1,0:T(8,128)S(1)} %collective-permute-done.refs_2_), custom_call_target="tpu_custom_call" | custom-call | tf_op jit(solution)/shard_map/gram/pallas_call | solution.py:162
  10.3 0.7 %collective-permute-start.1 = (f32[32,128]{1,0:T(8,128)S(1)}, f32[32,128]{1,0:T(8,128)S(1)}, u32[]{:S(2)}, u32[]{:S(2)}) collective-permute-start(f32[32,128]{1,0:T(8,128)S(1)} %get-tuple-element.8), channel_id=1, source_target_pairs={{0,0},{1,3},{2,2},{3,1},{4,4},{5,7},{6,6},{7,5},{8,8},{9,11},{10,1... | collective-permute-start | bytes 49160 | tf_op jit(solution)/shard_map/ppermute | solution.py:266
  10.9 0.0 collective-permute-done.1
  11.0 0.7 %collective-permute-start.2 = (f32[32,128]{1,0:T(8,128)S(1)}, f32[32,128]{1,0:T(8,128)S(1)}, u32[]{:S(2)}, u32[]{:S(2)}) collective-permute-start(f32[32,128]{1,0:T(8,128)S(1)} %add.12), channel_id=1, source_target_pairs={{0,0},{1,5},{2,2},{3,7},{4,4},{5,1},{6,6},{7,3},{8,8},{9,13},{10,1... | collective-permute-start | bytes 49160 | tf_op jit(solution)/shard_map/ppermute | solution.py:266
  11.6 0.0 collective-permute-done.2
  11.7 0.7 %collective-permute-start.3 = (f32[32,128]{1,0:T(8,128)S(1)}, f32[32,128]{1,0:T(8,128)S(1)}, u32[]{:S(2)}, u32[]{:S(2)}) collective-permute-start(f32[32,128]{1,0:T(8,128)S(1)} %add.13), channel_id=1, source_target_pairs={{0,0},{1,9},{2,2},{3,11},{4,4},{5,13},{6,6},{7,15},{8,8},{9,1},{10... | collective-permute-start | bytes 49160 | tf_op jit(solution)/shard_map/ppermute | solution.py:266
  12.3 0.0 collective-permute-done.3
  12.3 0.7 %collective-permute-start.4 = (f32[32,128]{1,0:T(8,128)S(1)}, f32[32,128]{1,0:T(8,128)S(1)}, u32[]{:S(2)}, u32[]{:S(2)}) collective-permute-start(f32[32,128]{1,0:T(8,128)S(1)} %add.14), channel_id=1, source_target_pairs={{0,0},{1,17},{2,2},{3,19},{4,4},{5,21},{6,6},{7,23},{8,8},{9,25},{... | collective-permute-start | bytes 49160 | tf_op jit(solution)/shard_map/ppermute | solution.py:266
  13.0 0.0 collective-permute-done.4
  13.0 17.5 %collective-permute-start.5 = (f32[32,128]{1,0:T(8,128)S(1)}, f32[32,128]{1,0:T(8,128)S(1)}, u32[]{:S(2)}, u32[]{:S(2)}) collective-permute-start(f32[32,128]{1,0:T(8,128)S(1)} %add.15), channel_id=1, source_target_pairs={{0,1},{1,0},{2,3},{3,2},{4,5},{5,4},{6,7},{7,6},{8,9},{9,8},{10,11... | collective-permute-start | bytes 49160 | tf_op jit(solution)/shard_map/ppermute | solution.py:270
  30.5 0.8 %collective-permute-done.5 = f32[32,128]{1,0:T(8,128)S(1)} collective-permute-done((f32[32,128]{1,0:T(8,128)S(1)}, f32[32,128]{1,0:T(8,128)S(1)}, u32[]{:S(2)}, u32[]{:S(2)}) %collective-permute-start.5) | collective-permute-done | bytes 16416 | tf_op jit(solution)/shard_map/ppermute | solution.py:270
  31.4 4.6 %whiten.1 = f32[1,64,64]{2,1,0:T(8,128)} custom-call(f32[1,64,128]{2,1,0:T(8,128)S(1)} %get-tuple-element.7.rows_ref, f32[32,128]{1,0:T(8,128)S(1)} %broadcast_select_fusion.gram_ref), custom_call_target="tpu_custom_call" | custom-call | tf_op jit(solution)/shard_map/whiten/pallas_call | solution.py:244
  (5 shorter events, 0.0 us)
Async XLA Ops:
  8.2 1.5 %collective-permute-start = (f32[128,256]{1,0:T(8,128)S(1)}, f32[128,256]{1,0:T(8,128)S(1)}, u32[]{:S(2)}, u32[]{:S(2)}) collective-permute-start(f32[128,256]{1,0:T(8,128)S(1)} %project.1.refs_1_), channel_id=1, source_target_pairs={{0,1},{1,0},{2,3},{3,2},{4,5},{5,4},{6,7},{7,6},{8,9},{9,8},{10,11... | collective-permute-start | bytes 393224 | tf_op jit(solution)/shard_map/ppermute | solution.py:286
  10.3 0.7 %collective-permute-start.1 = (f32[32,128]{1,0:T(8,128)S(1)}, f32[32,128]{1,0:T(8,128)S(1)}, u32[]{:S(2)}, u32[]{:S(2)}) collective-permute-start(f32[32,128]{1,0:T(8,128)S(1)} %get-tuple-element.8), channel_id=1, source_target_pairs={{0,0},{1,3},{2,2},{3,1},{4,4},{5,7},{6,6},{7,5},{8,8},{9,11},{10,1... | collective-permute-start | bytes 49160 | tf_op jit(solution)/shard_map/ppermute | solution.py:266
  11.0 0.7 %collective-permute-start.2 = (f32[32,128]{1,0:T(8,128)S(1)}, f32[32,128]{1,0:T(8,128)S(1)}, u32[]{:S(2)}, u32[]{:S(2)}) collective-permute-start(f32[32,128]{1,0:T(8,128)S(1)} %add.12), channel_id=1, source_target_pairs={{0,0},{1,5},{2,2},{3,7},{4,4},{5,1},{6,6},{7,3},{8,8},{9,13},{10,1... | collective-permute-start | bytes 49160 | tf_op jit(solution)/shard_map/ppermute | solution.py:266
  11.7 0.7 %collective-permute-start.3 = (f32[32,128]{1,0:T(8,128)S(1)}, f32[32,128]{1,0:T(8,128)S(1)}, u32[]{:S(2)}, u32[]{:S(2)}) collective-permute-start(f32[32,128]{1,0:T(8,128)S(1)} %add.13), channel_id=1, source_target_pairs={{0,0},{1,9},{2,2},{3,11},{4,4},{5,13},{6,6},{7,15},{8,8},{9,1},{10... | collective-permute-start | bytes 49160 | tf_op jit(solution)/shard_map/ppermute | solution.py:266
  12.3 0.7 %collective-permute-start.4 = (f32[32,128]{1,0:T(8,128)S(1)}, f32[32,128]{1,0:T(8,128)S(1)}, u32[]{:S(2)}, u32[]{:S(2)}) collective-permute-start(f32[32,128]{1,0:T(8,128)S(1)} %add.14), channel_id=1, source_target_pairs={{0,0},{1,17},{2,2},{3,19},{4,4},{5,21},{6,6},{7,23},{8,8},{9,25},{... | collective-permute-start | bytes 49160 | tf_op jit(solution)/shard_map/ppermute | solution.py:266
  13.0 18.3 %collective-permute-start.5 = (f32[32,128]{1,0:T(8,128)S(1)}, f32[32,128]{1,0:T(8,128)S(1)}, u32[]{:S(2)}, u32[]{:S(2)}) collective-permute-start(f32[32,128]{1,0:T(8,128)S(1)} %add.15), channel_id=1, source_target_pairs={{0,1},{1,0},{2,3},{3,2},{4,5},{5,4},{6,7},{7,6},{8,9},{9,8},{10,11... | collective-permute-start | bytes 49160 | tf_op jit(solution)/shard_map/ppermute | solution.py:270

commit v5 on v4

--- a/solution.py
+++ b/solution.py
@@ -74,17 +74,33 @@
     for group in copies[:AHEAD]:
         for copy in group:
             copy.start()
-    hidden_sum = jnp.zeros((2 * rows, WIDE), jnp.float32)
-    for piece, (begin, size) in enumerate(hidden_cuts):
-        arrive(piece)
+    def gated(begin, size):
+        parts = []
         for first, step in cuts_of(size, STEP):
             cut = slice(begin + first, begin + first + step)
             half = gate_v[:, cut].astype(jnp.float32) * 0.5
             act = half + half * jnp.tanh(half)
             up_grad = (grad_v[:, cut].astype(jnp.float32) * act).astype(jnp.bfloat16)
             hidden = (act * up_v[:, cut].astype(jnp.float32)).astype(jnp.bfloat16)
-            both = jnp.concatenate([up_grad, hidden], axis=0)
-            hidden_sum += jnp.dot(both, hidden_w[cut, :], preferred_element_type=jnp.float32)
+            parts.append(jnp.concatenate([up_grad, hidden], axis=0))
+        return jnp.concatenate(parts, axis=1)
+
+    hidden_sum = jnp.zeros((2 * rows, WIDE), jnp.float32)
+    both = None
+    for piece, (begin, size) in enumerate(hidden_cuts):
+        arrive(piece)
+        if piece:
+            before, width = hidden_cuts[piece - 1]
+            hidden_sum += jnp.dot(
+                both,
+                hidden_w[before : before + width, :],
+                preferred_element_type=jnp.float32,
+            )
+        both = gated(begin, size)
+    before, width = hidden_cuts[-1]
+    hidden_sum += jnp.dot(
+        both, hidden_w[before : before + width, :], preferred_element_type=jnp.float32
+    )
     model_sum = jnp.zeros((2 * rows, WIDE), jnp.float32)
     for piece, (begin, size) in enumerate(model_cuts):
         arrive(len(hidden_cuts) + piece)
@@ -197,34 +213,48 @@
         if held + 1 < blocks:
             ahead = [across(state[held + 1], base + k) for k in range(height)]
         factors = {}
-        inverses = []
-        for k in range(height):
-            inverse = pl.reciprocal(corner[k, k], approx=True)
-            inverses.append(inverse)
-            for m in range(k + 1, height):
-                factor = corner[k, m] * inverse
-                factors[k, m] = factor
+        solved = [None] * height
+        for k in range(0, height, 2):
+            first, cross, second = corner[k, k], corner[k, k + 1], corner[k + 1, k + 1]
+            determinant = first * second - cross * cross
+            inverse = pl.reciprocal(determinant, approx=True)
+            solved[k] = (second * rows[k] - cross * rows[k + 1]) * inverse
+            solved[k + 1] = (first * rows[k + 1] - cross * rows[k]) * inverse
+            for m in range(k + 2, height):
+                left, right = corner[k, m], corner[k + 1, m]
+                upper = second * left - cross * right
+                lower = first * right - cross * left
                 for n in range(m, height):
-                    corner[m, n] = corner[m, n] - factor * corner[k, n]
-                rows[m] = rows[m] - factor * rows[k]
-                if ahead is not None:
-                    ahead[m] = ahead[m] - factor * ahead[k]
+                    taken = upper * corner[k, n] + lower * corner[k + 1, n]
+                    corner[m, n] = corner[m, n] - taken * inverse
+                factors[k, m], factors[k + 1, m] = upper * inverse, lower * inverse
+                for several in (rows, ahead):
+                    if several is not None:
+                        several[m] = several[m] - (
+                            factors[k, m] * several[k] + factors[k + 1, m] * several[k + 1]
+                        )
         if ahead is not None:
-            taken = [ahead[k] * (inverses[k] * rows[k]) for k in range(height)]
+            taken = [ahead[k] * solved[k] for k in range(height)]
             while len(taken) > 1:
                 taken = [left + right for left, right in zip(taken[::2], taken[1::2])]
             state[held + 1] = state[held + 1] - taken[0]
         if held + 2 < blocks:
-            back = [inverses[k] * rows[k] for k in range(height)]
-            for k in reversed(range(height)):
-                for m in range(k):
-                    back[m] = back[m] - factors[m, k] * back[k]
+            back = list(solved)
+            for m in reversed(range(2, height)):
+                for k in range(m - m % 2):
+                    back[k] = back[k] - factors[k, m] * back[m]
             for other in range(held + 2, blocks):
                 for k in range(height):
                     state[other] = state[other] - across(state[other], base + k) * back[k]
-        block = rows[0] * lax.rsqrt(corner[0, 0])
-        for k in range(1, height):
-            block = jnp.where(sub == k, rows[k] * lax.rsqrt(corner[k, k]), block)
+        block = jnp.zeros_like(own)
+        for k in range(0, height, 2):
+            first, cross, second = corner[k, k], corner[k, k + 1], corner[k + 1, k + 1]
+            ratio = cross * pl.reciprocal(first, approx=True)
+            final = second - cross * ratio
+            block = jnp.where(sub == k, rows[k] * lax.rsqrt(first), block)
+            block = jnp.where(
+                sub == k + 1, (rows[k + 1] - ratio * rows[k]) * lax.rsqrt(final), block
+            )
         done.append(block)
     return done
 
@@ -253,23 +283,15 @@
 
 def summed_over_groups(value):
     groups, model_shards = lax.axis_size("dp"), lax.axis_size("mp")
-    last = model_shards - 1
+    other = 1 if model_shards % 2 == 0 else 0
     for level in range(groups.bit_length() - 1):
         pairs = [
-            (
-                group * model_shards + shard,
-                (group ^ 2**level if shard == last else group) * model_shards + shard,
-            )
+            (group * model_shards + shard, (group ^ 2**level) * model_shards + (shard ^ other))
             for group in range(groups)
             for shard in range(model_shards)
         ]
         value = value + lax.ppermute(value, ("dp", "mp"), pairs)
-    result = value
-    for away in range(1, model_shards):
-        pairs = [(source, (source + away) % model_shards) for source in range(model_shards)]
-        received = lax.ppermute(value, "mp", pairs)
-        result = jnp.where(lax.axis_index("mp") == away - 1, received, result)
-    return result
+    return value
 
 
 def shards(tokens_in, gate_pre, up_pre, hidden_grad, out_grad, proj_model, proj_hidden):

time: 36.2 us -> 30.2 us (0.83)
  starting transfers between devices: 20.7 us -> 9.39 us
  waiting for transfers between devices: 1.84 us -> 6.76 us
  Pallas kernels: 13.4 us -> 13.9 us
    ppermute x1 -> x0, starting transfers between devices: 17.5 us -> none  [summed_over_groups(): received = lax.ppermute(value, 'mp', pairs)]
    ppermute x4, starting transfers between devices: 2.64 us -> 8.87 us  [summed_over_groups(): value = value + lax.ppermute(value, ('dp', 'mp'), pairs)]
    ppermute x4, waiting for transfers between devices: 0.01 us -> 5.77 us  [summed_over_groups(): value = value + lax.ppermute(value, ('dp', 'mp'), pairs)]
    ppermute x1 -> x0, waiting for transfers between devices: 0.84 us -> none  [summed_over_groups(): received = lax.ppermute(value, 'mp', pairs)]
    pallas_call x1, Pallas kernels: 8.18 us -> 8.72 us  [project(): pl.pallas_call(project_kernel, out_shape=jax.ShapeDtypeStruct((rows, 2 *...]
  transfers between devices with their start and end apart: 6 -> 5, of which waited for: 2 -> 5; matrix products, arithmetic and copies ran while one was open for 0% -> 0% of each run, Pallas kernels for 0% -> 0%
where the time goes in v5:
time: 30.2 us; the launch traced here: 30.1 us
  Pallas kernels  13.9 us (46%)
  starting transfers between devices  9.39 us (31%)
  waiting for transfers between devices  6.76 us (22%)
    ppermute x4, starting transfers between devices, summed_over_groups(): value = value + lax.ppermute(value, ('dp', 'mp'), pairs)  8.87 us
    pallas_call x1, Pallas kernels, project(): pl.pallas_call(project_kernel, out_shape=jax.ShapeDtypeStruct((rows, 2 *...  8.72 us
    ppermute x4, waiting for transfers between devices, summed_over_groups(): value = value + lax.ppermute(value, ('dp', 'mp'), pairs)  5.77 us
    pallas_call x1, Pallas kernels, whiten(): pl.pallas_call(functools.partial(whiten_kernel, factor, rows_each), out_s...  4.58 us
    ppermute x1, waiting for transfers between devices, shards(): parts.append(lax.ppermute(part, 'mp', pairs))  0.99 us
  transfers between devices with their start and end apart: 5, of which 5 were waited for; matrix products, arithmetic and copies ran while one was open for 0% of the time, Pallas kernels for 0%

profile of v5, /device:TPU:0, one launch (start us, length us, event | category | flops | bytes accessed | tf_op | source)
XLA Modules:
  0.0 30.1 jit_solution(12067930672471877725)
XLA Ops:
  0.0 8.7 %project.1.refs_1_ = f32[128,256]{1,0:T(8,128)S(1)} custom-call(bf16[128,14336]{1,0:T(8,128)(2,1)} %gate.1, bf16[128,14336]{1,0:T(8,128)(2,1)} %up.1, bf16[128,14336]{1,0:T(8,128)(2,1)} %grad.1, bf16[14336,128]{1,0:T(8,128)(2,1)} %proj_hidden.1, bf16[128,4096]{1,0:T(8,128)(2,1)} %tokens.1, bf16[128,4096]{1,0:T(8,128)(2,1)} %outer.1, bf16[4096,128]{1,0:T(8,128)(2,1)} %proj_model.1), custom_call_target="tpu_custom_call" | custom-call | tf_op jit(solution)/shard_map/project/pallas_call | solution.py:122
  8.7 0.5 %collective-permute-start = (f32[128,256]{1,0:T(8,128)S(1)}, f32[128,256]{1,0:T(8,128)S(1)}, u32[]{:S(2)}, u32[]{:S(2)}) collective-permute-start(f32[128,256]{1,0:T(8,128)S(1)} %project.1.refs_1_), channel_id=1, source_target_pairs={{0,1},{1,0},{2,3},{3,2},{4,5},{5,4},{6,7},{7,6},{8,9},{9,8},{10,11... | collective-permute-start | bytes 393224 | tf_op jit(solution)/shard_map/ppermute | solution.py:308
  9.2 1.0 %collective-permute-done.refs_2_ = f32[128,256]{1,0:T(8,128)S(1)} collective-permute-done((f32[128,256]{1,0:T(8,128)S(1)}, f32[128,256]{1,0:T(8,128)S(1)}, u32[]{:S(2)}, u32[]{:S(2)}) %collective-permute-start) | collective-permute-done | bytes 131104 | tf_op jit(solution)/shard_map/ppermute | solution.py:308
  10.2 0.6 %gram.1 = (f32[1,64,128]{2,1,0:T(8,128)S(1)}, f32[32,128]{1,0:T(8,128)S(1)}) custom-call(s32[1]{0:T(128)} %bitcast.refs_0_, f32[128,256]{1,0:T(8,128)S(1)} %project.1.refs_1_, f32[128,256]{1,0:T(8,128)S(1)} %collective-permute-done.refs_2_), custom_call_target="tpu_custom_call" | custom-call | tf_op jit(solution)/shard_map/gram/pallas_call | solution.py:178
  10.8 2.6 %collective-permute-start.1 = (f32[32,128]{1,0:T(8,128)S(1)}, f32[32,128]{1,0:T(8,128)S(1)}, u32[]{:S(2)}, u32[]{:S(2)}) collective-permute-start(f32[32,128]{1,0:T(8,128)S(1)} %get-tuple-element.8), channel_id=1, source_target_pairs={{0,3},{1,2},{2,1},{3,0},{4,7},{5,6},{6,5},{7,4},{8,11},{9,10},{10,... | collective-permute-start | bytes 49160 | tf_op jit(solution)/shard_map/ppermute | solution.py:293
  13.4 1.4 %collective-permute-done.1 = f32[32,128]{1,0:T(8,128)S(1)} collective-permute-done((f32[32,128]{1,0:T(8,128)S(1)}, f32[32,128]{1,0:T(8,128)S(1)}, u32[]{:S(2)}, u32[]{:S(2)}) %collective-permute-start.1) | collective-permute-done | bytes 16416 | tf_op jit(solution)/shard_map/ppermute | solution.py:293
  14.9 1.7 %collective-permute-start.2 = (f32[32,128]{1,0:T(8,128)S(1)}, f32[32,128]{1,0:T(8,128)S(1)}, u32[]{:S(2)}, u32[]{:S(2)}) collective-permute-start(f32[32,128]{1,0:T(8,128)S(1)} %add.12), channel_id=1, source_target_pairs={{0,5},{1,4},{2,7},{3,6},{4,1},{5,0},{6,3},{7,2},{8,13},{9,12},{10,... | collective-permute-start | bytes 49160 | tf_op jit(solution)/shard_map/ppermute | solution.py:293
  16.6 1.4 %collective-permute-done.2 = f32[32,128]{1,0:T(8,128)S(1)} collective-permute-done((f32[32,128]{1,0:T(8,128)S(1)}, f32[32,128]{1,0:T(8,128)S(1)}, u32[]{:S(2)}, u32[]{:S(2)}) %collective-permute-start.2) | collective-permute-done | bytes 16416 | tf_op jit(solution)/shard_map/ppermute | solution.py:293
  18.1 1.8 %collective-permute-start.3 = (f32[32,128]{1,0:T(8,128)S(1)}, f32[32,128]{1,0:T(8,128)S(1)}, u32[]{:S(2)}, u32[]{:S(2)}) collective-permute-start(f32[32,128]{1,0:T(8,128)S(1)} %add.13), channel_id=1, source_target_pairs={{0,9},{1,8},{2,11},{3,10},{4,13},{5,12},{6,15},{7,14},{8,1},{9,0},... | collective-permute-start | bytes 49160 | tf_op jit(solution)/shard_map/ppermute | solution.py:293
  19.8 1.4 %collective-permute-done.3 = f32[32,128]{1,0:T(8,128)S(1)} collective-permute-done((f32[32,128]{1,0:T(8,128)S(1)}, f32[32,128]{1,0:T(8,128)S(1)}, u32[]{:S(2)}, u32[]{:S(2)}) %collective-permute-start.3) | collective-permute-done | bytes 16416 | tf_op jit(solution)/shard_map/ppermute | solution.py:293
  21.3 2.7 %collective-permute-start.4 = (f32[32,128]{1,0:T(8,128)S(1)}, f32[32,128]{1,0:T(8,128)S(1)}, u32[]{:S(2)}, u32[]{:S(2)}) collective-permute-start(f32[32,128]{1,0:T(8,128)S(1)} %add.14), channel_id=1, source_target_pairs={{0,17},{1,16},{2,19},{3,18},{4,21},{5,20},{6,23},{7,22},{8,25},{9,... | collective-permute-start | bytes 49160 | tf_op jit(solution)/shard_map/ppermute | solution.py:293
  24.0 1.4 %collective-permute-done.4 = f32[32,128]{1,0:T(8,128)S(1)} collective-permute-done((f32[32,128]{1,0:T(8,128)S(1)}, f32[32,128]{1,0:T(8,128)S(1)}, u32[]{:S(2)}, u32[]{:S(2)}) %collective-permute-start.4) | collective-permute-done | bytes 16416 | tf_op jit(solution)/shard_map/ppermute | solution.py:293
  25.5 4.6 %whiten.1 = f32[1,64,64]{2,1,0:T(8,128)} custom-call(f32[1,64,128]{2,1,0:T(8,128)S(1)} %get-tuple-element.7.rows_ref, f32[32,128]{1,0:T(8,128)S(1)} %add.15.gram_ref), custom_call_target="tpu_custom_call" | custom-call | tf_op jit(solution)/shard_map/whiten/pallas_call | solution.py:274
  (4 shorter events, 0.0 us)
Async XLA Ops:
  8.7 1.5 %collective-permute-start = (f32[128,256]{1,0:T(8,128)S(1)}, f32[128,256]{1,0:T(8,128)S(1)}, u32[]{:S(2)}, u32[]{:S(2)}) collective-permute-start(f32[128,256]{1,0:T(8,128)S(1)} %project.1.refs_1_), channel_id=1, source_target_pairs={{0,1},{1,0},{2,3},{3,2},{4,5},{5,4},{6,7},{7,6},{8,9},{9,8},{10,11... | collective-permute-start | bytes 393224 | tf_op jit(solution)/shard_map/ppermute | solution.py:308
  10.8 4.1 %collective-permute-start.1 = (f32[32,128]{1,0:T(8,128)S(1)}, f32[32,128]{1,0:T(8,128)S(1)}, u32[]{:S(2)}, u32[]{:S(2)}) collective-permute-start(f32[32,128]{1,0:T(8,128)S(1)} %get-tuple-element.8), channel_id=1, source_target_pairs={{0,3},{1,2},{2,1},{3,0},{4,7},{5,6},{6,5},{7,4},{8,11},{9,10},{10,... | collective-permute-start | bytes 49160 | tf_op jit(solution)/shard_map/ppermute | solution.py:293
  14.9 3.2 %collective-permute-start.2 = (f32[32,128]{1,0:T(8,128)S(1)}, f32[32,128]{1,0:T(8,128)S(1)}, u32[]{:S(2)}, u32[]{:S(2)}) collective-permute-start(f32[32,128]{1,0:T(8,128)S(1)} %add.12), channel_id=1, source_target_pairs={{0,5},{1,4},{2,7},{3,6},{4,1},{5,0},{6,3},{7,2},{8,13},{9,12},{10,... | collective-permute-start | bytes 49160 | tf_op jit(solution)/shard_map/ppermute | solution.py:293
  18.1 3.2 %collective-permute-start.3 = (f32[32,128]{1,0:T(8,128)S(1)}, f32[32,128]{1,0:T(8,128)S(1)}, u32[]{:S(2)}, u32[]{:S(2)}) collective-permute-start(f32[32,128]{1,0:T(8,128)S(1)} %add.13), channel_id=1, source_target_pairs={{0,9},{1,8},{2,11},{3,10},{4,13},{5,12},{6,15},{7,14},{8,1},{9,0},... | collective-permute-start | bytes 49160 | tf_op jit(solution)/shard_map/ppermute | solution.py:293
  21.3 4.2 %collective-permute-start.4 = (f32[32,128]{1,0:T(8,128)S(1)}, f32[32,128]{1,0:T(8,128)S(1)}, u32[]{:S(2)}, u32[]{:S(2)}) collective-permute-start(f32[32,128]{1,0:T(8,128)S(1)} %add.14), channel_id=1, source_target_pairs={{0,17},{1,16},{2,19},{3,18},{4,21},{5,20},{6,23},{7,22},{8,25},{9,... | collective-permute-start | bytes 49160 | tf_op jit(solution)/shard_map/ppermute | solution.py:293

commit v6 on v5

--- a/solution.py
+++ b/solution.py
@@ -21,98 +21,96 @@
 small = pltpu.CompilerParams(vmem_limit_bytes=8 * 2**20)
 
 
-def cuts_of(width, each):
-    return [(first, min(each, width - first)) for first in range(0, width, each)]
-
-
 def lanes_of(shape):
     return lax.broadcasted_iota(jnp.int32, shape, len(shape) - 1)
 
 
 def project_kernel(gate, up, grad, proj_hidden, tokens, outer, proj_model, out, *rest):
-    gate_v, up_v, grad_v, hidden_w, tokens_v, outer_v, model_w, sems, model_sems = rest
-    rows, hidden_width = gate.shape
-    model_width = tokens.shape[1]
-    hidden_cuts, model_cuts = cuts_of(hidden_width, EACH), cuts_of(model_width, EACH)
-
-    copies = []
-    for piece, (first, size) in enumerate(hidden_cuts):
-        cut = pl.ds(first, size)
+    gate_v, up_v, grad_v, hidden_w, tokens_v, outer_v, model_w = rest[:7]
+    hidden_sum, model_sum, sems, model_sems = rest[7:]
+    rows = gate.shape[0]
+    hidden_each, model_each = math.gcd(gate.shape[1], EACH), math.gcd(tokens.shape[1], EACH)
+    hidden_count = gate.shape[1] // hidden_each
+    model_count = tokens.shape[1] // model_each
+
+    def hidden_copies(piece):
+        cut = pl.ds(pl.multiple_of(piece * hidden_each, hidden_each), hidden_each)
         pairs = [
             (gate.at[:, cut], gate_v.at[:, cut]),
             (grad.at[:, cut], grad_v.at[:, cut]),
             (up.at[:, cut], up_v.at[:, cut]),
             (proj_hidden.at[cut, :], hidden_w.at[cut, :]),
         ]
-        copies.append(
-            [
-                pltpu.make_async_copy(source, target, sems.at[piece, which])
-                for which, (source, target) in enumerate(pairs)
-            ]
-        )
-    for piece, (first, size) in enumerate(model_cuts):
-        cut = pl.ds(first, size)
+        return [
+            pltpu.make_async_copy(source, target, sems.at[piece, which])
+            for which, (source, target) in enumerate(pairs)
+        ]
+
+    def model_copies(piece):
+        cut = pl.ds(pl.multiple_of(piece * model_each, model_each), model_each)
         pairs = [
             (tokens.at[:, cut], tokens_v.at[:, cut]),
             (outer.at[:, cut], outer_v.at[:, cut]),
             (proj_model.at[cut, :], model_w.at[cut, :]),
         ]
-        copies.append(
-            [
-                pltpu.make_async_copy(source, target, model_sems.at[piece, which])
-                for which, (source, target) in enumerate(pairs)
-            ]
-        )
-
-    def arrive(which):
-        for copy in copies[which]:
+        return [
+            pltpu.make_async_copy(source, target, model_sems.at[piece, which])
+            for which, (source, target) in enumerate(pairs)
+        ]
+
+    def start(copies):
+        for copy in copies:
+            copy.start()
+
+    def arrive(copies):
+        for copy in copies:
             copy.wait()
-        if which + AHEAD < len(copies):
-            for copy in copies[which + AHEAD]:
-                copy.start()
-
-    for group in copies[:AHEAD]:
-        for copy in group:
-            copy.start()
-    def gated(begin, size):
-        parts = []
-        for first, step in cuts_of(size, STEP):
-            cut = slice(begin + first, begin + first + step)
+
+    ahead = min(AHEAD, hidden_count)
+    for piece in range(ahead):
+        start(hidden_copies(piece))
+    hidden_sum[...] = jnp.zeros_like(hidden_sum)
+    model_sum[...] = jnp.zeros_like(model_sum)
+
+    @pl.loop(0, hidden_count)
+    def _(piece):
+        arrive(hidden_copies(piece))
+
+        @pl.when(piece + ahead < hidden_count)
+        def _():
+            start(hidden_copies(piece + ahead))
+
+        @pl.when(piece + ahead == hidden_count)
+        def _():
+            for other in range(model_count):
+                start(model_copies(other))
+
+        base = piece * hidden_each
+        total = None
+        for first in range(0, hidden_each, STEP):
+            step = min(STEP, hidden_each - first)
+            cut = pl.ds(pl.multiple_of(base + first, 128), step)
             half = gate_v[:, cut].astype(jnp.float32) * 0.5
             act = half + half * jnp.tanh(half)
             up_grad = (grad_v[:, cut].astype(jnp.float32) * act).astype(jnp.bfloat16)
             hidden = (act * up_v[:, cut].astype(jnp.float32)).astype(jnp.bfloat16)
-            parts.append(jnp.concatenate([up_grad, hidden], axis=0))
-        return jnp.concatenate(parts, axis=1)
-
-    hidden_sum = jnp.zeros((2 * rows, WIDE), jnp.float32)
-    both = None
-    for piece, (begin, size) in enumerate(hidden_cuts):
-        arrive(piece)
-        if piece:
-            before, width = hidden_cuts[piece - 1]
-            hidden_sum += jnp.dot(
-                both,
-                hidden_w[before : before + width, :],
-                preferred_element_type=jnp.float32,
-            )
-        both = gated(begin, size)
-    before, width = hidden_cuts[-1]
-    hidden_sum += jnp.dot(
-        both, hidden_w[before : before + width, :], preferred_element_type=jnp.float32
-    )
-    model_sum = jnp.zeros((2 * rows, WIDE), jnp.float32)
-    for piece, (begin, size) in enumerate(model_cuts):
-        arrive(len(hidden_cuts) + piece)
-        cut = slice(begin, begin + size)
+            both = jnp.concatenate([up_grad, hidden], axis=0)
+            part = jnp.dot(both, hidden_w[cut, :], preferred_element_type=jnp.float32)
+            total = part if total is None else total + part
+        hidden_sum[...] += total
+
+    @pl.loop(0, model_count)
+    def _(piece):
+        arrive(model_copies(piece))
+        cut = pl.ds(pl.multiple_of(piece * model_each, model_each), model_each)
         both = jnp.concatenate([tokens_v[:, cut], outer_v[:, cut]], axis=0)
-        model_sum += jnp.dot(both, model_w[cut, :], preferred_element_type=jnp.float32)
+        model_sum[...] += jnp.dot(both, model_w[cut, :], preferred_element_type=jnp.float32)
 
     low = lanes_of((rows, WIDE)) < RANK
-    upward = pltpu.roll(hidden_sum[:rows], RANK, 1)
-    hidden_side = pltpu.roll(hidden_sum[rows:], RANK, 1)
-    out[:, :WIDE] = jnp.where(low, model_sum[:rows], upward)
-    out[:, WIDE:] = jnp.where(low, hidden_side, model_sum[rows:])
+    upward = pltpu.roll(hidden_sum[:rows, :], RANK, 1)
+    hidden_side = pltpu.roll(hidden_sum[rows:, :], RANK, 1)
+    out[:, :WIDE] = jnp.where(low, model_sum[:rows, :], upward)
+    out[:, WIDE:] = jnp.where(low, hidden_side, model_sum[rows:, :])
 
 
 def project(gate_pre, up_pre, hidden_grad, proj_hidden, tokens_in, out_grad, proj_model):
@@ -132,8 +130,10 @@
             pltpu.VMEM((rows, model_width), held),
             pltpu.VMEM((rows, model_width), held),
             pltpu.VMEM((model_width, WIDE), held),
-            pltpu.SemaphoreType.DMA((len(cuts_of(hidden_width, EACH)), 4)),
-            pltpu.SemaphoreType.DMA((len(cuts_of(model_width, EACH)), 3)),
+            pltpu.VMEM((2 * rows, WIDE), jnp.float32),
+            pltpu.VMEM((2 * rows, WIDE), jnp.float32),
+            pltpu.SemaphoreType.DMA((hidden_width // math.gcd(hidden_width, EACH), 4)),
+            pltpu.SemaphoreType.DMA((model_width // math.gcd(model_width, EACH), 3)),
         ],
         compiler_params=pltpu.CompilerParams(vmem_limit_bytes=56 * 10**6),
         name="project",

time: 30.2 us -> 29.8 us (0.987)
  Pallas kernels: 13.9 us -> 13.5 us
    pallas_call x1, Pallas kernels: 8.72 us -> 8.3 us  [project(): pl.pallas_call(project_kernel, out_shape=jax.ShapeDtypeStruct((rows, 2 *...]
where the time goes in v6:
time: 29.8 us; the launch traced here: 29.6 us
  Pallas kernels  13.5 us (45%)
  starting transfers between devices  9.39 us (32%)
  waiting for transfers between devices  6.76 us (23%)
    ppermute x4, starting transfers between devices, summed_over_groups(): value = value + lax.ppermute(value, ('dp', 'mp'), pairs)  8.87 us
    pallas_call x1, Pallas kernels, project(): pl.pallas_call(project_kernel, out_shape=jax.ShapeDtypeStruct((rows, 2 *...  8.3 us
    ppermute x4, waiting for transfers between devices, summed_over_groups(): value = value + lax.ppermute(value, ('dp', 'mp'), pairs)  5.77 us
    pallas_call x1, Pallas kernels, whiten(): pl.pallas_call(functools.partial(whiten_kernel, factor, rows_each), out_s...  4.58 us
    ppermute x1, waiting for transfers between devices, shards(): parts.append(lax.ppermute(part, 'mp', pairs))  0.99 us
  transfers between devices with their start and end apart: 5, of which 5 were waited for; matrix products, arithmetic and copies ran while one was open for 0% of the time, Pallas kernels for 0%

profile of v6, /device:TPU:0, one launch (start us, length us, event | category | flops | bytes accessed | tf_op | source)
XLA Modules:
  0.0 29.6 jit_solution(13325323946476524648)
XLA Ops:
  0.0 8.3 %project.1.refs_1_ = f32[128,256]{1,0:T(8,128)S(1)} custom-call(bf16[128,14336]{1,0:T(8,128)(2,1)} %gate.1, bf16[128,14336]{1,0:T(8,128)(2,1)} %up.1, bf16[128,14336]{1,0:T(8,128)(2,1)} %grad.1, bf16[14336,128]{1,0:T(8,128)(2,1)} %proj_hidden.1, bf16[128,4096]{1,0:T(8,128)(2,1)} %tokens.1, bf16[128,4096]{1,0:T(8,128)(2,1)} %outer.1, bf16[4096,128]{1,0:T(8,128)(2,1)} %proj_model.1), custom_call_target="tpu_custom_call" | custom-call | tf_op jit(solution)/shard_map/project/pallas_call | solution.py:120
  8.3 0.5 %collective-permute-start = (f32[128,256]{1,0:T(8,128)S(1)}, f32[128,256]{1,0:T(8,128)S(1)}, u32[]{:S(2)}, u32[]{:S(2)}) collective-permute-start(f32[128,256]{1,0:T(8,128)S(1)} %project.1.refs_1_), channel_id=1, source_target_pairs={{0,1},{1,0},{2,3},{3,2},{4,5},{5,4},{6,7},{7,6},{8,9},{9,8},{10,11... | collective-permute-start | bytes 393224 | tf_op jit(solution)/shard_map/ppermute | solution.py:308
  8.8 1.0 %collective-permute-done.refs_2_ = f32[128,256]{1,0:T(8,128)S(1)} collective-permute-done((f32[128,256]{1,0:T(8,128)S(1)}, f32[128,256]{1,0:T(8,128)S(1)}, u32[]{:S(2)}, u32[]{:S(2)}) %collective-permute-start) | collective-permute-done | bytes 131104 | tf_op jit(solution)/shard_map/ppermute | solution.py:308
  9.8 0.6 %gram.1 = (f32[1,64,128]{2,1,0:T(8,128)S(1)}, f32[32,128]{1,0:T(8,128)S(1)}) custom-call(s32[1]{0:T(128)} %bitcast.refs_0_, f32[128,256]{1,0:T(8,128)S(1)} %project.1.refs_1_, f32[128,256]{1,0:T(8,128)S(1)} %collective-permute-done.refs_2_), custom_call_target="tpu_custom_call" | custom-call | tf_op jit(solution)/shard_map/gram/pallas_call | solution.py:178
  10.4 2.6 %collective-permute-start.1 = (f32[32,128]{1,0:T(8,128)S(1)}, f32[32,128]{1,0:T(8,128)S(1)}, u32[]{:S(2)}, u32[]{:S(2)}) collective-permute-start(f32[32,128]{1,0:T(8,128)S(1)} %get-tuple-element.8), channel_id=1, source_target_pairs={{0,3},{1,2},{2,1},{3,0},{4,7},{5,6},{6,5},{7,4},{8,11},{9,10},{10,... | collective-permute-start | bytes 49160 | tf_op jit(solution)/shard_map/ppermute | solution.py:293
  13.0 1.4 %collective-permute-done.1 = f32[32,128]{1,0:T(8,128)S(1)} collective-permute-done((f32[32,128]{1,0:T(8,128)S(1)}, f32[32,128]{1,0:T(8,128)S(1)}, u32[]{:S(2)}, u32[]{:S(2)}) %collective-permute-start.1) | collective-permute-done | bytes 16416 | tf_op jit(solution)/shard_map/ppermute | solution.py:293
  14.5 1.7 %collective-permute-start.2 = (f32[32,128]{1,0:T(8,128)S(1)}, f32[32,128]{1,0:T(8,128)S(1)}, u32[]{:S(2)}, u32[]{:S(2)}) collective-permute-start(f32[32,128]{1,0:T(8,128)S(1)} %add.12), channel_id=1, source_target_pairs={{0,5},{1,4},{2,7},{3,6},{4,1},{5,0},{6,3},{7,2},{8,13},{9,12},{10,... | collective-permute-start | bytes 49160 | tf_op jit(solution)/shard_map/ppermute | solution.py:293
  16.2 1.4 %collective-permute-done.2 = f32[32,128]{1,0:T(8,128)S(1)} collective-permute-done((f32[32,128]{1,0:T(8,128)S(1)}, f32[32,128]{1,0:T(8,128)S(1)}, u32[]{:S(2)}, u32[]{:S(2)}) %collective-permute-start.2) | collective-permute-done | bytes 16416 | tf_op jit(solution)/shard_map/ppermute | solution.py:293
  17.7 1.8 %collective-permute-start.3 = (f32[32,128]{1,0:T(8,128)S(1)}, f32[32,128]{1,0:T(8,128)S(1)}, u32[]{:S(2)}, u32[]{:S(2)}) collective-permute-start(f32[32,128]{1,0:T(8,128)S(1)} %add.13), channel_id=1, source_target_pairs={{0,9},{1,8},{2,11},{3,10},{4,13},{5,12},{6,15},{7,14},{8,1},{9,0},... | collective-permute-start | bytes 49160 | tf_op jit(solution)/shard_map/ppermute | solution.py:293
  19.4 1.4 %collective-permute-done.3 = f32[32,128]{1,0:T(8,128)S(1)} collective-permute-done((f32[32,128]{1,0:T(8,128)S(1)}, f32[32,128]{1,0:T(8,128)S(1)}, u32[]{:S(2)}, u32[]{:S(2)}) %collective-permute-start.3) | collective-permute-done | bytes 16416 | tf_op jit(solution)/shard_map/ppermute | solution.py:293
  20.9 2.7 %collective-permute-start.4 = (f32[32,128]{1,0:T(8,128)S(1)}, f32[32,128]{1,0:T(8,128)S(1)}, u32[]{:S(2)}, u32[]{:S(2)}) collective-permute-start(f32[32,128]{1,0:T(8,128)S(1)} %add.14), channel_id=1, source_target_pairs={{0,17},{1,16},{2,19},{3,18},{4,21},{5,20},{6,23},{7,22},{8,25},{9,... | collective-permute-start | bytes 49160 | tf_op jit(solution)/shard_map/ppermute | solution.py:293
  23.6 1.4 %collective-permute-done.4 = f32[32,128]{1,0:T(8,128)S(1)} collective-permute-done((f32[32,128]{1,0:T(8,128)S(1)}, f32[32,128]{1,0:T(8,128)S(1)}, u32[]{:S(2)}, u32[]{:S(2)}) %collective-permute-start.4) | collective-permute-done | bytes 16416 | tf_op jit(solution)/shard_map/ppermute | solution.py:293
  25.1 4.6 %whiten.1 = f32[1,64,64]{2,1,0:T(8,128)} custom-call(f32[1,64,128]{2,1,0:T(8,128)S(1)} %get-tuple-element.7.rows_ref, f32[32,128]{1,0:T(8,128)S(1)} %add.15.gram_ref), custom_call_target="tpu_custom_call" | custom-call | tf_op jit(solution)/shard_map/whiten/pallas_call | solution.py:274
  (4 shorter events, 0.0 us)
Async XLA Ops:
  8.3 1.5 %collective-permute-start = (f32[128,256]{1,0:T(8,128)S(1)}, f32[128,256]{1,0:T(8,128)S(1)}, u32[]{:S(2)}, u32[]{:S(2)}) collective-permute-start(f32[128,256]{1,0:T(8,128)S(1)} %project.1.refs_1_), channel_id=1, source_target_pairs={{0,1},{1,0},{2,3},{3,2},{4,5},{5,4},{6,7},{7,6},{8,9},{9,8},{10,11... | collective-permute-start | bytes 393224 | tf_op jit(solution)/shard_map/ppermute | solution.py:308
  10.4 4.1 %collective-permute-start.1 = (f32[32,128]{1,0:T(8,128)S(1)}, f32[32,128]{1,0:T(8,128)S(1)}, u32[]{:S(2)}, u32[]{:S(2)}) collective-permute-start(f32[32,128]{1,0:T(8,128)S(1)} %get-tuple-element.8), channel_id=1, source_target_pairs={{0,3},{1,2},{2,1},{3,0},{4,7},{5,6},{6,5},{7,4},{8,11},{9,10},{10,... | collective-permute-start | bytes 49160 | tf_op jit(solution)/shard_map/ppermute | solution.py:293
  14.5 3.2 %collective-permute-start.2 = (f32[32,128]{1,0:T(8,128)S(1)}, f32[32,128]{1,0:T(8,128)S(1)}, u32[]{:S(2)}, u32[]{:S(2)}) collective-permute-start(f32[32,128]{1,0:T(8,128)S(1)} %add.12), channel_id=1, source_target_pairs={{0,5},{1,4},{2,7},{3,6},{4,1},{5,0},{6,3},{7,2},{8,13},{9,12},{10,... | collective-permute-start | bytes 49160 | tf_op jit(solution)/shard_map/ppermute | solution.py:293
  17.7 3.2 %collective-permute-start.3 = (f32[32,128]{1,0:T(8,128)S(1)}, f32[32,128]{1,0:T(8,128)S(1)}, u32[]{:S(2)}, u32[]{:S(2)}) collective-permute-start(f32[32,128]{1,0:T(8,128)S(1)} %add.13), channel_id=1, source_target_pairs={{0,9},{1,8},{2,11},{3,10},{4,13},{5,12},{6,15},{7,14},{8,1},{9,0},... | collective-permute-start | bytes 49160 | tf_op jit(solution)/shard_map/ppermute | solution.py:293
  20.9 4.2 %collective-permute-start.4 = (f32[32,128]{1,0:T(8,128)S(1)}, f32[32,128]{1,0:T(8,128)S(1)}, u32[]{:S(2)}, u32[]{:S(2)}) collective-permute-start(f32[32,128]{1,0:T(8,128)S(1)} %add.14), channel_id=1, source_target_pairs={{0,17},{1,16},{2,19},{3,18},{4,21},{5,20},{6,23},{7,22},{8,25},{9,... | collective-permute-start | bytes 49160 | tf_op jit(solution)/shard_map/ppermute | solution.py:293

commit v7 on v6

--- a/solution.py
+++ b/solution.py
@@ -86,7 +86,7 @@
                 start(model_copies(other))
 
         base = piece * hidden_each
-        total = None
+        totals = []
         for first in range(0, hidden_each, STEP):
             step = min(STEP, hidden_each - first)
             cut = pl.ds(pl.multiple_of(base + first, 128), step)
@@ -94,17 +94,24 @@
             act = half + half * jnp.tanh(half)
             up_grad = (grad_v[:, cut].astype(jnp.float32) * act).astype(jnp.bfloat16)
             hidden = (act * up_v[:, cut].astype(jnp.float32)).astype(jnp.bfloat16)
-            both = jnp.concatenate([up_grad, hidden], axis=0)
-            part = jnp.dot(both, hidden_w[cut, :], preferred_element_type=jnp.float32)
-            total = part if total is None else total + part
-        hidden_sum[...] += total
+            weights = hidden_w[cut, :]
+            parts = [
+                jnp.dot(side, weights, preferred_element_type=jnp.float32)
+                for side in (up_grad, hidden)
+            ]
+            totals = [old + new for old, new in zip(totals, parts)] if totals else parts
+        for which, total in enumerate(totals):
+            hidden_sum[which * rows : (which + 1) * rows, :] += total
 
     @pl.loop(0, model_count)
     def _(piece):
         arrive(model_copies(piece))
         cut = pl.ds(pl.multiple_of(piece * model_each, model_each), model_each)
-        both = jnp.concatenate([tokens_v[:, cut], outer_v[:, cut]], axis=0)
-        model_sum[...] += jnp.dot(both, model_w[cut, :], preferred_element_type=jnp.float32)
+        weights = model_w[cut, :]
+        for which, side in enumerate((tokens_v, outer_v)):
+            model_sum[which * rows : (which + 1) * rows, :] += jnp.dot(
+                side[:, cut], weights, preferred_element_type=jnp.float32
+            )
 
     low = lanes_of((rows, WIDE)) < RANK
     upward = pltpu.roll(hidden_sum[:rows, :], RANK, 1)
@@ -188,7 +195,7 @@
     )(place, *parts)
 
 
-def eliminated(state):
+def eliminated(state, spread):
     height = 8
     blocks = len(state)
     state = list(state)
@@ -197,18 +204,21 @@
     def across(block, at):
         return jnp.broadcast_to(block[:, at : at + 1], block.shape)
 
-    def down(block, at):
-        return jnp.broadcast_to(block[at : at + 1, :], block.shape)
+    def down(which, at):
+        return spread[which, pl.ds(at, height, stride=0), :]
 
     done = []
     for held in range(blocks):
         base = RANK + held * height
         own = state[held]
-        columns = [across(own, base + k) for k in range(height)]
+        first_slot = (held % 2) * (height + 1)
+        for k in range(height):
+            spread[first_slot + k] = across(own, base + k)
+        spread[first_slot + height] = own
         corner = {
-            (k, m): down(columns[m], k) for k in range(height) for m in range(k, height)
+            (k, m): down(first_slot + m, k) for k in range(height) for m in range(k, height)
         }
-        rows = [down(own, k) for k in range(height)]
+        rows = [down(first_slot + height, k) for k in range(height)]
         ahead = None
         if held + 1 < blocks:
             ahead = [across(state[held + 1], base + k) for k in range(height)]
@@ -243,9 +253,21 @@
             for m in reversed(range(2, height)):
                 for k in range(m - m % 2):
                     back[k] = back[k] - factors[k, m] * back[m]
+            packed = back[0]
+            for k in range(1, height):
+                packed = jnp.where(sub == k, back[k], packed)
+            weights = [jnp.zeros_like(own)] * (2 * blocks)
+            weights[blocks + held] = packed
+            later = jnp.concatenate(state[held + 2 :], axis=0)
+            later = later - jnp.dot(
+                later,
+                jnp.concatenate(weights, axis=0),
+                precision=highest,
+                preferred_element_type=jnp.float32,
+            )
             for other in range(held + 2, blocks):
-                for k in range(height):
-                    state[other] = state[other] - across(state[other], base + k) * back[k]
+                at = (other - held - 2) * height
+                state[other] = later[at : at + height]
         block = jnp.zeros_like(own)
         for k in range(0, height, 2):
             first, cross, second = corner[k, k], corner[k, k + 1], corner[k + 1, k + 1]
@@ -259,13 +281,13 @@
     return done
 
 
-def whiten_kernel(factor, rows_each, rows_ref, gram_ref, out_ref):
+def whiten_kernel(factor, rows_each, rows_ref, gram_ref, out_ref, spread):
     packed = gram_ref[...]
     gram = jnp.concatenate([pltpu.roll(packed, RANK, 1), packed], axis=0)
     low = lanes_of((RANK, WIDE)) < RANK
     for example in range(rows_ref.shape[0]):
         joined = jnp.where(low, rows_ref[example], gram)
-        done = eliminated([joined[at : at + 8] for at in range(0, RANK, 8)])
+        done = eliminated([joined[at : at + 8] for at in range(0, RANK, 8)], spread)
         solved = (jnp.concatenate(done, axis=0) * factor).T
         out_ref[example] = solved[:rows_each, :]
 
@@ -276,6 +298,7 @@
         out_shape=jax.ShapeDtypeStruct((rows.shape[0], rows_each, RANK), jnp.float32),
         in_specs=[whole_vmem] * 2,
         out_specs=whole_vmem,
+        scratch_shapes=[pltpu.VMEM((18, 8, WIDE), jnp.float32)],
         compiler_params=small,
         name="whiten",
     )(rows, gram)

time: 29.8 us -> 27.3 us (0.916)
  Pallas kernels: 13.5 us -> 10.9 us
    pallas_call x1, Pallas kernels: 4.58 us -> 2.33 us  [whiten(): pl.pallas_call(functools.partial(whiten_kernel, factor, rows_each), out_s...]
where the time goes in v7:
time: 27.3 us; the launch traced here: 27.1 us
  Pallas kernels  10.9 us (40%)
  starting transfers between devices  9.4 us (34%)
  waiting for transfers between devices  6.76 us (25%)
    ppermute x4, starting transfers between devices, summed_over_groups(): value = value + lax.ppermute(value, ('dp', 'mp'), pairs)  8.88 us
    pallas_call x1, Pallas kernels, project(): pl.pallas_call(project_kernel, out_shape=jax.ShapeDtypeStruct((rows, 2 *...  8.03 us
    ppermute x4, waiting for transfers between devices, summed_over_groups(): value = value + lax.ppermute(value, ('dp', 'mp'), pairs)  5.77 us
    pallas_call x1, Pallas kernels, whiten(): pl.pallas_call(functools.partial(whiten_kernel, factor, rows_each), out_s...  2.33 us
    ppermute x1, waiting for transfers between devices, shards(): parts.append(lax.ppermute(part, 'mp', pairs))  0.99 us
    pallas_call x1, Pallas kernels, gram_of(): pl.pallas_call(functools.partial(gram_kernel, rows_each, len(parts)), out...  0.58 us
  transfers between devices with their start and end apart: 5, of which 5 were waited for; matrix products, arithmetic and copies ran while one was open for 0% of the time, Pallas kernels for 0%

profile of v7, /device:TPU:0, one launch (start us, length us, event | category | flops | bytes accessed | tf_op | source)
XLA Modules:
  0.0 27.1 jit_solution(12360670382003633876)
XLA Ops:
  0.0 8.0 %project.1.refs_1_ = f32[128,256]{1,0:T(8,128)S(1)} custom-call(bf16[128,14336]{1,0:T(8,128)(2,1)} %gate.1, bf16[128,14336]{1,0:T(8,128)(2,1)} %up.1, bf16[128,14336]{1,0:T(8,128)(2,1)} %grad.1, bf16[14336,128]{1,0:T(8,128)(2,1)} %proj_hidden.1, bf16[128,4096]{1,0:T(8,128)(2,1)} %tokens.1, bf16[128,4096]{1,0:T(8,128)(2,1)} %outer.1, bf16[4096,128]{1,0:T(8,128)(2,1)} %proj_model.1), custom_call_target="tpu_custom_call" | custom-call | tf_op jit(solution)/shard_map/project/pallas_call | solution.py:127
  8.0 0.5 %collective-permute-start = (f32[128,256]{1,0:T(8,128)S(1)}, f32[128,256]{1,0:T(8,128)S(1)}, u32[]{:S(2)}, u32[]{:S(2)}) collective-permute-start(f32[128,256]{1,0:T(8,128)S(1)} %project.1.refs_1_), channel_id=1, source_target_pairs={{0,1},{1,0},{2,3},{3,2},{4,5},{5,4},{6,7},{7,6},{8,9},{9,8},{10,11... | collective-permute-start | bytes 393224 | tf_op jit(solution)/shard_map/ppermute | solution.py:331
  8.6 1.0 %collective-permute-done.refs_2_ = f32[128,256]{1,0:T(8,128)S(1)} collective-permute-done((f32[128,256]{1,0:T(8,128)S(1)}, f32[128,256]{1,0:T(8,128)S(1)}, u32[]{:S(2)}, u32[]{:S(2)}) %collective-permute-start) | collective-permute-done | bytes 131104 | tf_op jit(solution)/shard_map/ppermute | solution.py:331
  9.5 0.6 %gram.1 = (f32[1,64,128]{2,1,0:T(8,128)S(1)}, f32[32,128]{1,0:T(8,128)S(1)}) custom-call(s32[1]{0:T(128)} %bitcast.refs_0_, f32[128,256]{1,0:T(8,128)S(1)} %project.1.refs_1_, f32[128,256]{1,0:T(8,128)S(1)} %collective-permute-done.refs_2_), custom_call_target="tpu_custom_call" | custom-call | tf_op jit(solution)/shard_map/gram/pallas_call | solution.py:185
  10.1 2.6 %collective-permute-start.1 = (f32[32,128]{1,0:T(8,128)S(1)}, f32[32,128]{1,0:T(8,128)S(1)}, u32[]{:S(2)}, u32[]{:S(2)}) collective-permute-start(f32[32,128]{1,0:T(8,128)S(1)} %get-tuple-element.8), channel_id=1, source_target_pairs={{0,3},{1,2},{2,1},{3,0},{4,7},{5,6},{6,5},{7,4},{8,11},{9,10},{10,... | collective-permute-start | bytes 49160 | tf_op jit(solution)/shard_map/ppermute | solution.py:316
  12.7 1.4 %collective-permute-done.1 = f32[32,128]{1,0:T(8,128)S(1)} collective-permute-done((f32[32,128]{1,0:T(8,128)S(1)}, f32[32,128]{1,0:T(8,128)S(1)}, u32[]{:S(2)}, u32[]{:S(2)}) %collective-permute-start.1) | collective-permute-done | bytes 16416 | tf_op jit(solution)/shard_map/ppermute | solution.py:316
  14.2 1.8 %collective-permute-start.2 = (f32[32,128]{1,0:T(8,128)S(1)}, f32[32,128]{1,0:T(8,128)S(1)}, u32[]{:S(2)}, u32[]{:S(2)}) collective-permute-start(f32[32,128]{1,0:T(8,128)S(1)} %add.12), channel_id=1, source_target_pairs={{0,5},{1,4},{2,7},{3,6},{4,1},{5,0},{6,3},{7,2},{8,13},{9,12},{10,... | collective-permute-start | bytes 49160 | tf_op jit(solution)/shard_map/ppermute | solution.py:316
  15.9 1.4 %collective-permute-done.2 = f32[32,128]{1,0:T(8,128)S(1)} collective-permute-done((f32[32,128]{1,0:T(8,128)S(1)}, f32[32,128]{1,0:T(8,128)S(1)}, u32[]{:S(2)}, u32[]{:S(2)}) %collective-permute-start.2) | collective-permute-done | bytes 16416 | tf_op jit(solution)/shard_map/ppermute | solution.py:316
  17.4 1.8 %collective-permute-start.3 = (f32[32,128]{1,0:T(8,128)S(1)}, f32[32,128]{1,0:T(8,128)S(1)}, u32[]{:S(2)}, u32[]{:S(2)}) collective-permute-start(f32[32,128]{1,0:T(8,128)S(1)} %add.13), channel_id=1, source_target_pairs={{0,9},{1,8},{2,11},{3,10},{4,13},{5,12},{6,15},{7,14},{8,1},{9,0},... | collective-permute-start | bytes 49160 | tf_op jit(solution)/shard_map/ppermute | solution.py:316
  19.2 1.4 %collective-permute-done.3 = f32[32,128]{1,0:T(8,128)S(1)} collective-permute-done((f32[32,128]{1,0:T(8,128)S(1)}, f32[32,128]{1,0:T(8,128)S(1)}, u32[]{:S(2)}, u32[]{:S(2)}) %collective-permute-start.3) | collective-permute-done | bytes 16416 | tf_op jit(solution)/shard_map/ppermute | solution.py:316
  20.6 2.7 %collective-permute-start.4 = (f32[32,128]{1,0:T(8,128)S(1)}, f32[32,128]{1,0:T(8,128)S(1)}, u32[]{:S(2)}, u32[]{:S(2)}) collective-permute-start(f32[32,128]{1,0:T(8,128)S(1)} %add.14), channel_id=1, source_target_pairs={{0,17},{1,16},{2,19},{3,18},{4,21},{5,20},{6,23},{7,22},{8,25},{9,... | collective-permute-start | bytes 49160 | tf_op jit(solution)/shard_map/ppermute | solution.py:316
  23.4 1.4 %collective-permute-done.4 = f32[32,128]{1,0:T(8,128)S(1)} collective-permute-done((f32[32,128]{1,0:T(8,128)S(1)}, f32[32,128]{1,0:T(8,128)S(1)}, u32[]{:S(2)}, u32[]{:S(2)}) %collective-permute-start.4) | collective-permute-done | bytes 16416 | tf_op jit(solution)/shard_map/ppermute | solution.py:316
  24.8 2.3 %whiten.1 = f32[1,64,64]{2,1,0:T(8,128)} custom-call(f32[1,64,128]{2,1,0:T(8,128)S(1)} %get-tuple-element.7.rows_ref, f32[32,128]{1,0:T(8,128)S(1)} %add.15.gram_ref), custom_call_target="tpu_custom_call" | custom-call | tf_op jit(solution)/shard_map/whiten/pallas_call | solution.py:296
  (4 shorter events, 0.0 us)
Async XLA Ops:
  8.0 1.5 %collective-permute-start = (f32[128,256]{1,0:T(8,128)S(1)}, f32[128,256]{1,0:T(8,128)S(1)}, u32[]{:S(2)}, u32[]{:S(2)}) collective-permute-start(f32[128,256]{1,0:T(8,128)S(1)} %project.1.refs_1_), channel_id=1, source_target_pairs={{0,1},{1,0},{2,3},{3,2},{4,5},{5,4},{6,7},{7,6},{8,9},{9,8},{10,11... | collective-permute-start | bytes 393224 | tf_op jit(solution)/shard_map/ppermute | solution.py:331
  10.1 4.1 %collective-permute-start.1 = (f32[32,128]{1,0:T(8,128)S(1)}, f32[32,128]{1,0:T(8,128)S(1)}, u32[]{:S(2)}, u32[]{:S(2)}) collective-permute-start(f32[32,128]{1,0:T(8,128)S(1)} %get-tuple-element.8), channel_id=1, source_target_pairs={{0,3},{1,2},{2,1},{3,0},{4,7},{5,6},{6,5},{7,4},{8,11},{9,10},{10,... | collective-permute-start | bytes 49160 | tf_op jit(solution)/shard_map/ppermute | solution.py:316
  14.2 3.2 %collective-permute-start.2 = (f32[32,128]{1,0:T(8,128)S(1)}, f32[32,128]{1,0:T(8,128)S(1)}, u32[]{:S(2)}, u32[]{:S(2)}) collective-permute-start(f32[32,128]{1,0:T(8,128)S(1)} %add.12), channel_id=1, source_target_pairs={{0,5},{1,4},{2,7},{3,6},{4,1},{5,0},{6,3},{7,2},{8,13},{9,12},{10,... | collective-permute-start | bytes 49160 | tf_op jit(solution)/shard_map/ppermute | solution.py:316
  17.4 3.2 %collective-permute-start.3 = (f32[32,128]{1,0:T(8,128)S(1)}, f32[32,128]{1,0:T(8,128)S(1)}, u32[]{:S(2)}, u32[]{:S(2)}) collective-permute-start(f32[32,128]{1,0:T(8,128)S(1)} %add.13), channel_id=1, source_target_pairs={{0,9},{1,8},{2,11},{3,10},{4,13},{5,12},{6,15},{7,14},{8,1},{9,0},... | collective-permute-start | bytes 49160 | tf_op jit(solution)/shard_map/ppermute | solution.py:316
  20.6 4.2 %collective-permute-start.4 = (f32[32,128]{1,0:T(8,128)S(1)}, f32[32,128]{1,0:T(8,128)S(1)}, u32[]{:S(2)}, u32[]{:S(2)}) collective-permute-start(f32[32,128]{1,0:T(8,128)S(1)} %add.14), channel_id=1, source_target_pairs={{0,17},{1,16},{2,19},{3,18},{4,21},{5,20},{6,23},{7,22},{8,25},{9,... | collective-permute-start | bytes 49160 | tf_op jit(solution)/shard_map/ppermute | solution.py:316

commit v8 on v7

--- a/solution.py
+++ b/solution.py
@@ -11,9 +11,9 @@
 RANK = 64
 LEN = 128
 WIDE = 2 * RANK
-EACH = 1024
-STEP = 256
-AHEAD = 4
+EACH = 2048
+STEP = 512
+AHEAD = 3
 
 highest = lax.Precision.HIGHEST
 whole_vmem = pl.BlockSpec(memory_space=pltpu.VMEM)
@@ -21,6 +21,13 @@
 small = pltpu.CompilerParams(vmem_limit_bytes=8 * 2**20)
 
 
+def cuts_of(width):
+    ends = [min(EACH // 2, width)]
+    while ends[-1] < width:
+        ends.append(min(ends[-1] + EACH, width))
+    return [(begin, end - begin) for begin, end in zip([0] + ends, ends)]
+
+
 def lanes_of(shape):
     return lax.broadcasted_iota(jnp.int32, shape, len(shape) - 1)
 
@@ -29,84 +36,73 @@
     gate_v, up_v, grad_v, hidden_w, tokens_v, outer_v, model_w = rest[:7]
     hidden_sum, model_sum, sems, model_sems = rest[7:]
     rows = gate.shape[0]
-    hidden_each, model_each = math.gcd(gate.shape[1], EACH), math.gcd(tokens.shape[1], EACH)
-    hidden_count = gate.shape[1] // hidden_each
-    model_count = tokens.shape[1] // model_each
-
-    def hidden_copies(piece):
-        cut = pl.ds(pl.multiple_of(piece * hidden_each, hidden_each), hidden_each)
+    hidden_cuts, model_cuts = cuts_of(gate.shape[1]), cuts_of(tokens.shape[1])
+
+    copies = []
+    for piece, (begin, size) in enumerate(hidden_cuts):
+        cut = pl.ds(begin, size)
         pairs = [
             (gate.at[:, cut], gate_v.at[:, cut]),
             (grad.at[:, cut], grad_v.at[:, cut]),
             (up.at[:, cut], up_v.at[:, cut]),
             (proj_hidden.at[cut, :], hidden_w.at[cut, :]),
         ]
-        return [
-            pltpu.make_async_copy(source, target, sems.at[piece, which])
-            for which, (source, target) in enumerate(pairs)
-        ]
-
-    def model_copies(piece):
-        cut = pl.ds(pl.multiple_of(piece * model_each, model_each), model_each)
+        copies.append(
+            [
+                pltpu.make_async_copy(source, target, sems.at[piece, which])
+                for which, (source, target) in enumerate(pairs)
+            ]
+        )
+    for piece, (begin, size) in enumerate(model_cuts):
+        cut = pl.ds(begin, size)
         pairs = [
             (tokens.at[:, cut], tokens_v.at[:, cut]),
             (outer.at[:, cut], outer_v.at[:, cut]),
             (proj_model.at[cut, :], model_w.at[cut, :]),
         ]
-        return [
-            pltpu.make_async_copy(source, target, model_sems.at[piece, which])
-            for which, (source, target) in enumerate(pairs)
-        ]
-
-    def start(copies):
-        for copy in copies:
-            copy.start()
-
-    def arrive(copies):
-        for copy in copies:
+        copies.append(
+            [
+                pltpu.make_async_copy(source, target, model_sems.at[piece, which])
+                for which, (source, target) in enumerate(pairs)
+            ]
+        )
+
+    def start(which):
+        if which < len(copies):
+            for copy in copies[which]:
+                copy.start()
+
+    def arrive(which):
+        for copy in copies[which]:
             copy.wait()
 
-    ahead = min(AHEAD, hidden_count)
-    for piece in range(ahead):
-        start(hidden_copies(piece))
+    for which in range(AHEAD):
+        start(which)
     hidden_sum[...] = jnp.zeros_like(hidden_sum)
     model_sum[...] = jnp.zeros_like(model_sum)
 
-    @pl.loop(0, hidden_count)
-    def _(piece):
-        arrive(hidden_copies(piece))
-
-        @pl.when(piece + ahead < hidden_count)
-        def _():
-            start(hidden_copies(piece + ahead))
-
-        @pl.when(piece + ahead == hidden_count)
-        def _():
-            for other in range(model_count):
-                start(model_copies(other))
-
-        base = piece * hidden_each
-        totals = []
-        for first in range(0, hidden_each, STEP):
-            step = min(STEP, hidden_each - first)
-            cut = pl.ds(pl.multiple_of(base + first, 128), step)
-            half = gate_v[:, cut].astype(jnp.float32) * 0.5
+    for piece, (begin, size) in enumerate(hidden_cuts):
+        arrive(piece)
+        start(piece + AHEAD)
+        step = math.gcd(STEP, size)
+
+        @pl.loop(0, size // step)
+        def _(part, begin=begin, step=step):
+            cut = pl.ds(pl.multiple_of(begin + part * step, 128), step)
+            half = (gate_v[:, cut] * 0.5).astype(jnp.float32)
             act = half + half * jnp.tanh(half)
             up_grad = (grad_v[:, cut].astype(jnp.float32) * act).astype(jnp.bfloat16)
             hidden = (act * up_v[:, cut].astype(jnp.float32)).astype(jnp.bfloat16)
             weights = hidden_w[cut, :]
-            parts = [
-                jnp.dot(side, weights, preferred_element_type=jnp.float32)
-                for side in (up_grad, hidden)
-            ]
-            totals = [old + new for old, new in zip(totals, parts)] if totals else parts
-        for which, total in enumerate(totals):
-            hidden_sum[which * rows : (which + 1) * rows, :] += total
-
-    @pl.loop(0, model_count)
-    def _(piece):
-        arrive(model_copies(piece))
-        cut = pl.ds(pl.multiple_of(piece * model_each, model_each), model_each)
+            for which, side in enumerate((up_grad, hidden)):
+                hidden_sum[which * rows : (which + 1) * rows, :] += jnp.dot(
+                    side, weights, preferred_element_type=jnp.float32
+                )
+
+    for piece, (begin, size) in enumerate(model_cuts):
+        arrive(len(hidden_cuts) + piece)
+        start(len(hidden_cuts) + piece + AHEAD)
+        cut = slice(begin, begin + size)
         weights = model_w[cut, :]
         for which, side in enumerate((tokens_v, outer_v)):
             model_sum[which * rows : (which + 1) * rows, :] += jnp.dot(
@@ -139,8 +135,8 @@
             pltpu.VMEM((model_width, WIDE), held),
             pltpu.VMEM((2 * rows, WIDE), jnp.float32),
             pltpu.VMEM((2 * rows, WIDE), jnp.float32),
-            pltpu.SemaphoreType.DMA((hidden_width // math.gcd(hidden_width, EACH), 4)),
-            pltpu.SemaphoreType.DMA((model_width // math.gcd(model_width, EACH), 3)),
+            pltpu.SemaphoreType.DMA((len(cuts_of(hidden_width)), 4)),
+            pltpu.SemaphoreType.DMA((len(cuts_of(model_width)), 3)),
         ],
         compiler_params=pltpu.CompilerParams(vmem_limit_bytes=56 * 10**6),
         name="project",
@@ -175,9 +171,14 @@
             preferred_element_type=jnp.float32,
         )
     top, bottom = gram[: RANK // 2], gram[RANK // 2 :]
-    gram_ref[...] = jnp.where(
-        lanes_of(top.shape) < RANK, pltpu.roll(top, RANK, 1), bottom
-    )
+    packed = jnp.where(lanes_of(top.shape) < RANK, pltpu.roll(top, RANK, 1), bottom)
+    height = packed.shape[0] // count
+    mine = packed[:height]
+    for shard in range(1, count):
+        block = packed[shard * height : (shard + 1) * height]
+        mine = jnp.where(place[0] == shard, block, mine)
+    for group in range(gram_ref.shape[0]):
+        gram_ref[group] = mine
 
 
 def gram_of(place, parts, rows_each):
@@ -186,7 +187,9 @@
         functools.partial(gram_kernel, rows_each, len(parts)),
         out_shape=[
             jax.ShapeDtypeStruct((examples, RANK, WIDE), jnp.float32),
-            jax.ShapeDtypeStruct((RANK // 2, WIDE), jnp.float32),
+            jax.ShapeDtypeStruct(
+                (lax.axis_size("dp"), RANK // 2 // len(parts), WIDE), jnp.float32
+            ),
         ],
         in_specs=[pl.BlockSpec(memory_space=pltpu.SMEM)] + [whole_vmem] * len(parts),
         out_specs=[whole_vmem] * 2,
@@ -281,8 +284,16 @@
     return done
 
 
-def whiten_kernel(factor, rows_each, rows_ref, gram_ref, out_ref, spread):
-    packed = gram_ref[...]
+def whiten_kernel(factor, rows_each, place, rows_ref, *refs):
+    halves, (out_ref, spread) = refs[:-2], refs[-2:]
+    count = len(halves)
+    ordered = []
+    for shard in range(count):
+        block = halves[0][...]
+        for away in range(1, count):
+            block = jnp.where(place[0] == (shard + away) % count, halves[away][...], block)
+        ordered.append(block)
+    packed = jnp.concatenate(ordered, axis=0)
     gram = jnp.concatenate([pltpu.roll(packed, RANK, 1), packed], axis=0)
     low = lanes_of((RANK, WIDE)) < RANK
     for example in range(rows_ref.shape[0]):
@@ -292,47 +303,43 @@
         out_ref[example] = solved[:rows_each, :]
 
 
-def whiten(rows, gram, rows_each, factor):
+def whiten(place, rows, gram, rows_each, factor):
     return pl.pallas_call(
         functools.partial(whiten_kernel, factor, rows_each),
         out_shape=jax.ShapeDtypeStruct((rows.shape[0], rows_each, RANK), jnp.float32),
-        in_specs=[whole_vmem] * 2,
+        in_specs=[pl.BlockSpec(memory_space=pltpu.SMEM)] + [whole_vmem] * (1 + len(gram)),
         out_specs=whole_vmem,
         scratch_shapes=[pltpu.VMEM((18, 8, WIDE), jnp.float32)],
         compiler_params=small,
         name="whiten",
-    )(rows, gram)
-
-
-def summed_over_groups(value):
-    groups, model_shards = lax.axis_size("dp"), lax.axis_size("mp")
-    other = 1 if model_shards % 2 == 0 else 0
-    for level in range(groups.bit_length() - 1):
-        pairs = [
-            (group * model_shards + shard, (group ^ 2**level) * model_shards + (shard ^ other))
-            for group in range(groups)
-            for shard in range(model_shards)
-        ]
-        value = value + lax.ppermute(value, ("dp", "mp"), pairs)
-    return value
+    )(place, rows, *gram)
+
+
+def summed_over_groups(copies):
+    received = lax.all_to_all(copies, "dp", 0, 0, tiled=True)
+    total = jnp.sum(received, axis=0)
+    return [total] + from_shards(total)
+
+
+def from_shards(value):
+    shards = lax.axis_size("mp")
+    return [
+        lax.ppermute(value, "mp", [(source, (source + away) % shards) for source in range(shards)])
+        for away in range(1, shards)
+    ]
 
 
 def shards(tokens_in, gate_pre, up_pre, hidden_grad, out_grad, proj_model, proj_hidden):
-    model_shards = lax.axis_size("mp")
-    rows_each = WIDE // model_shards
+    rows_each = WIDE // lax.axis_size("mp")
     local_examples = tokens_in.shape[0] // LEN
     place = lax.axis_index("mp").astype(jnp.int32).reshape(1)
     part = project(
         gate_pre, up_pre, hidden_grad, proj_hidden, tokens_in, out_grad, proj_model
     )
-    parts = [part]
-    for away in range(1, model_shards):
-        pairs = [(source, (source + away) % model_shards) for source in range(model_shards)]
-        parts.append(lax.ppermute(part, "mp", pairs))
-    rows, gram = gram_of(place, parts, rows_each)
-    gram = summed_over_groups(gram)
+    rows, copies = gram_of(place, [part] + from_shards(part), rows_each)
+    gram = summed_over_groups(copies)
     factor = math.sqrt(local_examples * lax.axis_size("dp") * 2 * RANK)
-    return whiten(rows, gram, rows_each, factor)
+    return whiten(place, rows, gram, rows_each, factor)
 
 
 def solution(mesh):

time: 27.3 us -> 31.3 us (1.15)
  blocking collectives: 0 us -> 15.8 us
  starting transfers between devices: 9.4 us -> 0.59 us
  waiting for transfers between devices: 6.76 us -> 2.15 us
  Pallas kernels: 10.9 us -> 12.5 us
    all_to_all x0 -> x1, blocking collectives: none -> 15.8 us  [summed_over_groups(): received = lax.all_to_all(copies, 'dp', 0, 0, tiled=True)]
    ppermute x5 -> x2, starting transfers between devices: 9.4 us -> 0.59 us  [from_shards(): lax.ppermute(value, 'mp', [(source, (source + away) % shards) for source...]
    ppermute x5 -> x2, waiting for transfers between devices: 6.76 us -> 2.15 us  [from_shards(): lax.ppermute(value, 'mp', [(source, (source + away) % shards) for source...]
    pallas_call x1, Pallas kernels: 8.03 us -> 9.62 us  [project(): pl.pallas_call(project_kernel, out_shape=jax.ShapeDtypeStruct((rows, 2 *...]
  transfers between devices with their start and end apart: 5 -> 2, of which waited for: 5 -> 2; matrix products, arithmetic and copies ran while one was open for 0% -> 0% of each run, Pallas kernels for 0% -> 0%
where the time goes in v8:
time: 31.3 us; the launch traced here: 31.2 us
  blocking collectives  15.8 us (50%)
  Pallas kernels  12.5 us (40%)
  waiting for transfers between devices  2.15 us (7%)
  starting transfers between devices  0.59 us (2%)
    all_to_all x1, blocking collectives, summed_over_groups(): received = lax.all_to_all(copies, 'dp', 0, 0, tiled=True)  15.8 us
    pallas_call x1, Pallas kernels, project(): pl.pallas_call(project_kernel, out_shape=jax.ShapeDtypeStruct((rows, 2 *...  9.62 us
    pallas_call x1, Pallas kernels, whiten(): pl.pallas_call(functools.partial(whiten_kernel, factor, rows_each), out_s...  2.33 us
    ppermute x2, waiting for transfers between devices, from_shards(): lax.ppermute(value, 'mp', [(source, (source + away) % shards) for source...  2.15 us
  transfers between devices with their start and end apart: 2, of which 2 were waited for; matrix products, arithmetic and copies ran while one was open for 0% of the time, Pallas kernels for 0%

profile of v8, /device:TPU:0, one launch (start us, length us, event | category | flops | bytes accessed | tf_op | source)
XLA Modules:
  0.0 31.2 jit_solution(7752281278721405372)
XLA Ops:
  0.0 9.6 %project.1.refs_1_ = f32[128,256]{1,0:T(8,128)S(1)} custom-call(bf16[128,14336]{1,0:T(8,128)(2,1)} %gate.1, bf16[128,14336]{1,0:T(8,128)(2,1)} %up.1, bf16[128,14336]{1,0:T(8,128)(2,1)} %grad.1, bf16[14336,128]{1,0:T(8,128)(2,1)} %proj_hidden.1, bf16[128,4096]{1,0:T(8,128)(2,1)} %tokens.1, bf16[128,4096]{1,0:T(8,128)(2,1)} %outer.1, bf16[4096,128]{1,0:T(8,128)(2,1)} %proj_model.1), custom_call_target="tpu_custom_call" | custom-call | tf_op jit(solution)/shard_map/project/pallas_call | solution.py:123
  9.6 0.5 %collective-permute-start = (f32[128,256]{1,0:T(8,128)S(1)}, f32[128,256]{1,0:T(8,128)S(1)}, u32[]{:S(2)}, u32[]{:S(2)}) collective-permute-start(f32[128,256]{1,0:T(8,128)S(1)} %project.1.refs_1_), channel_id=1, source_target_pairs={{0,1},{1,0},{2,3},{3,2},{4,5},{5,4},{6,7},{7,6},{8,9},{9,8},{10,11... | collective-permute-start | bytes 393224 | tf_op jit(solution)/shard_map/ppermute | solution.py:327
  10.1 1.0 %collective-permute-done.refs_2_ = f32[128,256]{1,0:T(8,128)S(1)} collective-permute-done((f32[128,256]{1,0:T(8,128)S(1)}, f32[128,256]{1,0:T(8,128)S(1)}, u32[]{:S(2)}, u32[]{:S(2)}) %collective-permute-start) | collective-permute-done | bytes 131104 | tf_op jit(solution)/shard_map/ppermute | solution.py:327
  11.1 0.6 %gram.1 = (f32[1,64,128]{2,1,0:T(8,128)S(1)}, f32[16,16,128]{2,1,0:T(8,128)S(1)}) custom-call(s32[1]{0:T(128)} %bitcast.refs_0_.place, f32[128,256]{1,0:T(8,128)S(1)} %project.1.refs_1_, f32[128,256]{1,0:T(8,128)S(1)} %collective-permute-done.refs_2_), custom_call_target="tpu_custom_call" | custom-call | tf_op jit(solution)/shard_map/gram/pallas_call | solution.py:186
  11.7 15.8 %all_to_all.5 = f32[16,16,128]{2,1,0:T(8,128)S(1)} all-to-all(f32[16,16,128]{2,1,0:T(8,128)S(1)} %get-tuple-element.8), channel_id=1, replica_groups=mesh['dp'=16,'mp'=2] {'dp'}, dimensions={0} | all-to-all | bytes 262144 | tf_op jit(solution)/shard_map/all_to_all | solution.py:319
  27.6 0.1 collective-permute-start.1
  27.7 1.2 %collective-permute-done.1.refs_1_ = f32[16,128]{1,0:T(8,128)S(1)} collective-permute-done((f32[16,128]{1,0:T(8,128)S(1)}, f32[16,128]{1,0:T(8,128)S(1)}, u32[]{:S(2)}, u32[]{:S(2)}) %collective-permute-start.1) | collective-permute-done | bytes 8224 | tf_op jit(solution)/shard_map/ppermute | solution.py:327
  28.8 2.3 %whiten.1 = f32[1,64,64]{2,1,0:T(8,128)} custom-call(s32[1]{0:T(128)} %bitcast.refs_0_.place, f32[1,64,128]{2,1,0:T(8,128)S(1)} %get-tuple-element.7.rows_ref, f32[16,128]{1,0:T(8,128)S(1)} %reduce_sum.9.refs_0_, f32[16,128]{1,0:T(8,128)S(1)} %collective-permute-done.1.refs_1_), custom_call_target="tpu_custom_call" | custom-call | tf_op jit(solution)/shard_map/whiten/pallas_call | solution.py:307
  (1 shorter events, 0.0 us)
Async XLA Ops:
  9.6 1.5 %collective-permute-start = (f32[128,256]{1,0:T(8,128)S(1)}, f32[128,256]{1,0:T(8,128)S(1)}, u32[]{:S(2)}, u32[]{:S(2)}) collective-permute-start(f32[128,256]{1,0:T(8,128)S(1)} %project.1.refs_1_), channel_id=1, source_target_pairs={{0,1},{1,0},{2,3},{3,2},{4,5},{5,4},{6,7},{7,6},{8,9},{9,8},{10,11... | collective-permute-start | bytes 393224 | tf_op jit(solution)/shard_map/ppermute | solution.py:327
  27.6 1.2 %collective-permute-start.1 = (f32[16,128]{1,0:T(8,128)S(1)}, f32[16,128]{1,0:T(8,128)S(1)}, u32[]{:S(2)}, u32[]{:S(2)}) collective-permute-start(f32[16,128]{1,0:T(8,128)S(1)} %reduce_sum.9.refs_0_), channel_id=1, source_target_pairs={{0,1},{1,0},{2,3},{3,2},{4,5},{5,4},{6,7},{7,6},{8,9},{9,8},{10,11... | collective-permute-start | bytes 24584 | tf_op jit(solution)/shard_map/ppermute | solution.py:327

commit v9 on v7

--- a/solution.py
+++ b/solution.py
@@ -23,6 +23,12 @@
 
 def lanes_of(shape):
     return lax.broadcasted_iota(jnp.int32, shape, len(shape) - 1)
+
+
+def across_columns(weights, sides):
+    return lax.dot_general(
+        weights, sides, (((0,), (1,)), ((), ())), preferred_element_type=jnp.float32
+    )
 
 
 def project_kernel(gate, up, grad, proj_hidden, tokens, outer, proj_model, out, *rest):
@@ -86,7 +92,7 @@
                 start(model_copies(other))
 
         base = piece * hidden_each
-        totals = []
+        total = None
         for first in range(0, hidden_each, STEP):
             step = min(STEP, hidden_each - first)
             cut = pl.ds(pl.multiple_of(base + first, 128), step)
@@ -94,30 +100,22 @@
             act = half + half * jnp.tanh(half)
             up_grad = (grad_v[:, cut].astype(jnp.float32) * act).astype(jnp.bfloat16)
             hidden = (act * up_v[:, cut].astype(jnp.float32)).astype(jnp.bfloat16)
-            weights = hidden_w[cut, :]
-            parts = [
-                jnp.dot(side, weights, preferred_element_type=jnp.float32)
-                for side in (up_grad, hidden)
-            ]
-            totals = [old + new for old, new in zip(totals, parts)] if totals else parts
-        for which, total in enumerate(totals):
-            hidden_sum[which * rows : (which + 1) * rows, :] += total
+            both = jnp.concatenate([up_grad, hidden], axis=0)
+            part = across_columns(hidden_w[cut, :], both)
+            total = part if total is None else total + part
+        hidden_sum[...] += total
 
     @pl.loop(0, model_count)
     def _(piece):
         arrive(model_copies(piece))
         cut = pl.ds(pl.multiple_of(piece * model_each, model_each), model_each)
-        weights = model_w[cut, :]
-        for which, side in enumerate((tokens_v, outer_v)):
-            model_sum[which * rows : (which + 1) * rows, :] += jnp.dot(
-                side[:, cut], weights, preferred_element_type=jnp.float32
-            )
-
-    low = lanes_of((rows, WIDE)) < RANK
-    upward = pltpu.roll(hidden_sum[:rows, :], RANK, 1)
-    hidden_side = pltpu.roll(hidden_sum[rows:, :], RANK, 1)
-    out[:, :WIDE] = jnp.where(low, model_sum[:rows, :], upward)
-    out[:, WIDE:] = jnp.where(low, hidden_side, model_sum[rows:, :])
+        both = jnp.concatenate([tokens_v[:, cut], outer_v[:, cut]], axis=0)
+        model_sum[...] += across_columns(model_w[cut, :], both)
+
+    out[:RANK, :] = model_sum[:RANK, :rows]
+    out[RANK:WIDE, :] = hidden_sum[:RANK, :rows]
+    out[WIDE : WIDE + RANK, :] = hidden_sum[RANK:, rows:]
+    out[WIDE + RANK :, :] = model_sum[RANK:, rows:]
 
 
 def project(gate_pre, up_pre, hidden_grad, proj_hidden, tokens_in, out_grad, proj_model):
@@ -126,7 +124,7 @@
     held = jnp.bfloat16
     return pl.pallas_call(
         project_kernel,
-        out_shape=jax.ShapeDtypeStruct((rows, 2 * WIDE), jnp.float32),
+        out_shape=jax.ShapeDtypeStruct((2 * WIDE, rows), jnp.float32),
         in_specs=[left_in_hbm] * 7,
         out_specs=whole_vmem,
         scratch_shapes=[
@@ -137,8 +135,8 @@
             pltpu.VMEM((rows, model_width), held),
             pltpu.VMEM((rows, model_width), held),
             pltpu.VMEM((model_width, WIDE), held),
-            pltpu.VMEM((2 * rows, WIDE), jnp.float32),
-            pltpu.VMEM((2 * rows, WIDE), jnp.float32),
+            pltpu.VMEM((WIDE, 2 * rows), jnp.float32),
+            pltpu.VMEM((WIDE, 2 * rows), jnp.float32),
             pltpu.SemaphoreType.DMA((hidden_width // math.gcd(hidden_width, EACH), 4)),
             pltpu.SemaphoreType.DMA((model_width // math.gcd(model_width, EACH), 3)),
         ],
@@ -157,12 +155,16 @@
     low = lanes_of((RANK, WIDE)) < RANK
     gram = jnp.zeros((RANK, WIDE), jnp.float32)
     shift = lax.rem(WIDE - place[0] * rows_each, WIDE)
-    for example in range(total.shape[0] // LEN):
+    for example in range(total.shape[1] // LEN):
         mixed = []
         for at in (0, WIDE):
-            sides = total[example * LEN : (example + 1) * LEN, at : at + WIDE]
-            crossed = jnp.dot(
-                sides.T, sides, precision=highest, preferred_element_type=jnp.float32
+            sides = total[at : at + WIDE, example * LEN : (example + 1) * LEN]
+            crossed = lax.dot_general(
+                sides,
+                sides,
+                (((1,), (1,)), ((), ())),
+                precision=highest,
+                preferred_element_type=jnp.float32,
             )
             mixed.append(jnp.where((row < RANK) != (lane < RANK), crossed, 0.0))
         up_block, down_block = mixed[0][RANK:], mixed[1][RANK:]
@@ -181,7 +183,7 @@
 
 
 def gram_of(place, parts, rows_each):
-    examples = parts[0].shape[0] // LEN
+    examples = parts[0].shape[1] // LEN
     return pl.pallas_call(
         functools.partial(gram_kernel, rows_each, len(parts)),
         out_shape=[

time: 27.3 us -> 28.3 us (1.037)
  Pallas kernels: 10.9 us -> 11.9 us
    pallas_call x1, Pallas kernels: 8.03 us -> 8.96 us  [project(): pl.pallas_call(project_kernel, out_shape=jax.ShapeDtypeStruct((2 * WIDE,...]
where the time goes in v9:
time: 28.3 us; the launch traced here: 28.1 us
  Pallas kernels  11.9 us (42%)
  starting transfers between devices  9.39 us (33%)
  waiting for transfers between devices  6.76 us (24%)
    pallas_call x1, Pallas kernels, project(): pl.pallas_call(project_kernel, out_shape=jax.ShapeDtypeStruct((2 * WIDE,...  8.96 us
    ppermute x4, starting transfers between devices, summed_over_groups(): value = value + lax.ppermute(value, ('dp', 'mp'), pairs)  8.87 us
    ppermute x4, waiting for transfers between devices, summed_over_groups(): value = value + lax.ppermute(value, ('dp', 'mp'), pairs)  5.77 us
    pallas_call x1, Pallas kernels, whiten(): pl.pallas_call(functools.partial(whiten_kernel, factor, rows_each), out_s...  2.33 us
    ppermute x1, waiting for transfers between devices, shards(): parts.append(lax.ppermute(part, 'mp', pairs))  0.99 us
    pallas_call x1, Pallas kernels, gram_of(): pl.pallas_call(functools.partial(gram_kernel, rows_each, len(parts)), out...  0.65 us
  transfers between devices with their start and end apart: 5, of which 5 were waited for; matrix products, arithmetic and copies ran while one was open for 0% of the time, Pallas kernels for 0%

profile of v9, /device:TPU:0, one launch (start us, length us, event | category | flops | bytes accessed | tf_op | source)
XLA Modules:
  0.0 28.1 jit_solution(231450392960859143)
XLA Ops:
  0.0 9.0 %project.1.refs_1_ = f32[256,128]{1,0:T(8,128)S(1)} custom-call(bf16[128,14336]{1,0:T(8,128)(2,1)} %gate.1, bf16[128,14336]{1,0:T(8,128)(2,1)} %up.1, bf16[128,14336]{1,0:T(8,128)(2,1)} %grad.1, bf16[14336,128]{1,0:T(8,128)(2,1)} %proj_hidden.1, bf16[128,4096]{1,0:T(8,128)(2,1)} %tokens.1, bf16[128,4096]{1,0:T(8,128)(2,1)} %outer.1, bf16[4096,128]{1,0:T(8,128)(2,1)} %proj_model.1), custom_call_target="tpu_custom_call" | custom-call | tf_op jit(solution)/shard_map/project/pallas_call | solution.py:125
  9.0 0.5 %collective-permute-start = (f32[256,128]{1,0:T(8,128)S(1)}, f32[256,128]{1,0:T(8,128)S(1)}, u32[]{:S(2)}, u32[]{:S(2)}) collective-permute-start(f32[256,128]{1,0:T(8,128)S(1)} %project.1.refs_1_), channel_id=1, source_target_pairs={{0,1},{1,0},{2,3},{3,2},{4,5},{5,4},{6,7},{7,6},{8,9},{9,8},{10,11... | collective-permute-start | bytes 393224 | tf_op jit(solution)/shard_map/ppermute | solution.py:333
  9.5 1.0 %collective-permute-done.refs_2_ = f32[256,128]{1,0:T(8,128)S(1)} collective-permute-done((f32[256,128]{1,0:T(8,128)S(1)}, f32[256,128]{1,0:T(8,128)S(1)}, u32[]{:S(2)}, u32[]{:S(2)}) %collective-permute-start) | collective-permute-done | bytes 131104 | tf_op jit(solution)/shard_map/ppermute | solution.py:333
  10.5 0.6 %gram.1 = (f32[1,64,128]{2,1,0:T(8,128)S(1)}, f32[32,128]{1,0:T(8,128)S(1)}) custom-call(s32[1]{0:T(128)} %bitcast.refs_0_, f32[256,128]{1,0:T(8,128)S(1)} %project.1.refs_1_, f32[256,128]{1,0:T(8,128)S(1)} %collective-permute-done.refs_2_), custom_call_target="tpu_custom_call" | custom-call | tf_op jit(solution)/shard_map/gram/pallas_call | solution.py:187
  11.1 2.6 %collective-permute-start.1 = (f32[32,128]{1,0:T(8,128)S(1)}, f32[32,128]{1,0:T(8,128)S(1)}, u32[]{:S(2)}, u32[]{:S(2)}) collective-permute-start(f32[32,128]{1,0:T(8,128)S(1)} %get-tuple-element.8), channel_id=1, source_target_pairs={{0,3},{1,2},{2,1},{3,0},{4,7},{5,6},{6,5},{7,4},{8,11},{9,10},{10,... | collective-permute-start | bytes 49160 | tf_op jit(solution)/shard_map/ppermute | solution.py:318
  13.8 1.4 %collective-permute-done.1 = f32[32,128]{1,0:T(8,128)S(1)} collective-permute-done((f32[32,128]{1,0:T(8,128)S(1)}, f32[32,128]{1,0:T(8,128)S(1)}, u32[]{:S(2)}, u32[]{:S(2)}) %collective-permute-start.1) | collective-permute-done | bytes 16416 | tf_op jit(solution)/shard_map/ppermute | solution.py:318
  15.2 1.7 %collective-permute-start.2 = (f32[32,128]{1,0:T(8,128)S(1)}, f32[32,128]{1,0:T(8,128)S(1)}, u32[]{:S(2)}, u32[]{:S(2)}) collective-permute-start(f32[32,128]{1,0:T(8,128)S(1)} %add.12), channel_id=1, source_target_pairs={{0,5},{1,4},{2,7},{3,6},{4,1},{5,0},{6,3},{7,2},{8,13},{9,12},{10,... | collective-permute-start | bytes 49160 | tf_op jit(solution)/shard_map/ppermute | solution.py:318
  16.9 1.4 %collective-permute-done.2 = f32[32,128]{1,0:T(8,128)S(1)} collective-permute-done((f32[32,128]{1,0:T(8,128)S(1)}, f32[32,128]{1,0:T(8,128)S(1)}, u32[]{:S(2)}, u32[]{:S(2)}) %collective-permute-start.2) | collective-permute-done | bytes 16416 | tf_op jit(solution)/shard_map/ppermute | solution.py:318
  18.4 1.8 %collective-permute-start.3 = (f32[32,128]{1,0:T(8,128)S(1)}, f32[32,128]{1,0:T(8,128)S(1)}, u32[]{:S(2)}, u32[]{:S(2)}) collective-permute-start(f32[32,128]{1,0:T(8,128)S(1)} %add.13), channel_id=1, source_target_pairs={{0,9},{1,8},{2,11},{3,10},{4,13},{5,12},{6,15},{7,14},{8,1},{9,0},... | collective-permute-start | bytes 49160 | tf_op jit(solution)/shard_map/ppermute | solution.py:318
  20.2 1.4 %collective-permute-done.3 = f32[32,128]{1,0:T(8,128)S(1)} collective-permute-done((f32[32,128]{1,0:T(8,128)S(1)}, f32[32,128]{1,0:T(8,128)S(1)}, u32[]{:S(2)}, u32[]{:S(2)}) %collective-permute-start.3) | collective-permute-done | bytes 16416 | tf_op jit(solution)/shard_map/ppermute | solution.py:318
  21.6 2.7 %collective-permute-start.4 = (f32[32,128]{1,0:T(8,128)S(1)}, f32[32,128]{1,0:T(8,128)S(1)}, u32[]{:S(2)}, u32[]{:S(2)}) collective-permute-start(f32[32,128]{1,0:T(8,128)S(1)} %add.14), channel_id=1, source_target_pairs={{0,17},{1,16},{2,19},{3,18},{4,21},{5,20},{6,23},{7,22},{8,25},{9,... | collective-permute-start | bytes 49160 | tf_op jit(solution)/shard_map/ppermute | solution.py:318
  24.4 1.4 %collective-permute-done.4 = f32[32,128]{1,0:T(8,128)S(1)} collective-permute-done((f32[32,128]{1,0:T(8,128)S(1)}, f32[32,128]{1,0:T(8,128)S(1)}, u32[]{:S(2)}, u32[]{:S(2)}) %collective-permute-start.4) | collective-permute-done | bytes 16416 | tf_op jit(solution)/shard_map/ppermute | solution.py:318
  25.8 2.3 %whiten.1 = f32[1,64,64]{2,1,0:T(8,128)} custom-call(f32[1,64,128]{2,1,0:T(8,128)S(1)} %get-tuple-element.7.rows_ref, f32[32,128]{1,0:T(8,128)S(1)} %add.15.gram_ref), custom_call_target="tpu_custom_call" | custom-call | tf_op jit(solution)/shard_map/whiten/pallas_call | solution.py:298
  (4 shorter events, 0.0 us)
Async XLA Ops:
  9.0 1.5 %collective-permute-start = (f32[256,128]{1,0:T(8,128)S(1)}, f32[256,128]{1,0:T(8,128)S(1)}, u32[]{:S(2)}, u32[]{:S(2)}) collective-permute-start(f32[256,128]{1,0:T(8,128)S(1)} %project.1.refs_1_), channel_id=1, source_target_pairs={{0,1},{1,0},{2,3},{3,2},{4,5},{5,4},{6,7},{7,6},{8,9},{9,8},{10,11... | collective-permute-start | bytes 393224 | tf_op jit(solution)/shard_map/ppermute | solution.py:333
  11.1 4.1 %collective-permute-start.1 = (f32[32,128]{1,0:T(8,128)S(1)}, f32[32,128]{1,0:T(8,128)S(1)}, u32[]{:S(2)}, u32[]{:S(2)}) collective-permute-start(f32[32,128]{1,0:T(8,128)S(1)} %get-tuple-element.8), channel_id=1, source_target_pairs={{0,3},{1,2},{2,1},{3,0},{4,7},{5,6},{6,5},{7,4},{8,11},{9,10},{10,... | collective-permute-start | bytes 49160 | tf_op jit(solution)/shard_map/ppermute | solution.py:318
  15.2 3.2 %collective-permute-start.2 = (f32[32,128]{1,0:T(8,128)S(1)}, f32[32,128]{1,0:T(8,128)S(1)}, u32[]{:S(2)}, u32[]{:S(2)}) collective-permute-start(f32[32,128]{1,0:T(8,128)S(1)} %add.12), channel_id=1, source_target_pairs={{0,5},{1,4},{2,7},{3,6},{4,1},{5,0},{6,3},{7,2},{8,13},{9,12},{10,... | collective-permute-start | bytes 49160 | tf_op jit(solution)/shard_map/ppermute | solution.py:318
  18.4 3.2 %collective-permute-start.3 = (f32[32,128]{1,0:T(8,128)S(1)}, f32[32,128]{1,0:T(8,128)S(1)}, u32[]{:S(2)}, u32[]{:S(2)}) collective-permute-start(f32[32,128]{1,0:T(8,128)S(1)} %add.13), channel_id=1, source_target_pairs={{0,9},{1,8},{2,11},{3,10},{4,13},{5,12},{6,15},{7,14},{8,1},{9,0},... | collective-permute-start | bytes 49160 | tf_op jit(solution)/shard_map/ppermute | solution.py:318
  21.6 4.2 %collective-permute-start.4 = (f32[32,128]{1,0:T(8,128)S(1)}, f32[32,128]{1,0:T(8,128)S(1)}, u32[]{:S(2)}, u32[]{:S(2)}) collective-permute-start(f32[32,128]{1,0:T(8,128)S(1)} %add.14), channel_id=1, source_target_pairs={{0,17},{1,16},{2,19},{3,18},{4,21},{5,20},{6,23},{7,22},{8,25},{9,... | collective-permute-start | bytes 49160 | tf_op jit(solution)/shard_map/ppermute | solution.py:318

commit v10 on v7

--- a/solution.py
+++ b/solution.py
@@ -28,13 +28,14 @@
 def project_kernel(gate, up, grad, proj_hidden, tokens, outer, proj_model, out, *rest):
     gate_v, up_v, grad_v, hidden_w, tokens_v, outer_v, model_w = rest[:7]
     hidden_sum, model_sum, sems, model_sems = rest[7:]
-    rows = gate.shape[0]
-    hidden_each, model_each = math.gcd(gate.shape[1], EACH), math.gcd(tokens.shape[1], EACH)
-    hidden_count = gate.shape[1] // hidden_each
+    rows, hidden_width = gate.shape
+    each = math.gcd(hidden_width, STEP)
+    full, spare = divmod(hidden_width - each, EACH)
+    model_each = math.gcd(tokens.shape[1], EACH)
     model_count = tokens.shape[1] // model_each
 
-    def hidden_copies(piece):
-        cut = pl.ds(pl.multiple_of(piece * hidden_each, hidden_each), hidden_each)
+    def hidden_copies(piece, begin, size):
+        cut = pl.ds(pl.multiple_of(begin, 128), size)
         pairs = [
             (gate.at[:, cut], gate_v.at[:, cut]),
             (grad.at[:, cut], grad_v.at[:, cut]),
@@ -45,6 +46,12 @@
             pltpu.make_async_copy(source, target, sems.at[piece, which])
             for which, (source, target) in enumerate(pairs)
         ]
+
+    def full_copies(piece):
+        return hidden_copies(piece + 1, each + piece * EACH, EACH)
+
+    def spare_copies():
+        return hidden_copies(full + 1, each + full * EACH, spare) if spare else []
 
     def model_copies(piece):
         cut = pl.ds(pl.multiple_of(piece * model_each, model_each), model_each)
@@ -66,42 +73,61 @@
         for copy in copies:
             copy.wait()
 
-    ahead = min(AHEAD, hidden_count)
+    def gated(begin):
+        cut = pl.ds(pl.multiple_of(begin, 128), each)
+        half = (gate_v[:, cut] * 0.5).astype(jnp.float32)
+        act = half + half * jnp.tanh(half)
+        up_grad = (grad_v[:, cut].astype(jnp.float32) * act).astype(jnp.bfloat16)
+        hidden = (act * up_v[:, cut].astype(jnp.float32)).astype(jnp.bfloat16)
+        return up_grad, hidden
+
+    def projected(begin, sides):
+        weights = hidden_w[pl.ds(pl.multiple_of(begin, 128), each), :]
+        return [jnp.dot(side, weights, preferred_element_type=jnp.float32) for side in sides]
+
+    def advance(begin, size, sides):
+        totals = None
+        for first in range(0, size, each):
+            parts = projected(begin + first - each, sides)
+            totals = [old + new for old, new in zip(totals, parts)] if totals else parts
+            sides = gated(begin + first)
+        for which, total in enumerate(totals):
+            hidden_sum[which * rows : (which + 1) * rows, :] += total
+        return sides
+
+    ahead = min(AHEAD, full)
+    start(hidden_copies(0, 0, each))
     for piece in range(ahead):
-        start(hidden_copies(piece))
+        start(full_copies(piece))
+    if not full:
+        start(spare_copies())
+        for other in range(model_count):
+            start(model_copies(other))
     hidden_sum[...] = jnp.zeros_like(hidden_sum)
     model_sum[...] = jnp.zeros_like(model_sum)
-
-    @pl.loop(0, hidden_count)
-    def _(piece):
-        arrive(hidden_copies(piece))
-
-        @pl.when(piece + ahead < hidden_count)
+    arrive(hidden_copies(0, 0, each))
+
+    def body(piece, sides):
+        arrive(full_copies(piece))
+
+        @pl.when(piece + ahead < full)
         def _():
-            start(hidden_copies(piece + ahead))
-
-        @pl.when(piece + ahead == hidden_count)
+            start(full_copies(piece + ahead))
+
+        @pl.when(piece + ahead == full)
         def _():
+            start(spare_copies())
             for other in range(model_count):
                 start(model_copies(other))
 
-        base = piece * hidden_each
-        totals = []
-        for first in range(0, hidden_each, STEP):
-            step = min(STEP, hidden_each - first)
-            cut = pl.ds(pl.multiple_of(base + first, 128), step)
-            half = gate_v[:, cut].astype(jnp.float32) * 0.5
-            act = half + half * jnp.tanh(half)
-            up_grad = (grad_v[:, cut].astype(jnp.float32) * act).astype(jnp.bfloat16)
-            hidden = (act * up_v[:, cut].astype(jnp.float32)).astype(jnp.bfloat16)
-            weights = hidden_w[cut, :]
-            parts = [
-                jnp.dot(side, weights, preferred_element_type=jnp.float32)
-                for side in (up_grad, hidden)
-            ]
-            totals = [old + new for old, new in zip(totals, parts)] if totals else parts
-        for which, total in enumerate(totals):
-            hidden_sum[which * rows : (which + 1) * rows, :] += total
+        return advance(each + piece * EACH, EACH, sides)
+
+    sides = lax.fori_loop(0, full, body, gated(0))
+    if spare:
+        arrive(spare_copies())
+        sides = advance(each + full * EACH, spare, sides)
+    for which, total in enumerate(projected(hidden_width - each, sides)):
+        hidden_sum[which * rows : (which + 1) * rows, :] += total
 
     @pl.loop(0, model_count)
     def _(piece):
@@ -139,7 +165,7 @@
             pltpu.VMEM((model_width, WIDE), held),
             pltpu.VMEM((2 * rows, WIDE), jnp.float32),
             pltpu.VMEM((2 * rows, WIDE), jnp.float32),
-            pltpu.SemaphoreType.DMA((hidden_width // math.gcd(hidden_width, EACH), 4)),
+            pltpu.SemaphoreType.DMA((hidden_width // EACH + 2, 4)),
             pltpu.SemaphoreType.DMA((model_width // math.gcd(model_width, EACH), 3)),
         ],
         compiler_params=pltpu.CompilerParams(vmem_limit_bytes=56 * 10**6),

time: 27.3 us -> 27.6 us (1.011)
  Pallas kernels: 10.9 us -> 11.3 us
    pallas_call x1, Pallas kernels: 8.03 us -> 8.35 us  [project(): pl.pallas_call(project_kernel, out_shape=jax.ShapeDtypeStruct((rows, 2 *...]
where the time goes in v10:
time: 27.6 us; the launch traced here: 27.5 us
  Pallas kernels  11.3 us (41%)
  starting transfers between devices  9.41 us (34%)
  waiting for transfers between devices  6.77 us (25%)
    ppermute x4, starting transfers between devices, summed_over_groups(): value = value + lax.ppermute(value, ('dp', 'mp'), pairs)  8.86 us
    pallas_call x1, Pallas kernels, project(): pl.pallas_call(project_kernel, out_shape=jax.ShapeDtypeStruct((rows, 2 *...  8.35 us
    ppermute x4, waiting for transfers between devices, summed_over_groups(): value = value + lax.ppermute(value, ('dp', 'mp'), pairs)  5.78 us
    pallas_call x1, Pallas kernels, whiten(): pl.pallas_call(functools.partial(whiten_kernel, factor, rows_each), out_s...  2.33 us
    ppermute x1, waiting for transfers between devices, shards(): parts.append(lax.ppermute(part, 'mp', pairs))  0.99 us
    pallas_call x1, Pallas kernels, gram_of(): pl.pallas_call(functools.partial(gram_kernel, rows_each, len(parts)), out...  0.58 us
    ppermute x1, starting transfers between devices, shards(): parts.append(lax.ppermute(part, 'mp', pairs))  0.56 us
  transfers between devices with their start and end apart: 5, of which 5 were waited for; matrix products, arithmetic and copies ran while one was open for 0% of the time, Pallas kernels for 0%

profile of v10, /device:TPU:0, one launch (start us, length us, event | category | flops | bytes accessed | tf_op | source)
XLA Modules:
  0.0 27.5 jit_solution(3160251667653265978)
XLA Ops:
  0.0 8.4 %project.1.refs_1_ = f32[128,256]{1,0:T(8,128)S(1)} custom-call(bf16[128,14336]{1,0:T(8,128)(2,1)} %gate.1, bf16[128,14336]{1,0:T(8,128)(2,1)} %up.1, bf16[128,14336]{1,0:T(8,128)(2,1)} %grad.1, bf16[14336,128]{1,0:T(8,128)(2,1)} %proj_hidden.1, bf16[128,4096]{1,0:T(8,128)(2,1)} %tokens.1, bf16[128,4096]{1,0:T(8,128)(2,1)} %outer.1, bf16[4096,128]{1,0:T(8,128)(2,1)} %proj_model.1), custom_call_target="tpu_custom_call" | custom-call | tf_op jit(solution)/shard_map/project/pallas_call | solution.py:153
  8.4 0.6 %collective-permute-start = (f32[128,256]{1,0:T(8,128)S(1)}, f32[128,256]{1,0:T(8,128)S(1)}, u32[]{:S(2)}, u32[]{:S(2)}) collective-permute-start(f32[128,256]{1,0:T(8,128)S(1)} %project.1.refs_1_), channel_id=1, source_target_pairs={{0,1},{1,0},{2,3},{3,2},{4,5},{5,4},{6,7},{7,6},{8,9},{9,8},{10,11... | collective-permute-start | bytes 393224 | tf_op jit(solution)/shard_map/ppermute | solution.py:357
  8.9 1.0 %collective-permute-done.refs_2_ = f32[128,256]{1,0:T(8,128)S(1)} collective-permute-done((f32[128,256]{1,0:T(8,128)S(1)}, f32[128,256]{1,0:T(8,128)S(1)}, u32[]{:S(2)}, u32[]{:S(2)}) %collective-permute-start) | collective-permute-done | bytes 131104 | tf_op jit(solution)/shard_map/ppermute | solution.py:357
  9.9 0.6 %gram.1 = (f32[1,64,128]{2,1,0:T(8,128)S(1)}, f32[32,128]{1,0:T(8,128)S(1)}) custom-call(s32[1]{0:T(128)} %bitcast.refs_0_, f32[128,256]{1,0:T(8,128)S(1)} %project.1.refs_1_, f32[128,256]{1,0:T(8,128)S(1)} %collective-permute-done.refs_2_), custom_call_target="tpu_custom_call" | custom-call | tf_op jit(solution)/shard_map/gram/pallas_call | solution.py:211
  10.5 2.6 %collective-permute-start.1 = (f32[32,128]{1,0:T(8,128)S(1)}, f32[32,128]{1,0:T(8,128)S(1)}, u32[]{:S(2)}, u32[]{:S(2)}) collective-permute-start(f32[32,128]{1,0:T(8,128)S(1)} %get-tuple-element.8), channel_id=1, source_target_pairs={{0,3},{1,2},{2,1},{3,0},{4,7},{5,6},{6,5},{7,4},{8,11},{9,10},{10,... | collective-permute-start | bytes 49160 | tf_op jit(solution)/shard_map/ppermute | solution.py:342
  13.1 1.4 %collective-permute-done.1 = f32[32,128]{1,0:T(8,128)S(1)} collective-permute-done((f32[32,128]{1,0:T(8,128)S(1)}, f32[32,128]{1,0:T(8,128)S(1)}, u32[]{:S(2)}, u32[]{:S(2)}) %collective-permute-start.1) | collective-permute-done | bytes 16416 | tf_op jit(solution)/shard_map/ppermute | solution.py:342
  14.5 1.7 %collective-permute-start.2 = (f32[32,128]{1,0:T(8,128)S(1)}, f32[32,128]{1,0:T(8,128)S(1)}, u32[]{:S(2)}, u32[]{:S(2)}) collective-permute-start(f32[32,128]{1,0:T(8,128)S(1)} %add.12), channel_id=1, source_target_pairs={{0,5},{1,4},{2,7},{3,6},{4,1},{5,0},{6,3},{7,2},{8,13},{9,12},{10,... | collective-permute-start | bytes 49160 | tf_op jit(solution)/shard_map/ppermute | solution.py:342
  16.3 1.5 %collective-permute-done.2 = f32[32,128]{1,0:T(8,128)S(1)} collective-permute-done((f32[32,128]{1,0:T(8,128)S(1)}, f32[32,128]{1,0:T(8,128)S(1)}, u32[]{:S(2)}, u32[]{:S(2)}) %collective-permute-start.2) | collective-permute-done | bytes 16416 | tf_op jit(solution)/shard_map/ppermute | solution.py:342
  17.7 1.8 %collective-permute-start.3 = (f32[32,128]{1,0:T(8,128)S(1)}, f32[32,128]{1,0:T(8,128)S(1)}, u32[]{:S(2)}, u32[]{:S(2)}) collective-permute-start(f32[32,128]{1,0:T(8,128)S(1)} %add.13), channel_id=1, source_target_pairs={{0,9},{1,8},{2,11},{3,10},{4,13},{5,12},{6,15},{7,14},{8,1},{9,0},... | collective-permute-start | bytes 49160 | tf_op jit(solution)/shard_map/ppermute | solution.py:342
  19.5 1.4 %collective-permute-done.3 = f32[32,128]{1,0:T(8,128)S(1)} collective-permute-done((f32[32,128]{1,0:T(8,128)S(1)}, f32[32,128]{1,0:T(8,128)S(1)}, u32[]{:S(2)}, u32[]{:S(2)}) %collective-permute-start.3) | collective-permute-done | bytes 16416 | tf_op jit(solution)/shard_map/ppermute | solution.py:342
  20.9 2.8 %collective-permute-start.4 = (f32[32,128]{1,0:T(8,128)S(1)}, f32[32,128]{1,0:T(8,128)S(1)}, u32[]{:S(2)}, u32[]{:S(2)}) collective-permute-start(f32[32,128]{1,0:T(8,128)S(1)} %add.14), channel_id=1, source_target_pairs={{0,17},{1,16},{2,19},{3,18},{4,21},{5,20},{6,23},{7,22},{8,25},{9,... | collective-permute-start | bytes 49160 | tf_op jit(solution)/shard_map/ppermute | solution.py:342
  23.7 1.4 %collective-permute-done.4 = f32[32,128]{1,0:T(8,128)S(1)} collective-permute-done((f32[32,128]{1,0:T(8,128)S(1)}, f32[32,128]{1,0:T(8,128)S(1)}, u32[]{:S(2)}, u32[]{:S(2)}) %collective-permute-start.4) | collective-permute-done | bytes 16416 | tf_op jit(solution)/shard_map/ppermute | solution.py:342
  25.1 2.3 %whiten.1 = f32[1,64,64]{2,1,0:T(8,128)} custom-call(f32[1,64,128]{2,1,0:T(8,128)S(1)} %get-tuple-element.7.rows_ref, f32[32,128]{1,0:T(8,128)S(1)} %add.15.gram_ref), custom_call_target="tpu_custom_call" | custom-call | tf_op jit(solution)/shard_map/whiten/pallas_call | solution.py:322
  (4 shorter events, 0.0 us)
Async XLA Ops:
  8.4 1.5 %collective-permute-start = (f32[128,256]{1,0:T(8,128)S(1)}, f32[128,256]{1,0:T(8,128)S(1)}, u32[]{:S(2)}, u32[]{:S(2)}) collective-permute-start(f32[128,256]{1,0:T(8,128)S(1)} %project.1.refs_1_), channel_id=1, source_target_pairs={{0,1},{1,0},{2,3},{3,2},{4,5},{5,4},{6,7},{7,6},{8,9},{9,8},{10,11... | collective-permute-start | bytes 393224 | tf_op jit(solution)/shard_map/ppermute | solution.py:357
  10.5 4.1 %collective-permute-start.1 = (f32[32,128]{1,0:T(8,128)S(1)}, f32[32,128]{1,0:T(8,128)S(1)}, u32[]{:S(2)}, u32[]{:S(2)}) collective-permute-start(f32[32,128]{1,0:T(8,128)S(1)} %get-tuple-element.8), channel_id=1, source_target_pairs={{0,3},{1,2},{2,1},{3,0},{4,7},{5,6},{6,5},{7,4},{8,11},{9,10},{10,... | collective-permute-start | bytes 49160 | tf_op jit(solution)/shard_map/ppermute | solution.py:342
  14.5 3.2 %collective-permute-start.2 = (f32[32,128]{1,0:T(8,128)S(1)}, f32[32,128]{1,0:T(8,128)S(1)}, u32[]{:S(2)}, u32[]{:S(2)}) collective-permute-start(f32[32,128]{1,0:T(8,128)S(1)} %add.12), channel_id=1, source_target_pairs={{0,5},{1,4},{2,7},{3,6},{4,1},{5,0},{6,3},{7,2},{8,13},{9,12},{10,... | collective-permute-start | bytes 49160 | tf_op jit(solution)/shard_map/ppermute | solution.py:342
  17.7 3.2 %collective-permute-start.3 = (f32[32,128]{1,0:T(8,128)S(1)}, f32[32,128]{1,0:T(8,128)S(1)}, u32[]{:S(2)}, u32[]{:S(2)}) collective-permute-start(f32[32,128]{1,0:T(8,128)S(1)} %add.13), channel_id=1, source_target_pairs={{0,9},{1,8},{2,11},{3,10},{4,13},{5,12},{6,15},{7,14},{8,1},{9,0},... | collective-permute-start | bytes 49160 | tf_op jit(solution)/shard_map/ppermute | solution.py:342
  20.9 4.2 %collective-permute-start.4 = (f32[32,128]{1,0:T(8,128)S(1)}, f32[32,128]{1,0:T(8,128)S(1)}, u32[]{:S(2)}, u32[]{:S(2)}) collective-permute-start(f32[32,128]{1,0:T(8,128)S(1)} %add.14), channel_id=1, source_target_pairs={{0,17},{1,16},{2,19},{3,18},{4,21},{5,20},{6,23},{7,22},{8,25},{9,... | collective-permute-start | bytes 49160 | tf_op jit(solution)/shard_map/ppermute | solution.py:342

commit v11 on v7

--- a/solution.py
+++ b/solution.py
@@ -13,7 +13,7 @@
 WIDE = 2 * RANK
 EACH = 1024
 STEP = 256
-AHEAD = 4
+AHEAD = 8
 
 highest = lax.Precision.HIGHEST
 whole_vmem = pl.BlockSpec(memory_space=pltpu.VMEM)
@@ -306,15 +306,21 @@
 
 def summed_over_groups(value):
     groups, model_shards = lax.axis_size("dp"), lax.axis_size("mp")
-    other = 1 if model_shards % 2 == 0 else 0
-    for level in range(groups.bit_length() - 1):
-        pairs = [
-            (group * model_shards + shard, (group ^ 2**level) * model_shards + (shard ^ other))
-            for group in range(groups)
-            for shard in range(model_shards)
-        ]
-        value = value + lax.ppermute(value, ("dp", "mp"), pairs)
-    return value
+    place = lax.axis_index("mp")
+
+    def over_groups(value):
+        for level in range(groups.bit_length() - 1):
+            pairs = [(source, source ^ 2**level) for source in range(groups)]
+            value = value + lax.ppermute(value, "dp", pairs)
+        return value
+
+    value = lax.cond(place == model_shards - 1, over_groups, lambda value: value, value)
+    result = value
+    for away in range(1, model_shards):
+        pairs = [(source, (source + away) % model_shards) for source in range(model_shards)]
+        received = lax.ppermute(value, "mp", pairs)
+        result = jnp.where(place == away - 1, received, result)
+    return result
 
 
 def shards(tokens_in, gate_pre, up_pre, hidden_grad, out_grad, proj_model, proj_hidden):

time: 27.3 us -> 26.1 us (0.956)
  waiting for transfers between devices: 6.76 us -> 1.83 us
  starting transfers between devices: 9.4 us -> 13.3 us
    ppermute x4 -> x1, waiting for transfers between devices: 5.77 us -> 0.84 us  [summed_over_groups(): received = lax.ppermute(value, 'mp', pairs)]
    ppermute x4 -> x1, starting transfers between devices: 8.88 us -> 12.8 us  [summed_over_groups(): received = lax.ppermute(value, 'mp', pairs)]
  transfers between devices with their start and end apart: 5 -> 2, of which waited for: 5 -> 2; matrix products, arithmetic and copies ran while one was open for 0% -> 0% of each run, Pallas kernels for 0% -> 0%
where the time goes in v11:
time: 26.1 us; the launch traced here: 25.9 us
  starting transfers between devices  13.3 us (51%)
  Pallas kernels  10.8 us (41%)
  waiting for transfers between devices  1.83 us (7%)
    ppermute x1, starting transfers between devices, summed_over_groups(): received = lax.ppermute(value, 'mp', pairs)  12.8 us
    pallas_call x1, Pallas kernels, project(): pl.pallas_call(project_kernel, out_shape=jax.ShapeDtypeStruct((rows, 2 *...  7.89 us
    pallas_call x1, Pallas kernels, whiten(): pl.pallas_call(functools.partial(whiten_kernel, factor, rows_each), out_s...  2.33 us
    ppermute x1, waiting for transfers between devices, shards(): parts.append(lax.ppermute(part, 'mp', pairs))  0.99 us
    ppermute x1, waiting for transfers between devices, summed_over_groups(): received = lax.ppermute(value, 'mp', pairs)  0.84 us
    pallas_call x1, Pallas kernels, gram_of(): pl.pallas_call(functools.partial(gram_kernel, rows_each, len(parts)), out...  0.58 us
  transfers between devices with their start and end apart: 2, of which 2 were waited for; matrix products, arithmetic and copies ran while one was open for 0% of the time, Pallas kernels for 0%

profile of v11, /device:TPU:0, one launch (start us, length us, event | category | flops | bytes accessed | tf_op | source)
XLA Modules:
  0.0 25.9 jit_solution(16521487397273315774)
XLA Ops:
  0.0 7.9 %project.1.refs_1_ = f32[128,256]{1,0:T(8,128)S(1)} custom-call(bf16[128,14336]{1,0:T(8,128)(2,1)} %gate.1, bf16[128,14336]{1,0:T(8,128)(2,1)} %up.1, bf16[128,14336]{1,0:T(8,128)(2,1)} %grad.1, bf16[14336,128]{1,0:T(8,128)(2,1)} %proj_hidden.1, bf16[128,4096]{1,0:T(8,128)(2,1)} %tokens.1, bf16[128,4096]{1,0:T(8,128)(2,1)} %outer.1, bf16[4096,128]{1,0:T(8,128)(2,1)} %proj_model.1), custom_call_target="tpu_custom_call" | custom-call | tf_op jit(solution)/shard_map/project/pallas_call | solution.py:127
  7.9 0.5 %collective-permute-start.4 = (f32[128,256]{1,0:T(8,128)S(1)}, f32[128,256]{1,0:T(8,128)S(1)}, u32[]{:S(2)}, u32[]{:S(2)}) collective-permute-start(f32[128,256]{1,0:T(8,128)S(1)} %project.1.refs_1_), channel_id=1, source_target_pairs={{0,1},{1,0},{2,3},{3,2},{4,5},{5,4},{6,7},{7,6},{8,9},{9,8},{10,11... | collective-permute-start | bytes 393224 | tf_op jit(solution)/shard_map/ppermute | solution.py:337
  8.4 1.0 %collective-permute-done.4.refs_2_ = f32[128,256]{1,0:T(8,128)S(1)} collective-permute-done((f32[128,256]{1,0:T(8,128)S(1)}, f32[128,256]{1,0:T(8,128)S(1)}, u32[]{:S(2)}, u32[]{:S(2)}) %collective-permute-start.4) | collective-permute-done | bytes 131104 | tf_op jit(solution)/shard_map/ppermute | solution.py:337
  9.4 0.6 %gram.1 = (f32[1,64,128]{2,1,0:T(8,128)S(1)}, f32[32,128]{1,0:T(8,128)S(1)}) custom-call(s32[1]{0:T(128)} %bitcast.refs_0_, f32[128,256]{1,0:T(8,128)S(1)} %project.1.refs_1_, f32[128,256]{1,0:T(8,128)S(1)} %collective-permute-done.4.refs_2_), custom_call_target="tpu_custom_call" | custom-call | tf_op jit(solution)/shard_map/gram/pallas_call | solution.py:185
  10.0 12.8 %collective-permute-start.5 = (f32[32,128]{1,0:T(8,128)S(1)}, f32[32,128]{1,0:T(8,128)S(1)}, u32[]{:S(2)}, u32[]{:S(2)}) collective-permute-start(f32[32,128]{1,0:T(8,128)S(1)} %get-tuple-element.14), channel_id=1, source_target_pairs={{0,1},{1,0},{2,3},{3,2},{4,5},{5,4},{6,7},{7,6},{8,9},{9,8},{10,11... | collective-permute-start | bytes 49160 | tf_op jit(solution)/shard_map/ppermute | solution.py:321
  22.8 0.8 %collective-permute-done.5 = f32[32,128]{1,0:T(8,128)S(1)} collective-permute-done((f32[32,128]{1,0:T(8,128)S(1)}, f32[32,128]{1,0:T(8,128)S(1)}, u32[]{:S(2)}, u32[]{:S(2)}) %collective-permute-start.5) | collective-permute-done | bytes 16416 | tf_op jit(solution)/shard_map/ppermute | solution.py:321
  23.6 2.3 %whiten.1 = f32[1,64,64]{2,1,0:T(8,128)} custom-call(f32[1,64,128]{2,1,0:T(8,128)S(1)} %get-tuple-element.12.rows_ref, f32[32,128]{1,0:T(8,128)S(1)} %broadcast_select_fusion.gram_ref), custom_call_target="tpu_custom_call" | custom-call | tf_op jit(solution)/shard_map/whiten/pallas_call | solution.py:296
  (2 shorter events, 0.0 us)
Async XLA Ops:
  7.9 1.5 %collective-permute-start.4 = (f32[128,256]{1,0:T(8,128)S(1)}, f32[128,256]{1,0:T(8,128)S(1)}, u32[]{:S(2)}, u32[]{:S(2)}) collective-permute-start(f32[128,256]{1,0:T(8,128)S(1)} %project.1.refs_1_), channel_id=1, source_target_pairs={{0,1},{1,0},{2,3},{3,2},{4,5},{5,4},{6,7},{7,6},{8,9},{9,8},{10,11... | collective-permute-start | bytes 393224 | tf_op jit(solution)/shard_map/ppermute | solution.py:337
  10.0 13.6 %collective-permute-start.5 = (f32[32,128]{1,0:T(8,128)S(1)}, f32[32,128]{1,0:T(8,128)S(1)}, u32[]{:S(2)}, u32[]{:S(2)}) collective-permute-start(f32[32,128]{1,0:T(8,128)S(1)} %get-tuple-element.14), channel_id=1, source_target_pairs={{0,1},{1,0},{2,3},{3,2},{4,5},{5,4},{6,7},{7,6},{8,9},{9,8},{10,11... | collective-permute-start | bytes 49160 | tf_op jit(solution)/shard_map/ppermute | solution.py:321

commit v12 on v11

--- a/solution.py
+++ b/solution.py
@@ -11,9 +11,10 @@
 RANK = 64
 LEN = 128
 WIDE = 2 * RANK
-EACH = 1024
-STEP = 256
-AHEAD = 8
+EACH = 2048
+MODEL_EACH = 512
+STEP = 512
+AHEAD = 4
 
 highest = lax.Precision.HIGHEST
 whole_vmem = pl.BlockSpec(memory_space=pltpu.VMEM)
@@ -29,7 +30,7 @@
     gate_v, up_v, grad_v, hidden_w, tokens_v, outer_v, model_w = rest[:7]
     hidden_sum, model_sum, sems, model_sems = rest[7:]
     rows = gate.shape[0]
-    hidden_each, model_each = math.gcd(gate.shape[1], EACH), math.gcd(tokens.shape[1], EACH)
+    hidden_each, model_each = math.gcd(gate.shape[1], EACH), math.gcd(tokens.shape[1], MODEL_EACH)
     hidden_count = gate.shape[1] // hidden_each
     model_count = tokens.shape[1] // model_each
 
@@ -90,7 +91,7 @@
         for first in range(0, hidden_each, STEP):
             step = min(STEP, hidden_each - first)
             cut = pl.ds(pl.multiple_of(base + first, 128), step)
-            half = gate_v[:, cut].astype(jnp.float32) * 0.5
+            half = (gate_v[:, cut] * 0.5).astype(jnp.float32)
             act = half + half * jnp.tanh(half)
             up_grad = (grad_v[:, cut].astype(jnp.float32) * act).astype(jnp.bfloat16)
             hidden = (act * up_v[:, cut].astype(jnp.float32)).astype(jnp.bfloat16)
@@ -140,7 +141,7 @@
             pltpu.VMEM((2 * rows, WIDE), jnp.float32),
             pltpu.VMEM((2 * rows, WIDE), jnp.float32),
             pltpu.SemaphoreType.DMA((hidden_width // math.gcd(hidden_width, EACH), 4)),
-            pltpu.SemaphoreType.DMA((model_width // math.gcd(model_width, EACH), 3)),
+            pltpu.SemaphoreType.DMA((model_width // math.gcd(model_width, MODEL_EACH), 3)),
         ],
         compiler_params=pltpu.CompilerParams(vmem_limit_bytes=56 * 10**6),
         name="project",

time: 26.1 us -> 26.4 us (1.011)
  Pallas kernels: 10.8 us -> 11.1 us
    pallas_call x1, Pallas kernels: 7.89 us -> 8.23 us  [project(): pl.pallas_call(project_kernel, out_shape=jax.ShapeDtypeStruct((rows, 2 *...]
where the time goes in v12:
time: 26.4 us; the launch traced here: 26.3 us
  starting transfers between devices  13.3 us (50%)
  Pallas kernels  11.1 us (42%)
  waiting for transfers between devices  1.83 us (7%)
    ppermute x1, starting transfers between devices, summed_over_groups(): received = lax.ppermute(value, 'mp', pairs)  12.8 us
    pallas_call x1, Pallas kernels, project(): pl.pallas_call(project_kernel, out_shape=jax.ShapeDtypeStruct((rows, 2 *...  8.23 us
    pallas_call x1, Pallas kernels, whiten(): pl.pallas_call(functools.partial(whiten_kernel, factor, rows_each), out_s...  2.33 us
    ppermute x1, waiting for transfers between devices, shards(): parts.append(lax.ppermute(part, 'mp', pairs))  0.99 us
    ppermute x1, waiting for transfers between devices, summed_over_groups(): received = lax.ppermute(value, 'mp', pairs)  0.84 us
    pallas_call x1, Pallas kernels, gram_of(): pl.pallas_call(functools.partial(gram_kernel, rows_each, len(parts)), out...  0.58 us
  transfers between devices with their start and end apart: 2, of which 2 were waited for; matrix products, arithmetic and copies ran while one was open for 0% of the time, Pallas kernels for 0%

profile of v12, /device:TPU:0, one launch (start us, length us, event | category | flops | bytes accessed | tf_op | source)
XLA Modules:
  0.0 26.3 jit_solution(15876916785453146520)
XLA Ops:
  0.0 8.2 %project.1.refs_1_ = f32[128,256]{1,0:T(8,128)S(1)} custom-call(bf16[128,14336]{1,0:T(8,128)(2,1)} %gate.1, bf16[128,14336]{1,0:T(8,128)(2,1)} %up.1, bf16[128,14336]{1,0:T(8,128)(2,1)} %grad.1, bf16[14336,128]{1,0:T(8,128)(2,1)} %proj_hidden.1, bf16[128,4096]{1,0:T(8,128)(2,1)} %tokens.1, bf16[128,4096]{1,0:T(8,128)(2,1)} %outer.1, bf16[4096,128]{1,0:T(8,128)(2,1)} %proj_model.1), custom_call_target="tpu_custom_call" | custom-call | tf_op jit(solution)/shard_map/project/pallas_call | solution.py:128
  8.2 0.5 %collective-permute-start.4 = (f32[128,256]{1,0:T(8,128)S(1)}, f32[128,256]{1,0:T(8,128)S(1)}, u32[]{:S(2)}, u32[]{:S(2)}) collective-permute-start(f32[128,256]{1,0:T(8,128)S(1)} %project.1.refs_1_), channel_id=1, source_target_pairs={{0,1},{1,0},{2,3},{3,2},{4,5},{5,4},{6,7},{7,6},{8,9},{9,8},{10,11... | collective-permute-start | bytes 393224 | tf_op jit(solution)/shard_map/ppermute | solution.py:338
  8.8 1.0 %collective-permute-done.4.refs_2_ = f32[128,256]{1,0:T(8,128)S(1)} collective-permute-done((f32[128,256]{1,0:T(8,128)S(1)}, f32[128,256]{1,0:T(8,128)S(1)}, u32[]{:S(2)}, u32[]{:S(2)}) %collective-permute-start.4) | collective-permute-done | bytes 131104 | tf_op jit(solution)/shard_map/ppermute | solution.py:338
  9.7 0.6 %gram.1 = (f32[1,64,128]{2,1,0:T(8,128)S(1)}, f32[32,128]{1,0:T(8,128)S(1)}) custom-call(s32[1]{0:T(128)} %bitcast.refs_0_, f32[128,256]{1,0:T(8,128)S(1)} %project.1.refs_1_, f32[128,256]{1,0:T(8,128)S(1)} %collective-permute-done.4.refs_2_), custom_call_target="tpu_custom_call" | custom-call | tf_op jit(solution)/shard_map/gram/pallas_call | solution.py:186
  10.3 12.8 %collective-permute-start.5 = (f32[32,128]{1,0:T(8,128)S(1)}, f32[32,128]{1,0:T(8,128)S(1)}, u32[]{:S(2)}, u32[]{:S(2)}) collective-permute-start(f32[32,128]{1,0:T(8,128)S(1)} %get-tuple-element.14), channel_id=1, source_target_pairs={{0,1},{1,0},{2,3},{3,2},{4,5},{5,4},{6,7},{7,6},{8,9},{9,8},{10,11... | collective-permute-start | bytes 49160 | tf_op jit(solution)/shard_map/ppermute | solution.py:322
  23.1 0.8 %collective-permute-done.5 = f32[32,128]{1,0:T(8,128)S(1)} collective-permute-done((f32[32,128]{1,0:T(8,128)S(1)}, f32[32,128]{1,0:T(8,128)S(1)}, u32[]{:S(2)}, u32[]{:S(2)}) %collective-permute-start.5) | collective-permute-done | bytes 16416 | tf_op jit(solution)/shard_map/ppermute | solution.py:322
  23.9 2.3 %whiten.1 = f32[1,64,64]{2,1,0:T(8,128)} custom-call(f32[1,64,128]{2,1,0:T(8,128)S(1)} %get-tuple-element.12.rows_ref, f32[32,128]{1,0:T(8,128)S(1)} %broadcast_select_fusion.gram_ref), custom_call_target="tpu_custom_call" | custom-call | tf_op jit(solution)/shard_map/whiten/pallas_call | solution.py:297
  (2 shorter events, 0.0 us)
Async XLA Ops:
  8.2 1.5 %collective-permute-start.4 = (f32[128,256]{1,0:T(8,128)S(1)}, f32[128,256]{1,0:T(8,128)S(1)}, u32[]{:S(2)}, u32[]{:S(2)}) collective-permute-start(f32[128,256]{1,0:T(8,128)S(1)} %project.1.refs_1_), channel_id=1, source_target_pairs={{0,1},{1,0},{2,3},{3,2},{4,5},{5,4},{6,7},{7,6},{8,9},{9,8},{10,11... | collective-permute-start | bytes 393224 | tf_op jit(solution)/shard_map/ppermute | solution.py:338
  10.3 13.6 %collective-permute-start.5 = (f32[32,128]{1,0:T(8,128)S(1)}, f32[32,128]{1,0:T(8,128)S(1)}, u32[]{:S(2)}, u32[]{:S(2)}) collective-permute-start(f32[32,128]{1,0:T(8,128)S(1)} %get-tuple-element.14), channel_id=1, source_target_pairs={{0,1},{1,0},{2,3},{3,2},{4,5},{5,4},{6,7},{7,6},{8,9},{9,8},{10,11... | collective-permute-start | bytes 49160 | tf_op jit(solution)/shard_map/ppermute | solution.py:322

commit v13 on v11

--- a/solution.py
+++ b/solution.py
@@ -59,8 +59,8 @@
         ]
 
     def start(copies):
-        for copy in copies:
-            copy.start()
+        for which, copy in enumerate(copies):
+            copy.start(priority=which % 2)
 
     def arrive(copies):
         for copy in copies:

time: 26.1 us -> 27.2 us (1.042)
  Pallas kernels: 10.8 us -> 11.9 us
    pallas_call x1, Pallas kernels: 7.89 us -> 9 us  [project(): pl.pallas_call(project_kernel, out_shape=jax.ShapeDtypeStruct((rows, 2 *...]
where the time goes in v13:
time: 27.2 us; the launch traced here: 27 us
  starting transfers between devices  13.3 us (49%)
  Pallas kernels  11.9 us (44%)
  waiting for transfers between devices  1.83 us (7%)
    ppermute x1, starting transfers between devices, summed_over_groups(): received = lax.ppermute(value, 'mp', pairs)  12.8 us
    pallas_call x1, Pallas kernels, project(): pl.pallas_call(project_kernel, out_shape=jax.ShapeDtypeStruct((rows, 2 *...  9 us
    pallas_call x1, Pallas kernels, whiten(): pl.pallas_call(functools.partial(whiten_kernel, factor, rows_each), out_s...  2.33 us
    ppermute x1, waiting for transfers between devices, shards(): parts.append(lax.ppermute(part, 'mp', pairs))  0.99 us
    ppermute x1, waiting for transfers between devices, summed_over_groups(): received = lax.ppermute(value, 'mp', pairs)  0.84 us
    pallas_call x1, Pallas kernels, gram_of(): pl.pallas_call(functools.partial(gram_kernel, rows_each, len(parts)), out...  0.58 us
  transfers between devices with their start and end apart: 2, of which 2 were waited for; matrix products, arithmetic and copies ran while one was open for 0% of the time, Pallas kernels for 0%

profile of v13, /device:TPU:0, one launch (start us, length us, event | category | flops | bytes accessed | tf_op | source)
XLA Modules:
  0.0 27.0 jit_solution(3119519835947289221)
XLA Ops:
  0.0 9.0 %project.1.refs_1_ = f32[128,256]{1,0:T(8,128)S(1)} custom-call(bf16[128,14336]{1,0:T(8,128)(2,1)} %gate.1, bf16[128,14336]{1,0:T(8,128)(2,1)} %up.1, bf16[128,14336]{1,0:T(8,128)(2,1)} %grad.1, bf16[14336,128]{1,0:T(8,128)(2,1)} %proj_hidden.1, bf16[128,4096]{1,0:T(8,128)(2,1)} %tokens.1, bf16[128,4096]{1,0:T(8,128)(2,1)} %outer.1, bf16[4096,128]{1,0:T(8,128)(2,1)} %proj_model.1), custom_call_target="tpu_custom_call" | custom-call | tf_op jit(solution)/shard_map/project/pallas_call | solution.py:127
  9.0 0.5 %collective-permute-start.4 = (f32[128,256]{1,0:T(8,128)S(1)}, f32[128,256]{1,0:T(8,128)S(1)}, u32[]{:S(2)}, u32[]{:S(2)}) collective-permute-start(f32[128,256]{1,0:T(8,128)S(1)} %project.1.refs_1_), channel_id=1, source_target_pairs={{0,1},{1,0},{2,3},{3,2},{4,5},{5,4},{6,7},{7,6},{8,9},{9,8},{10,11... | collective-permute-start | bytes 393224 | tf_op jit(solution)/shard_map/ppermute | solution.py:337
  9.5 1.0 %collective-permute-done.4.refs_2_ = f32[128,256]{1,0:T(8,128)S(1)} collective-permute-done((f32[128,256]{1,0:T(8,128)S(1)}, f32[128,256]{1,0:T(8,128)S(1)}, u32[]{:S(2)}, u32[]{:S(2)}) %collective-permute-start.4) | collective-permute-done | bytes 131104 | tf_op jit(solution)/shard_map/ppermute | solution.py:337
  10.5 0.6 %gram.1 = (f32[1,64,128]{2,1,0:T(8,128)S(1)}, f32[32,128]{1,0:T(8,128)S(1)}) custom-call(s32[1]{0:T(128)} %bitcast.refs_0_, f32[128,256]{1,0:T(8,128)S(1)} %project.1.refs_1_, f32[128,256]{1,0:T(8,128)S(1)} %collective-permute-done.4.refs_2_), custom_call_target="tpu_custom_call" | custom-call | tf_op jit(solution)/shard_map/gram/pallas_call | solution.py:185
  11.1 12.8 %collective-permute-start.5 = (f32[32,128]{1,0:T(8,128)S(1)}, f32[32,128]{1,0:T(8,128)S(1)}, u32[]{:S(2)}, u32[]{:S(2)}) collective-permute-start(f32[32,128]{1,0:T(8,128)S(1)} %get-tuple-element.14), channel_id=1, source_target_pairs={{0,1},{1,0},{2,3},{3,2},{4,5},{5,4},{6,7},{7,6},{8,9},{9,8},{10,11... | collective-permute-start | bytes 49160 | tf_op jit(solution)/shard_map/ppermute | solution.py:321
  23.9 0.8 %collective-permute-done.5 = f32[32,128]{1,0:T(8,128)S(1)} collective-permute-done((f32[32,128]{1,0:T(8,128)S(1)}, f32[32,128]{1,0:T(8,128)S(1)}, u32[]{:S(2)}, u32[]{:S(2)}) %collective-permute-start.5) | collective-permute-done | bytes 16416 | tf_op jit(solution)/shard_map/ppermute | solution.py:321
  24.7 2.3 %whiten.1 = f32[1,64,64]{2,1,0:T(8,128)} custom-call(f32[1,64,128]{2,1,0:T(8,128)S(1)} %get-tuple-element.12.rows_ref, f32[32,128]{1,0:T(8,128)S(1)} %broadcast_select_fusion.gram_ref), custom_call_target="tpu_custom_call" | custom-call | tf_op jit(solution)/shard_map/whiten/pallas_call | solution.py:296
  (2 shorter events, 0.0 us)
Async XLA Ops:
  9.0 1.5 %collective-permute-start.4 = (f32[128,256]{1,0:T(8,128)S(1)}, f32[128,256]{1,0:T(8,128)S(1)}, u32[]{:S(2)}, u32[]{:S(2)}) collective-permute-start(f32[128,256]{1,0:T(8,128)S(1)} %project.1.refs_1_), channel_id=1, source_target_pairs={{0,1},{1,0},{2,3},{3,2},{4,5},{5,4},{6,7},{7,6},{8,9},{9,8},{10,11... | collective-permute-start | bytes 393224 | tf_op jit(solution)/shard_map/ppermute | solution.py:337
  11.1 13.6 %collective-permute-start.5 = (f32[32,128]{1,0:T(8,128)S(1)}, f32[32,128]{1,0:T(8,128)S(1)}, u32[]{:S(2)}, u32[]{:S(2)}) collective-permute-start(f32[32,128]{1,0:T(8,128)S(1)} %get-tuple-element.14), channel_id=1, source_target_pairs={{0,1},{1,0},{2,3},{3,2},{4,5},{5,4},{6,7},{7,6},{8,9},{9,8},{10,11... | collective-permute-start | bytes 49160 | tf_op jit(solution)/shard_map/ppermute | solution.py:321

commit v14 on v12

--- a/solution.py
+++ b/solution.py
@@ -12,9 +12,10 @@
 LEN = 128
 WIDE = 2 * RANK
 EACH = 2048
-MODEL_EACH = 512
-STEP = 512
-AHEAD = 4
+HEAD = 512
+MODEL_EACH = 1024
+STEP = 256
+AHEAD = 3
 
 highest = lax.Precision.HIGHEST
 whole_vmem = pl.BlockSpec(memory_space=pltpu.VMEM)
@@ -22,6 +23,15 @@
 small = pltpu.CompilerParams(vmem_limit_bytes=8 * 2**20)
 
 
+def cuts_of(width):
+    full = max((width - 1) // EACH, 0)
+    head = width - full * EACH
+    ends = [0, min(HEAD, head)]
+    while ends[-1] < head:
+        ends.append(min(ends[-1] + EACH // 2, head))
+    return [(begin, end - begin) for begin, end in zip(ends, ends[1:])], full
+
+
 def lanes_of(shape):
     return lax.broadcasted_iota(jnp.int32, shape, len(shape) - 1)
 
@@ -30,12 +40,13 @@
     gate_v, up_v, grad_v, hidden_w, tokens_v, outer_v, model_w = rest[:7]
     hidden_sum, model_sum, sems, model_sems = rest[7:]
     rows = gate.shape[0]
-    hidden_each, model_each = math.gcd(gate.shape[1], EACH), math.gcd(tokens.shape[1], MODEL_EACH)
-    hidden_count = gate.shape[1] // hidden_each
+    model_each = math.gcd(tokens.shape[1], MODEL_EACH)
     model_count = tokens.shape[1] // model_each
-
-    def hidden_copies(piece):
-        cut = pl.ds(pl.multiple_of(piece * hidden_each, hidden_each), hidden_each)
+    head, full = cuts_of(gate.shape[1])
+    head_width = gate.shape[1] - full * EACH
+
+    def hidden_copies(slot, begin, size):
+        cut = pl.ds(pl.multiple_of(begin, 128), size)
         pairs = [
             (gate.at[:, cut], gate_v.at[:, cut]),
             (grad.at[:, cut], grad_v.at[:, cut]),
@@ -43,9 +54,12 @@
             (proj_hidden.at[cut, :], hidden_w.at[cut, :]),
         ]
         return [
-            pltpu.make_async_copy(source, target, sems.at[piece, which])
+            pltpu.make_async_copy(source, target, sems.at[slot, which])
             for which, (source, target) in enumerate(pairs)
         ]
+
+    def full_copies(piece):
+        return hidden_copies(len(head) + piece, head_width + piece * EACH, EACH)
 
     def model_copies(piece):
         cut = pl.ds(pl.multiple_of(piece * model_each, model_each), model_each)
@@ -67,30 +81,15 @@
         for copy in copies:
             copy.wait()
 
-    ahead = min(AHEAD, hidden_count)
-    for piece in range(ahead):
-        start(hidden_copies(piece))
-    hidden_sum[...] = jnp.zeros_like(hidden_sum)
-    model_sum[...] = jnp.zeros_like(model_sum)
-
-    @pl.loop(0, hidden_count)
-    def _(piece):
-        arrive(hidden_copies(piece))
-
-        @pl.when(piece + ahead < hidden_count)
-        def _():
-            start(hidden_copies(piece + ahead))
-
-        @pl.when(piece + ahead == hidden_count)
-        def _():
-            for other in range(model_count):
-                start(model_copies(other))
-
-        base = piece * hidden_each
+    def start_models():
+        for other in range(model_count):
+            start(model_copies(other))
+
+    def advance(begin, size):
         totals = []
-        for first in range(0, hidden_each, STEP):
-            step = min(STEP, hidden_each - first)
-            cut = pl.ds(pl.multiple_of(base + first, 128), step)
+        for first in range(0, size, STEP):
+            step = min(STEP, size - first)
+            cut = pl.ds(pl.multiple_of(begin + first, 128), step)
             half = (gate_v[:, cut] * 0.5).astype(jnp.float32)
             act = half + half * jnp.tanh(half)
             up_grad = (grad_v[:, cut].astype(jnp.float32) * act).astype(jnp.bfloat16)
@@ -104,6 +103,33 @@
         for which, total in enumerate(totals):
             hidden_sum[which * rows : (which + 1) * rows, :] += total
 
+    ahead = min(AHEAD, full)
+    for slot, (begin, size) in enumerate(head):
+        start(hidden_copies(slot, begin, size))
+    for piece in range(ahead):
+        start(full_copies(piece))
+    if not full:
+        start_models()
+    hidden_sum[...] = jnp.zeros_like(hidden_sum)
+    model_sum[...] = jnp.zeros_like(model_sum)
+    for slot, (begin, size) in enumerate(head):
+        arrive(hidden_copies(slot, begin, size))
+        advance(begin, size)
+
+    @pl.loop(0, full)
+    def _(piece):
+        arrive(full_copies(piece))
+
+        @pl.when(piece + ahead < full)
+        def _():
+            start(full_copies(piece + ahead))
+
+        @pl.when(piece + ahead == full)
+        def _():
+            start_models()
+
+        advance(head_width + piece * EACH, EACH)
+
     @pl.loop(0, model_count)
     def _(piece):
         arrive(model_copies(piece))
@@ -124,6 +150,8 @@
 def project(gate_pre, up_pre, hidden_grad, proj_hidden, tokens_in, out_grad, proj_model):
     rows, hidden_width = gate_pre.shape
     model_width = tokens_in.shape[1]
+    head, full = cuts_of(hidden_width)
+    hidden_slots = len(head) + full
     held = jnp.bfloat16
     return pl.pallas_call(
         project_kernel,
@@ -140,7 +168,7 @@
             pltpu.VMEM((model_width, WIDE), held),
             pltpu.VMEM((2 * rows, WIDE), jnp.float32),
             pltpu.VMEM((2 * rows, WIDE), jnp.float32),
-            pltpu.SemaphoreType.DMA((hidden_width // math.gcd(hidden_width, EACH), 4)),
+            pltpu.SemaphoreType.DMA((hidden_slots, 4)),
             pltpu.SemaphoreType.DMA((model_width // math.gcd(model_width, MODEL_EACH), 3)),
         ],
         compiler_params=pltpu.CompilerParams(vmem_limit_bytes=56 * 10**6),

time: 26.4 us -> 25.9 us (0.981)
  Pallas kernels: 11.1 us -> 10.7 us
    pallas_call x1, Pallas kernels: 8.23 us -> 7.75 us  [project(): pl.pallas_call(project_kernel, out_shape=jax.ShapeDtypeStruct((rows, 2 *...]
where the time goes in v14:
time: 25.9 us; the launch traced here: 25.8 us
  starting transfers between devices  13.3 us (51%)
  Pallas kernels  10.7 us (41%)
  waiting for transfers between devices  1.83 us (7%)
    ppermute x1, starting transfers between devices, summed_over_groups(): received = lax.ppermute(value, 'mp', pairs)  12.8 us
    pallas_call x1, Pallas kernels, project(): pl.pallas_call(project_kernel, out_shape=jax.ShapeDtypeStruct((rows, 2 *...  7.75 us
    pallas_call x1, Pallas kernels, whiten(): pl.pallas_call(functools.partial(whiten_kernel, factor, rows_each), out_s...  2.33 us
    ppermute x1, waiting for transfers between devices, shards(): parts.append(lax.ppermute(part, 'mp', pairs))  0.99 us
    ppermute x1, waiting for transfers between devices, summed_over_groups(): received = lax.ppermute(value, 'mp', pairs)  0.84 us
    pallas_call x1, Pallas kernels, gram_of(): pl.pallas_call(functools.partial(gram_kernel, rows_each, len(parts)), out...  0.58 us
    ppermute x1, starting transfers between devices, shards(): parts.append(lax.ppermute(part, 'mp', pairs))  0.52 us
  transfers between devices with their start and end apart: 2, of which 2 were waited for; matrix products, arithmetic and copies ran while one was open for 0% of the time, Pallas kernels for 0%

profile of v14, /device:TPU:0, one launch (start us, length us, event | category | flops | bytes accessed | tf_op | source)
XLA Modules:
  0.0 25.8 jit_solution(7013025714173721691)
XLA Ops:
  0.0 7.8 %project.1.refs_1_ = f32[128,256]{1,0:T(8,128)S(1)} custom-call(bf16[128,14336]{1,0:T(8,128)(2,1)} %gate.1, bf16[128,14336]{1,0:T(8,128)(2,1)} %up.1, bf16[128,14336]{1,0:T(8,128)(2,1)} %grad.1, bf16[14336,128]{1,0:T(8,128)(2,1)} %proj_hidden.1, bf16[128,4096]{1,0:T(8,128)(2,1)} %tokens.1, bf16[128,4096]{1,0:T(8,128)(2,1)} %outer.1, bf16[4096,128]{1,0:T(8,128)(2,1)} %proj_model.1), custom_call_target="tpu_custom_call" | custom-call | tf_op jit(solution)/shard_map/project/pallas_call | solution.py:156
  7.8 0.5 %collective-permute-start.4 = (f32[128,256]{1,0:T(8,128)S(1)}, f32[128,256]{1,0:T(8,128)S(1)}, u32[]{:S(2)}, u32[]{:S(2)}) collective-permute-start(f32[128,256]{1,0:T(8,128)S(1)} %project.1.refs_1_), channel_id=1, source_target_pairs={{0,1},{1,0},{2,3},{3,2},{4,5},{5,4},{6,7},{7,6},{8,9},{9,8},{10,11... | collective-permute-start | bytes 393224 | tf_op jit(solution)/shard_map/ppermute | solution.py:366
  8.3 1.0 %collective-permute-done.4.refs_2_ = f32[128,256]{1,0:T(8,128)S(1)} collective-permute-done((f32[128,256]{1,0:T(8,128)S(1)}, f32[128,256]{1,0:T(8,128)S(1)}, u32[]{:S(2)}, u32[]{:S(2)}) %collective-permute-start.4) | collective-permute-done | bytes 131104 | tf_op jit(solution)/shard_map/ppermute | solution.py:366
  9.3 0.6 %gram.1 = (f32[1,64,128]{2,1,0:T(8,128)S(1)}, f32[32,128]{1,0:T(8,128)S(1)}) custom-call(s32[1]{0:T(128)} %bitcast.refs_0_, f32[128,256]{1,0:T(8,128)S(1)} %project.1.refs_1_, f32[128,256]{1,0:T(8,128)S(1)} %collective-permute-done.4.refs_2_), custom_call_target="tpu_custom_call" | custom-call | tf_op jit(solution)/shard_map/gram/pallas_call | solution.py:214
  9.8 12.8 %collective-permute-start.5 = (f32[32,128]{1,0:T(8,128)S(1)}, f32[32,128]{1,0:T(8,128)S(1)}, u32[]{:S(2)}, u32[]{:S(2)}) collective-permute-start(f32[32,128]{1,0:T(8,128)S(1)} %get-tuple-element.14), channel_id=1, source_target_pairs={{0,1},{1,0},{2,3},{3,2},{4,5},{5,4},{6,7},{7,6},{8,9},{9,8},{10,11... | collective-permute-start | bytes 49160 | tf_op jit(solution)/shard_map/ppermute | solution.py:350
  22.6 0.8 %collective-permute-done.5 = f32[32,128]{1,0:T(8,128)S(1)} collective-permute-done((f32[32,128]{1,0:T(8,128)S(1)}, f32[32,128]{1,0:T(8,128)S(1)}, u32[]{:S(2)}, u32[]{:S(2)}) %collective-permute-start.5) | collective-permute-done | bytes 16416 | tf_op jit(solution)/shard_map/ppermute | solution.py:350
  23.5 2.3 %whiten.1 = f32[1,64,64]{2,1,0:T(8,128)} custom-call(f32[1,64,128]{2,1,0:T(8,128)S(1)} %get-tuple-element.12.rows_ref, f32[32,128]{1,0:T(8,128)S(1)} %broadcast_select_fusion.gram_ref), custom_call_target="tpu_custom_call" | custom-call | tf_op jit(solution)/shard_map/whiten/pallas_call | solution.py:325
  (2 shorter events, 0.0 us)
Async XLA Ops:
  7.8 1.5 %collective-permute-start.4 = (f32[128,256]{1,0:T(8,128)S(1)}, f32[128,256]{1,0:T(8,128)S(1)}, u32[]{:S(2)}, u32[]{:S(2)}) collective-permute-start(f32[128,256]{1,0:T(8,128)S(1)} %project.1.refs_1_), channel_id=1, source_target_pairs={{0,1},{1,0},{2,3},{3,2},{4,5},{5,4},{6,7},{7,6},{8,9},{9,8},{10,11... | collective-permute-start | bytes 393224 | tf_op jit(solution)/shard_map/ppermute | solution.py:366
  9.8 13.6 %collective-permute-start.5 = (f32[32,128]{1,0:T(8,128)S(1)}, f32[32,128]{1,0:T(8,128)S(1)}, u32[]{:S(2)}, u32[]{:S(2)}) collective-permute-start(f32[32,128]{1,0:T(8,128)S(1)} %get-tuple-element.14), channel_id=1, source_target_pairs={{0,1},{1,0},{2,3},{3,2},{4,5},{5,4},{6,7},{7,6},{8,9},{9,8},{10,11... | collective-permute-start | bytes 49160 | tf_op jit(solution)/shard_map/ppermute | solution.py:350

commit v15 on v14

--- a/solution.py
+++ b/solution.py
@@ -13,7 +13,6 @@
 WIDE = 2 * RANK
 EACH = 2048
 HEAD = 512
-MODEL_EACH = 1024
 STEP = 256
 AHEAD = 3
 
@@ -32,6 +31,13 @@
     return [(begin, end - begin) for begin, end in zip(ends, ends[1:])], full
 
 
+def shares_of(width, slots):
+    count = max(slots - 1, 1)
+    while width % (count * 128):
+        count -= 1
+    return width // count, count
+
+
 def lanes_of(shape):
     return lax.broadcasted_iota(jnp.int32, shape, len(shape) - 1)
 
@@ -40,10 +46,9 @@
     gate_v, up_v, grad_v, hidden_w, tokens_v, outer_v, model_w = rest[:7]
     hidden_sum, model_sum, sems, model_sems = rest[7:]
     rows = gate.shape[0]
-    model_each = math.gcd(tokens.shape[1], MODEL_EACH)
-    model_count = tokens.shape[1] // model_each
     head, full = cuts_of(gate.shape[1])
     head_width = gate.shape[1] - full * EACH
+    model_each, model_count = shares_of(tokens.shape[1], len(head) + full)
 
     def hidden_copies(slot, begin, size):
         cut = pl.ds(pl.multiple_of(begin, 128), size)
@@ -81,11 +86,17 @@
         for copy in copies:
             copy.wait()
 
-    def start_models():
-        for other in range(model_count):
-            start(model_copies(other))
-
-    def advance(begin, size):
+    def model_dots(begin, size):
+        cut = pl.ds(pl.multiple_of(begin, 128), size)
+        weights = model_w[cut, :]
+        for which, side in enumerate((tokens_v, outer_v)):
+            model_sum[which * rows : (which + 1) * rows, :] += jnp.dot(
+                side[:, cut], weights, preferred_element_type=jnp.float32
+            )
+
+    def advance(begin, size, share=None):
+        if share is not None:
+            model_dots(share * model_each, model_each)
         totals = []
         for first in range(0, size, STEP):
             step = min(STEP, size - first)
@@ -103,42 +114,46 @@
         for which, total in enumerate(totals):
             hidden_sum[which * rows : (which + 1) * rows, :] += total
 
+    taken = min(len(head) - 1, model_count)
+    looped = full if model_count - taken >= full else 0
     ahead = min(AHEAD, full)
+
+    def start_full(piece):
+        start(full_copies(piece))
+        if looped:
+            start(model_copies(taken + piece))
+
     for slot, (begin, size) in enumerate(head):
         start(hidden_copies(slot, begin, size))
+        if 0 < slot <= taken:
+            start(model_copies(slot - 1))
     for piece in range(ahead):
-        start(full_copies(piece))
-    if not full:
-        start_models()
+        start_full(piece)
+    for share in range(taken + looped, model_count):
+        start(model_copies(share))
     hidden_sum[...] = jnp.zeros_like(hidden_sum)
     model_sum[...] = jnp.zeros_like(model_sum)
     for slot, (begin, size) in enumerate(head):
         arrive(hidden_copies(slot, begin, size))
-        advance(begin, size)
+        if 0 < slot <= taken:
+            arrive(model_copies(slot - 1))
+        advance(begin, size, slot - 1 if 0 < slot <= taken else None)
 
     @pl.loop(0, full)
     def _(piece):
         arrive(full_copies(piece))
+        if looped:
+            arrive(model_copies(taken + piece))
 
         @pl.when(piece + ahead < full)
         def _():
-            start(full_copies(piece + ahead))
-
-        @pl.when(piece + ahead == full)
-        def _():
-            start_models()
-
-        advance(head_width + piece * EACH, EACH)
-
-    @pl.loop(0, model_count)
-    def _(piece):
-        arrive(model_copies(piece))
-        cut = pl.ds(pl.multiple_of(piece * model_each, model_each), model_each)
-        weights = model_w[cut, :]
-        for which, side in enumerate((tokens_v, outer_v)):
-            model_sum[which * rows : (which + 1) * rows, :] += jnp.dot(
-                side[:, cut], weights, preferred_element_type=jnp.float32
-            )
+            start_full(piece + ahead)
+
+        advance(head_width + piece * EACH, EACH, taken + piece if looped else None)
+
+    for share in range(taken + looped, model_count):
+        arrive(model_copies(share))
+        model_dots(share * model_each, model_each)
 
     low = lanes_of((rows, WIDE)) < RANK
     upward = pltpu.roll(hidden_sum[:rows, :], RANK, 1)
@@ -169,7 +184,7 @@
             pltpu.VMEM((2 * rows, WIDE), jnp.float32),
             pltpu.VMEM((2 * rows, WIDE), jnp.float32),
             pltpu.SemaphoreType.DMA((hidden_slots, 4)),
-            pltpu.SemaphoreType.DMA((model_width // math.gcd(model_width, MODEL_EACH), 3)),
+            pltpu.SemaphoreType.DMA((shares_of(model_width, hidden_slots)[1], 3)),
         ],
         compiler_params=pltpu.CompilerParams(vmem_limit_bytes=56 * 10**6),
         name="project",

time: 25.9 us -> 25.8 us (level)
  no operation moved by 1% of the time
where the time goes in v15:
time: 25.8 us; the launch traced here: 25.7 us
  starting transfers between devices  13.3 us (52%)
  Pallas kernels  10.5 us (41%)
  waiting for transfers between devices  1.83 us (7%)
    ppermute x1, starting transfers between devices, summed_over_groups(): received = lax.ppermute(value, 'mp', pairs)  12.8 us
    pallas_call x1, Pallas kernels, project(): pl.pallas_call(project_kernel, out_shape=jax.ShapeDtypeStruct((rows, 2 *...  7.62 us
    pallas_call x1, Pallas kernels, whiten(): pl.pallas_call(functools.partial(whiten_kernel, factor, rows_each), out_s...  2.33 us
    ppermute x1, waiting for transfers between devices, shards(): parts.append(lax.ppermute(part, 'mp', pairs))  0.99 us
    ppermute x1, waiting for transfers between devices, summed_over_groups(): received = lax.ppermute(value, 'mp', pairs)  0.84 us
    pallas_call x1, Pallas kernels, gram_of(): pl.pallas_call(functools.partial(gram_kernel, rows_each, len(parts)), out...  0.58 us
    ppermute x1, starting transfers between devices, shards(): parts.append(lax.ppermute(part, 'mp', pairs))  0.52 us
  transfers between devices with their start and end apart: 2, of which 2 were waited for; matrix products, arithmetic and copies ran while one was open for 0% of the time, Pallas kernels for 0%

profile of v15, /device:TPU:0, one launch (start us, length us, event | category | flops | bytes accessed | tf_op | source)
XLA Modules:
  0.0 25.7 jit_solution(8598732068866603438)
XLA Ops:
  0.0 7.6 %project.1.refs_1_ = f32[128,256]{1,0:T(8,128)S(1)} custom-call(bf16[128,14336]{1,0:T(8,128)(2,1)} %gate.1, bf16[128,14336]{1,0:T(8,128)(2,1)} %up.1, bf16[128,14336]{1,0:T(8,128)(2,1)} %grad.1, bf16[14336,128]{1,0:T(8,128)(2,1)} %proj_hidden.1, bf16[128,4096]{1,0:T(8,128)(2,1)} %tokens.1, bf16[128,4096]{1,0:T(8,128)(2,1)} %outer.1, bf16[4096,128]{1,0:T(8,128)(2,1)} %proj_model.1), custom_call_target="tpu_custom_call" | custom-call | tf_op jit(solution)/shard_map/project/pallas_call | solution.py:171
  7.6 0.5 %collective-permute-start.4 = (f32[128,256]{1,0:T(8,128)S(1)}, f32[128,256]{1,0:T(8,128)S(1)}, u32[]{:S(2)}, u32[]{:S(2)}) collective-permute-start(f32[128,256]{1,0:T(8,128)S(1)} %project.1.refs_1_), channel_id=1, source_target_pairs={{0,1},{1,0},{2,3},{3,2},{4,5},{5,4},{6,7},{7,6},{8,9},{9,8},{10,11... | collective-permute-start | bytes 393224 | tf_op jit(solution)/shard_map/ppermute | solution.py:381
  8.1 1.0 %collective-permute-done.4.refs_2_ = f32[128,256]{1,0:T(8,128)S(1)} collective-permute-done((f32[128,256]{1,0:T(8,128)S(1)}, f32[128,256]{1,0:T(8,128)S(1)}, u32[]{:S(2)}, u32[]{:S(2)}) %collective-permute-start.4) | collective-permute-done | bytes 131104 | tf_op jit(solution)/shard_map/ppermute | solution.py:381
  9.1 0.6 %gram.1 = (f32[1,64,128]{2,1,0:T(8,128)S(1)}, f32[32,128]{1,0:T(8,128)S(1)}) custom-call(s32[1]{0:T(128)} %bitcast.refs_0_, f32[128,256]{1,0:T(8,128)S(1)} %project.1.refs_1_, f32[128,256]{1,0:T(8,128)S(1)} %collective-permute-done.4.refs_2_), custom_call_target="tpu_custom_call" | custom-call | tf_op jit(solution)/shard_map/gram/pallas_call | solution.py:229
  9.7 12.8 %collective-permute-start.5 = (f32[32,128]{1,0:T(8,128)S(1)}, f32[32,128]{1,0:T(8,128)S(1)}, u32[]{:S(2)}, u32[]{:S(2)}) collective-permute-start(f32[32,128]{1,0:T(8,128)S(1)} %get-tuple-element.14), channel_id=1, source_target_pairs={{0,1},{1,0},{2,3},{3,2},{4,5},{5,4},{6,7},{7,6},{8,9},{9,8},{10,11... | collective-permute-start | bytes 49160 | tf_op jit(solution)/shard_map/ppermute | solution.py:365
  22.5 0.8 %collective-permute-done.5 = f32[32,128]{1,0:T(8,128)S(1)} collective-permute-done((f32[32,128]{1,0:T(8,128)S(1)}, f32[32,128]{1,0:T(8,128)S(1)}, u32[]{:S(2)}, u32[]{:S(2)}) %collective-permute-start.5) | collective-permute-done | bytes 16416 | tf_op jit(solution)/shard_map/ppermute | solution.py:365
  23.3 2.3 %whiten.1 = f32[1,64,64]{2,1,0:T(8,128)} custom-call(f32[1,64,128]{2,1,0:T(8,128)S(1)} %get-tuple-element.12.rows_ref, f32[32,128]{1,0:T(8,128)S(1)} %broadcast_select_fusion.gram_ref), custom_call_target="tpu_custom_call" | custom-call | tf_op jit(solution)/shard_map/whiten/pallas_call | solution.py:340
  (2 shorter events, 0.0 us)
Async XLA Ops:
  7.6 1.5 %collective-permute-start.4 = (f32[128,256]{1,0:T(8,128)S(1)}, f32[128,256]{1,0:T(8,128)S(1)}, u32[]{:S(2)}, u32[]{:S(2)}) collective-permute-start(f32[128,256]{1,0:T(8,128)S(1)} %project.1.refs_1_), channel_id=1, source_target_pairs={{0,1},{1,0},{2,3},{3,2},{4,5},{5,4},{6,7},{7,6},{8,9},{9,8},{10,11... | collective-permute-start | bytes 393224 | tf_op jit(solution)/shard_map/ppermute | solution.py:381
  9.7 13.6 %collective-permute-start.5 = (f32[32,128]{1,0:T(8,128)S(1)}, f32[32,128]{1,0:T(8,128)S(1)}, u32[]{:S(2)}, u32[]{:S(2)}) collective-permute-start(f32[32,128]{1,0:T(8,128)S(1)} %get-tuple-element.14), channel_id=1, source_target_pairs={{0,1},{1,0},{2,3},{3,2},{4,5},{5,4},{6,7},{7,6},{8,9},{9,8},{10,11... | collective-permute-start | bytes 49160 | tf_op jit(solution)/shard_map/ppermute | solution.py:365

commit v16 on v14

--- a/solution.py
+++ b/solution.py
@@ -86,7 +86,6 @@
             start(model_copies(other))
 
     def advance(begin, size):
-        totals = []
         for first in range(0, size, STEP):
             step = min(STEP, size - first)
             cut = pl.ds(pl.multiple_of(begin + first, 128), step)
@@ -95,13 +94,10 @@
             up_grad = (grad_v[:, cut].astype(jnp.float32) * act).astype(jnp.bfloat16)
             hidden = (act * up_v[:, cut].astype(jnp.float32)).astype(jnp.bfloat16)
             weights = hidden_w[cut, :]
-            parts = [
-                jnp.dot(side, weights, preferred_element_type=jnp.float32)
-                for side in (up_grad, hidden)
-            ]
-            totals = [old + new for old, new in zip(totals, parts)] if totals else parts
-        for which, total in enumerate(totals):
-            hidden_sum[which * rows : (which + 1) * rows, :] += total
+            for which, side in enumerate((up_grad, hidden)):
+                hidden_sum[which * rows : (which + 1) * rows, :] += jnp.dot(
+                    side, weights, preferred_element_type=jnp.float32
+                )
 
     ahead = min(AHEAD, full)
     for slot, (begin, size) in enumerate(head):
@@ -282,20 +278,26 @@
             for m in reversed(range(2, height)):
                 for k in range(m - m % 2):
                     back[k] = back[k] - factors[k, m] * back[m]
+            near = state[held + 2]
+            taken = [across(near, base + k) * back[k] for k in range(height)]
+            while len(taken) > 1:
+                taken = [left + right for left, right in zip(taken[::2], taken[1::2])]
+            state[held + 2] = near - taken[0]
+        if held + 3 < blocks:
             packed = back[0]
             for k in range(1, height):
                 packed = jnp.where(sub == k, back[k], packed)
             weights = [jnp.zeros_like(own)] * (2 * blocks)
             weights[blocks + held] = packed
-            later = jnp.concatenate(state[held + 2 :], axis=0)
+            later = jnp.concatenate(state[held + 3 :], axis=0)
             later = later - jnp.dot(
                 later,
                 jnp.concatenate(weights, axis=0),
                 precision=highest,
                 preferred_element_type=jnp.float32,
             )
-            for other in range(held + 2, blocks):
-                at = (other - held - 2) * height
+            for other in range(held + 3, blocks):
+                at = (other - held - 3) * height
                 state[other] = later[at : at + height]
         block = jnp.zeros_like(own)
         for k in range(0, height, 2):

time: 25.9 us -> 25.8 us (level)
  no operation moved by 1% of the time
where the time goes in v16:
time: 25.8 us; the launch traced here: 25.7 us
  starting transfers between devices  13.3 us (52%)
  Pallas kernels  10.6 us (41%)
  waiting for transfers between devices  1.83 us (7%)
    ppermute x1, starting transfers between devices, summed_over_groups(): received = lax.ppermute(value, 'mp', pairs)  12.8 us
    pallas_call x1, Pallas kernels, project(): pl.pallas_call(project_kernel, out_shape=jax.ShapeDtypeStruct((rows, 2 *...  7.75 us
    pallas_call x1, Pallas kernels, whiten(): pl.pallas_call(functools.partial(whiten_kernel, factor, rows_each), out_s...  2.25 us
    ppermute x1, waiting for transfers between devices, shards(): parts.append(lax.ppermute(part, 'mp', pairs))  0.99 us
    ppermute x1, waiting for transfers between devices, summed_over_groups(): received = lax.ppermute(value, 'mp', pairs)  0.84 us
    pallas_call x1, Pallas kernels, gram_of(): pl.pallas_call(functools.partial(gram_kernel, rows_each, len(parts)), out...  0.58 us
    ppermute x1, starting transfers between devices, shards(): parts.append(lax.ppermute(part, 'mp', pairs))  0.52 us
  transfers between devices with their start and end apart: 2, of which 2 were waited for; matrix products, arithmetic and copies ran while one was open for 0% of the time, Pallas kernels for 0%

profile of v16, /device:TPU:0, one launch (start us, length us, event | category | flops | bytes accessed | tf_op | source)
XLA Modules:
  0.0 25.7 jit_solution(2948145011301648480)
XLA Ops:
  0.0 7.8 %project.1.refs_1_ = f32[128,256]{1,0:T(8,128)S(1)} custom-call(bf16[128,14336]{1,0:T(8,128)(2,1)} %gate.1, bf16[128,14336]{1,0:T(8,128)(2,1)} %up.1, bf16[128,14336]{1,0:T(8,128)(2,1)} %grad.1, bf16[14336,128]{1,0:T(8,128)(2,1)} %proj_hidden.1, bf16[128,4096]{1,0:T(8,128)(2,1)} %tokens.1, bf16[128,4096]{1,0:T(8,128)(2,1)} %outer.1, bf16[4096,128]{1,0:T(8,128)(2,1)} %proj_model.1), custom_call_target="tpu_custom_call" | custom-call | tf_op jit(solution)/shard_map/project/pallas_call | solution.py:152
  7.8 0.5 %collective-permute-start.4 = (f32[128,256]{1,0:T(8,128)S(1)}, f32[128,256]{1,0:T(8,128)S(1)}, u32[]{:S(2)}, u32[]{:S(2)}) collective-permute-start(f32[128,256]{1,0:T(8,128)S(1)} %project.1.refs_1_), channel_id=1, source_target_pairs={{0,1},{1,0},{2,3},{3,2},{4,5},{5,4},{6,7},{7,6},{8,9},{9,8},{10,11... | collective-permute-start | bytes 393224 | tf_op jit(solution)/shard_map/ppermute | solution.py:368
  8.3 1.0 %collective-permute-done.4.refs_2_ = f32[128,256]{1,0:T(8,128)S(1)} collective-permute-done((f32[128,256]{1,0:T(8,128)S(1)}, f32[128,256]{1,0:T(8,128)S(1)}, u32[]{:S(2)}, u32[]{:S(2)}) %collective-permute-start.4) | collective-permute-done | bytes 131104 | tf_op jit(solution)/shard_map/ppermute | solution.py:368
  9.3 0.6 %gram.1 = (f32[1,64,128]{2,1,0:T(8,128)S(1)}, f32[32,128]{1,0:T(8,128)S(1)}) custom-call(s32[1]{0:T(128)} %bitcast.refs_0_, f32[128,256]{1,0:T(8,128)S(1)} %project.1.refs_1_, f32[128,256]{1,0:T(8,128)S(1)} %collective-permute-done.4.refs_2_), custom_call_target="tpu_custom_call" | custom-call | tf_op jit(solution)/shard_map/gram/pallas_call | solution.py:210
  9.8 12.8 %collective-permute-start.5 = (f32[32,128]{1,0:T(8,128)S(1)}, f32[32,128]{1,0:T(8,128)S(1)}, u32[]{:S(2)}, u32[]{:S(2)}) collective-permute-start(f32[32,128]{1,0:T(8,128)S(1)} %get-tuple-element.14), channel_id=1, source_target_pairs={{0,1},{1,0},{2,3},{3,2},{4,5},{5,4},{6,7},{7,6},{8,9},{9,8},{10,11... | collective-permute-start | bytes 49160 | tf_op jit(solution)/shard_map/ppermute | solution.py:352
  22.6 0.8 %collective-permute-done.5 = f32[32,128]{1,0:T(8,128)S(1)} collective-permute-done((f32[32,128]{1,0:T(8,128)S(1)}, f32[32,128]{1,0:T(8,128)S(1)}, u32[]{:S(2)}, u32[]{:S(2)}) %collective-permute-start.5) | collective-permute-done | bytes 16416 | tf_op jit(solution)/shard_map/ppermute | solution.py:352
  23.5 2.2 %whiten.1 = f32[1,64,64]{2,1,0:T(8,128)} custom-call(f32[1,64,128]{2,1,0:T(8,128)S(1)} %get-tuple-element.12.rows_ref, f32[32,128]{1,0:T(8,128)S(1)} %broadcast_select_fusion.gram_ref), custom_call_target="tpu_custom_call" | custom-call | tf_op jit(solution)/shard_map/whiten/pallas_call | solution.py:327
  (2 shorter events, 0.0 us)
Async XLA Ops:
  7.8 1.5 %collective-permute-start.4 = (f32[128,256]{1,0:T(8,128)S(1)}, f32[128,256]{1,0:T(8,128)S(1)}, u32[]{:S(2)}, u32[]{:S(2)}) collective-permute-start(f32[128,256]{1,0:T(8,128)S(1)} %project.1.refs_1_), channel_id=1, source_target_pairs={{0,1},{1,0},{2,3},{3,2},{4,5},{5,4},{6,7},{7,6},{8,9},{9,8},{10,11... | collective-permute-start | bytes 393224 | tf_op jit(solution)/shard_map/ppermute | solution.py:368
  9.8 13.6 %collective-permute-start.5 = (f32[32,128]{1,0:T(8,128)S(1)}, f32[32,128]{1,0:T(8,128)S(1)}, u32[]{:S(2)}, u32[]{:S(2)}) collective-permute-start(f32[32,128]{1,0:T(8,128)S(1)} %get-tuple-element.14), channel_id=1, source_target_pairs={{0,1},{1,0},{2,3},{3,2},{4,5},{5,4},{6,7},{7,6},{8,9},{9,8},{10,11... | collective-permute-start | bytes 49160 | tf_op jit(solution)/shard_map/ppermute | solution.py:352

commit v17 on v16

--- a/solution.py
+++ b/solution.py
@@ -15,7 +15,7 @@
 HEAD = 512
 MODEL_EACH = 1024
 STEP = 256
-AHEAD = 3
+AHEAD = 6
 
 highest = lax.Precision.HIGHEST
 whole_vmem = pl.BlockSpec(memory_space=pltpu.VMEM)
@@ -34,6 +34,16 @@
 
 def lanes_of(shape):
     return lax.broadcasted_iota(jnp.int32, shape, len(shape) - 1)
+
+
+def paired(left, right, weights):
+    low = lanes_of(weights.shape) < RANK
+    none = jnp.zeros_like(weights)
+    return jnp.dot(
+        jnp.concatenate([left, right], axis=1),
+        jnp.concatenate([jnp.where(low, weights, none), jnp.where(low, none, weights)], axis=0),
+        preferred_element_type=jnp.float32,
+    )
 
 
 def project_kernel(gate, up, grad, proj_hidden, tokens, outer, proj_model, out, *rest):
@@ -86,6 +96,7 @@
             start(model_copies(other))
 
     def advance(begin, size):
+        total = None
         for first in range(0, size, STEP):
             step = min(STEP, size - first)
             cut = pl.ds(pl.multiple_of(begin + first, 128), step)
@@ -93,11 +104,9 @@
             act = half + half * jnp.tanh(half)
             up_grad = (grad_v[:, cut].astype(jnp.float32) * act).astype(jnp.bfloat16)
             hidden = (act * up_v[:, cut].astype(jnp.float32)).astype(jnp.bfloat16)
-            weights = hidden_w[cut, :]
-            for which, side in enumerate((up_grad, hidden)):
-                hidden_sum[which * rows : (which + 1) * rows, :] += jnp.dot(
-                    side, weights, preferred_element_type=jnp.float32
-                )
+            part = paired(up_grad, hidden, hidden_w[cut, :])
+            total = part if total is None else total + part
+        hidden_sum[...] += total
 
     ahead = min(AHEAD, full)
     for slot, (begin, size) in enumerate(head):
@@ -130,17 +139,12 @@
     def _(piece):
         arrive(model_copies(piece))
         cut = pl.ds(pl.multiple_of(piece * model_each, model_each), model_each)
-        weights = model_w[cut, :]
-        for which, side in enumerate((tokens_v, outer_v)):
-            model_sum[which * rows : (which + 1) * rows, :] += jnp.dot(
-                side[:, cut], weights, preferred_element_type=jnp.float32
-            )
+        model_sum[...] += paired(tokens_v[:, cut], outer_v[:, cut], model_w[cut, :])
 
     low = lanes_of((rows, WIDE)) < RANK
-    upward = pltpu.roll(hidden_sum[:rows, :], RANK, 1)
-    hidden_side = pltpu.roll(hidden_sum[rows:, :], RANK, 1)
-    out[:, :WIDE] = jnp.where(low, model_sum[:rows, :], upward)
-    out[:, WIDE:] = jnp.where(low, hidden_side, model_sum[rows:, :])
+    turned = pltpu.roll(hidden_sum[...], RANK, 1)
+    out[:, :WIDE] = jnp.where(low, model_sum[...], turned)
+    out[:, WIDE:] = jnp.where(low, turned, model_sum[...])
 
 
 def project(gate_pre, up_pre, hidden_grad, proj_hidden, tokens_in, out_grad, proj_model):
@@ -162,8 +166,8 @@
             pltpu.VMEM((rows, model_width), held),
             pltpu.VMEM((rows, model_width), held),
             pltpu.VMEM((model_width, WIDE), held),
-            pltpu.VMEM((2 * rows, WIDE), jnp.float32),
-            pltpu.VMEM((2 * rows, WIDE), jnp.float32),
+            pltpu.VMEM((rows, WIDE), jnp.float32),
+            pltpu.VMEM((rows, WIDE), jnp.float32),
             pltpu.SemaphoreType.DMA((hidden_slots, 4)),
             pltpu.SemaphoreType.DMA((model_width // math.gcd(model_width, MODEL_EACH), 3)),
         ],

time: 25.8 us -> 25.8 us (level)
  no operation moved by 1% of the time
where the time goes in v17:
time: 25.8 us; the launch traced here: 25.6 us
  starting transfers between devices  13.3 us (52%)
  Pallas kernels  10.5 us (41%)
  waiting for transfers between devices  1.83 us (7%)
    ppermute x1, starting transfers between devices, summed_over_groups(): received = lax.ppermute(value, 'mp', pairs)  12.8 us
    pallas_call x1, Pallas kernels, project(): pl.pallas_call(project_kernel, out_shape=jax.ShapeDtypeStruct((rows, 2 *...  7.68 us
    pallas_call x1, Pallas kernels, whiten(): pl.pallas_call(functools.partial(whiten_kernel, factor, rows_each), out_s...  2.25 us
    ppermute x1, waiting for transfers between devices, shards(): parts.append(lax.ppermute(part, 'mp', pairs))  0.99 us
    ppermute x1, waiting for transfers between devices, summed_over_groups(): received = lax.ppermute(value, 'mp', pairs)  0.84 us
    pallas_call x1, Pallas kernels, gram_of(): pl.pallas_call(functools.partial(gram_kernel, rows_each, len(parts)), out...  0.58 us
  transfers between devices with their start and end apart: 2, of which 2 were waited for; matrix products, arithmetic and copies ran while one was open for 0% of the time, Pallas kernels for 0%

profile of v17, /device:TPU:0, one launch (start us, length us, event | category | flops | bytes accessed | tf_op | source)
XLA Modules:
  0.0 25.6 jit_solution(6520400771426603691)
XLA Ops:
  0.0 7.7 %project.1.refs_1_ = f32[128,256]{1,0:T(8,128)S(1)} custom-call(bf16[128,14336]{1,0:T(8,128)(2,1)} %gate.1, bf16[128,14336]{1,0:T(8,128)(2,1)} %up.1, bf16[128,14336]{1,0:T(8,128)(2,1)} %grad.1, bf16[14336,128]{1,0:T(8,128)(2,1)} %proj_hidden.1, bf16[128,4096]{1,0:T(8,128)(2,1)} %tokens.1, bf16[128,4096]{1,0:T(8,128)(2,1)} %outer.1, bf16[4096,128]{1,0:T(8,128)(2,1)} %proj_model.1), custom_call_target="tpu_custom_call" | custom-call | tf_op jit(solution)/shard_map/project/pallas_call | solution.py:156
  7.7 0.5 %collective-permute-start.4 = (f32[128,256]{1,0:T(8,128)S(1)}, f32[128,256]{1,0:T(8,128)S(1)}, u32[]{:S(2)}, u32[]{:S(2)}) collective-permute-start(f32[128,256]{1,0:T(8,128)S(1)} %project.1.refs_1_), channel_id=1, source_target_pairs={{0,1},{1,0},{2,3},{3,2},{4,5},{5,4},{6,7},{7,6},{8,9},{9,8},{10,11... | collective-permute-start | bytes 393224 | tf_op jit(solution)/shard_map/ppermute | solution.py:372
  8.2 1.0 %collective-permute-done.4.refs_2_ = f32[128,256]{1,0:T(8,128)S(1)} collective-permute-done((f32[128,256]{1,0:T(8,128)S(1)}, f32[128,256]{1,0:T(8,128)S(1)}, u32[]{:S(2)}, u32[]{:S(2)}) %collective-permute-start.4) | collective-permute-done | bytes 131104 | tf_op jit(solution)/shard_map/ppermute | solution.py:372
  9.2 0.6 %gram.1 = (f32[1,64,128]{2,1,0:T(8,128)S(1)}, f32[32,128]{1,0:T(8,128)S(1)}) custom-call(s32[1]{0:T(128)} %bitcast.refs_0_, f32[128,256]{1,0:T(8,128)S(1)} %project.1.refs_1_, f32[128,256]{1,0:T(8,128)S(1)} %collective-permute-done.4.refs_2_), custom_call_target="tpu_custom_call" | custom-call | tf_op jit(solution)/shard_map/gram/pallas_call | solution.py:214
  9.8 12.8 %collective-permute-start.5 = (f32[32,128]{1,0:T(8,128)S(1)}, f32[32,128]{1,0:T(8,128)S(1)}, u32[]{:S(2)}, u32[]{:S(2)}) collective-permute-start(f32[32,128]{1,0:T(8,128)S(1)} %get-tuple-element.14), channel_id=1, source_target_pairs={{0,1},{1,0},{2,3},{3,2},{4,5},{5,4},{6,7},{7,6},{8,9},{9,8},{10,11... | collective-permute-start | bytes 49160 | tf_op jit(solution)/shard_map/ppermute | solution.py:356
  22.5 0.8 %collective-permute-done.5 = f32[32,128]{1,0:T(8,128)S(1)} collective-permute-done((f32[32,128]{1,0:T(8,128)S(1)}, f32[32,128]{1,0:T(8,128)S(1)}, u32[]{:S(2)}, u32[]{:S(2)}) %collective-permute-start.5) | collective-permute-done | bytes 16416 | tf_op jit(solution)/shard_map/ppermute | solution.py:356
  23.4 2.2 %whiten.1 = f32[1,64,64]{2,1,0:T(8,128)} custom-call(f32[1,64,128]{2,1,0:T(8,128)S(1)} %get-tuple-element.12.rows_ref, f32[32,128]{1,0:T(8,128)S(1)} %broadcast_select_fusion.gram_ref), custom_call_target="tpu_custom_call" | custom-call | tf_op jit(solution)/shard_map/whiten/pallas_call | solution.py:331
  (2 shorter events, 0.0 us)
Async XLA Ops:
  7.7 1.5 %collective-permute-start.4 = (f32[128,256]{1,0:T(8,128)S(1)}, f32[128,256]{1,0:T(8,128)S(1)}, u32[]{:S(2)}, u32[]{:S(2)}) collective-permute-start(f32[128,256]{1,0:T(8,128)S(1)} %project.1.refs_1_), channel_id=1, source_target_pairs={{0,1},{1,0},{2,3},{3,2},{4,5},{5,4},{6,7},{7,6},{8,9},{9,8},{10,11... | collective-permute-start | bytes 393224 | tf_op jit(solution)/shard_map/ppermute | solution.py:372
  9.8 13.6 %collective-permute-start.5 = (f32[32,128]{1,0:T(8,128)S(1)}, f32[32,128]{1,0:T(8,128)S(1)}, u32[]{:S(2)}, u32[]{:S(2)}) collective-permute-start(f32[32,128]{1,0:T(8,128)S(1)} %get-tuple-element.14), channel_id=1, source_target_pairs={{0,1},{1,0},{2,3},{3,2},{4,5},{5,4},{6,7},{7,6},{8,9},{9,8},{10,11... | collective-permute-start | bytes 49160 | tf_op jit(solution)/shard_map/ppermute | solution.py:356

commit v18 on v17

--- a/solution.py
+++ b/solution.py
@@ -13,7 +13,7 @@
 WIDE = 2 * RANK
 EACH = 2048
 HEAD = 512
-MODEL_EACH = 1024
+LEAST = 256
 STEP = 256
 AHEAD = 6
 
@@ -30,6 +30,17 @@
     while ends[-1] < head:
         ends.append(min(ends[-1] + EACH // 2, head))
     return [(begin, end - begin) for begin, end in zip(ends, ends[1:])], full
+
+
+def shrinking(width):
+    cuts, begin = [], 0
+    while begin < width:
+        size = width - begin
+        if size > LEAST and size % 256 == 0:
+            size //= 2
+        cuts.append((begin, size))
+        begin += size
+    return cuts
 
 
 def lanes_of(shape):
@@ -48,10 +59,9 @@
 
 def project_kernel(gate, up, grad, proj_hidden, tokens, outer, proj_model, out, *rest):
     gate_v, up_v, grad_v, hidden_w, tokens_v, outer_v, model_w = rest[:7]
-    hidden_sum, model_sum, sems, model_sems = rest[7:]
+    hidden_sum, sems, model_sems = rest[7:]
     rows = gate.shape[0]
-    model_each = math.gcd(tokens.shape[1], MODEL_EACH)
-    model_count = tokens.shape[1] // model_each
+    model_cuts = shrinking(tokens.shape[1])
     head, full = cuts_of(gate.shape[1])
     head_width = gate.shape[1] - full * EACH
 
@@ -72,7 +82,7 @@
         return hidden_copies(len(head) + piece, head_width + piece * EACH, EACH)
 
     def model_copies(piece):
-        cut = pl.ds(pl.multiple_of(piece * model_each, model_each), model_each)
+        cut = pl.ds(*model_cuts[piece])
         pairs = [
             (tokens.at[:, cut], tokens_v.at[:, cut]),
             (outer.at[:, cut], outer_v.at[:, cut]),
@@ -92,7 +102,7 @@
             copy.wait()
 
     def start_models():
-        for other in range(model_count):
+        for other in range(len(model_cuts)):
             start(model_copies(other))
 
     def advance(begin, size):
@@ -116,7 +126,6 @@
     if not full:
         start_models()
     hidden_sum[...] = jnp.zeros_like(hidden_sum)
-    model_sum[...] = jnp.zeros_like(model_sum)
     for slot, (begin, size) in enumerate(head):
         arrive(hidden_copies(slot, begin, size))
         advance(begin, size)
@@ -135,16 +144,17 @@
 
         advance(head_width + piece * EACH, EACH)
 
-    @pl.loop(0, model_count)
-    def _(piece):
+    total = None
+    for piece, (begin, size) in enumerate(model_cuts):
         arrive(model_copies(piece))
-        cut = pl.ds(pl.multiple_of(piece * model_each, model_each), model_each)
-        model_sum[...] += paired(tokens_v[:, cut], outer_v[:, cut], model_w[cut, :])
+        cut = slice(begin, begin + size)
+        part = paired(tokens_v[:, cut], outer_v[:, cut], model_w[cut, :])
+        total = part if total is None else total + part
 
     low = lanes_of((rows, WIDE)) < RANK
     turned = pltpu.roll(hidden_sum[...], RANK, 1)
-    out[:, :WIDE] = jnp.where(low, model_sum[...], turned)
-    out[:, WIDE:] = jnp.where(low, turned, model_sum[...])
+    out[:, :WIDE] = jnp.where(low, total, turned)
+    out[:, WIDE:] = jnp.where(low, turned, total)
 
 
 def project(gate_pre, up_pre, hidden_grad, proj_hidden, tokens_in, out_grad, proj_model):
@@ -167,9 +177,8 @@
             pltpu.VMEM((rows, model_width), held),
             pltpu.VMEM((model_width, WIDE), held),
             pltpu.VMEM((rows, WIDE), jnp.float32),
-            pltpu.VMEM((rows, WIDE), jnp.float32),
             pltpu.SemaphoreType.DMA((hidden_slots, 4)),
-            pltpu.SemaphoreType.DMA((model_width // math.gcd(model_width, MODEL_EACH), 3)),
+            pltpu.SemaphoreType.DMA((len(shrinking(model_width)), 3)),
         ],
         compiler_params=pltpu.CompilerParams(vmem_limit_bytes=56 * 10**6),
         name="project",

time: 25.8 us -> 25.9 us (level)
  no operation moved by 1% of the time
where the time goes in v18:
time: 25.9 us; the launch traced here: 25.8 us
  starting transfers between devices  13.3 us (51%)
  Pallas kernels  10.6 us (41%)
  waiting for transfers between devices  1.83 us (7%)
    ppermute x1, starting transfers between devices, summed_over_groups(): received = lax.ppermute(value, 'mp', pairs)  12.8 us
    pallas_call x1, Pallas kernels, project(): pl.pallas_call(project_kernel, out_shape=jax.ShapeDtypeStruct((rows, 2 *...  7.79 us
    pallas_call x1, Pallas kernels, whiten(): pl.pallas_call(functools.partial(whiten_kernel, factor, rows_each), out_s...  2.25 us
    ppermute x1, waiting for transfers between devices, shards(): parts.append(lax.ppermute(part, 'mp', pairs))  0.99 us
    ppermute x1, waiting for transfers between devices, summed_over_groups(): received = lax.ppermute(value, 'mp', pairs)  0.84 us
    pallas_call x1, Pallas kernels, gram_of(): pl.pallas_call(functools.partial(gram_kernel, rows_each, len(parts)), out...  0.58 us
    ppermute x1, starting transfers between devices, shards(): parts.append(lax.ppermute(part, 'mp', pairs))  0.53 us
  transfers between devices with their start and end apart: 2, of which 2 were waited for; matrix products, arithmetic and copies ran while one was open for 0% of the time, Pallas kernels for 0%

profile of v18, /device:TPU:0, one launch (start us, length us, event | category | flops | bytes accessed | tf_op | source)
XLA Modules:
  0.0 25.8 jit_solution(11287137231594818922)
XLA Ops:
  0.0 7.8 %project.1.refs_1_ = f32[128,256]{1,0:T(8,128)S(1)} custom-call(bf16[128,14336]{1,0:T(8,128)(2,1)} %gate.1, bf16[128,14336]{1,0:T(8,128)(2,1)} %up.1, bf16[128,14336]{1,0:T(8,128)(2,1)} %grad.1, bf16[14336,128]{1,0:T(8,128)(2,1)} %proj_hidden.1, bf16[128,4096]{1,0:T(8,128)(2,1)} %tokens.1, bf16[128,4096]{1,0:T(8,128)(2,1)} %outer.1, bf16[4096,128]{1,0:T(8,128)(2,1)} %proj_model.1), custom_call_target="tpu_custom_call" | custom-call | tf_op jit(solution)/shard_map/project/pallas_call | solution.py:166
  7.8 0.5 %collective-permute-start.4 = (f32[128,256]{1,0:T(8,128)S(1)}, f32[128,256]{1,0:T(8,128)S(1)}, u32[]{:S(2)}, u32[]{:S(2)}) collective-permute-start(f32[128,256]{1,0:T(8,128)S(1)} %project.1.refs_1_), channel_id=1, source_target_pairs={{0,1},{1,0},{2,3},{3,2},{4,5},{5,4},{6,7},{7,6},{8,9},{9,8},{10,11... | collective-permute-start | bytes 393224 | tf_op jit(solution)/shard_map/ppermute | solution.py:381
  8.3 1.0 %collective-permute-done.4.refs_2_ = f32[128,256]{1,0:T(8,128)S(1)} collective-permute-done((f32[128,256]{1,0:T(8,128)S(1)}, f32[128,256]{1,0:T(8,128)S(1)}, u32[]{:S(2)}, u32[]{:S(2)}) %collective-permute-start.4) | collective-permute-done | bytes 131104 | tf_op jit(solution)/shard_map/ppermute | solution.py:381
  9.3 0.6 %gram.1 = (f32[1,64,128]{2,1,0:T(8,128)S(1)}, f32[32,128]{1,0:T(8,128)S(1)}) custom-call(s32[1]{0:T(128)} %bitcast.refs_0_, f32[128,256]{1,0:T(8,128)S(1)} %project.1.refs_1_, f32[128,256]{1,0:T(8,128)S(1)} %collective-permute-done.4.refs_2_), custom_call_target="tpu_custom_call" | custom-call | tf_op jit(solution)/shard_map/gram/pallas_call | solution.py:223
  9.9 12.8 %collective-permute-start.5 = (f32[32,128]{1,0:T(8,128)S(1)}, f32[32,128]{1,0:T(8,128)S(1)}, u32[]{:S(2)}, u32[]{:S(2)}) collective-permute-start(f32[32,128]{1,0:T(8,128)S(1)} %get-tuple-element.14), channel_id=1, source_target_pairs={{0,1},{1,0},{2,3},{3,2},{4,5},{5,4},{6,7},{7,6},{8,9},{9,8},{10,11... | collective-permute-start | bytes 49160 | tf_op jit(solution)/shard_map/ppermute | solution.py:365
  22.7 0.8 %collective-permute-done.5 = f32[32,128]{1,0:T(8,128)S(1)} collective-permute-done((f32[32,128]{1,0:T(8,128)S(1)}, f32[32,128]{1,0:T(8,128)S(1)}, u32[]{:S(2)}, u32[]{:S(2)}) %collective-permute-start.5) | collective-permute-done | bytes 16416 | tf_op jit(solution)/shard_map/ppermute | solution.py:365
  23.5 2.2 %whiten.1 = f32[1,64,64]{2,1,0:T(8,128)} custom-call(f32[1,64,128]{2,1,0:T(8,128)S(1)} %get-tuple-element.12.rows_ref, f32[32,128]{1,0:T(8,128)S(1)} %broadcast_select_fusion.gram_ref), custom_call_target="tpu_custom_call" | custom-call | tf_op jit(solution)/shard_map/whiten/pallas_call | solution.py:340
  (2 shorter events, 0.0 us)
Async XLA Ops:
  7.8 1.5 %collective-permute-start.4 = (f32[128,256]{1,0:T(8,128)S(1)}, f32[128,256]{1,0:T(8,128)S(1)}, u32[]{:S(2)}, u32[]{:S(2)}) collective-permute-start(f32[128,256]{1,0:T(8,128)S(1)} %project.1.refs_1_), channel_id=1, source_target_pairs={{0,1},{1,0},{2,3},{3,2},{4,5},{5,4},{6,7},{7,6},{8,9},{9,8},{10,11... | collective-permute-start | bytes 393224 | tf_op jit(solution)/shard_map/ppermute | solution.py:381
  9.9 13.6 %collective-permute-start.5 = (f32[32,128]{1,0:T(8,128)S(1)}, f32[32,128]{1,0:T(8,128)S(1)}, u32[]{:S(2)}, u32[]{:S(2)}) collective-permute-start(f32[32,128]{1,0:T(8,128)S(1)} %get-tuple-element.14), channel_id=1, source_target_pairs={{0,1},{1,0},{2,3},{3,2},{4,5},{5,4},{6,7},{7,6},{8,9},{9,8},{10,11... | collective-permute-start | bytes 49160 | tf_op jit(solution)/shard_map/ppermute | solution.py:365

commit v19 on v17

--- a/solution.py
+++ b/solution.py
@@ -46,9 +46,20 @@
     )
 
 
+def paired_across(left, right, weights):
+    both = lax.dot_general(
+        weights,
+        jnp.concatenate([left, right], axis=0),
+        (((0,), (1,)), ((), ())),
+        preferred_element_type=jnp.float32,
+    )
+    rows = left.shape[0]
+    return jnp.concatenate([both[:RANK, :rows], both[RANK:, rows:]], axis=0)
+
+
 def project_kernel(gate, up, grad, proj_hidden, tokens, outer, proj_model, out, *rest):
     gate_v, up_v, grad_v, hidden_w, tokens_v, outer_v, model_w = rest[:7]
-    hidden_sum, model_sum, sems, model_sems = rest[7:]
+    hidden_sum, model_sum, hidden_turned, model_turned, sems, model_sems = rest[7:]
     rows = gate.shape[0]
     model_each = math.gcd(tokens.shape[1], MODEL_EACH)
     model_count = tokens.shape[1] // model_each
@@ -95,8 +106,10 @@
         for other in range(model_count):
             start(model_copies(other))
 
+    forms = (paired, paired_across)
+
     def advance(begin, size):
-        total = None
+        totals = {}
         for first in range(0, size, STEP):
             step = min(STEP, size - first)
             cut = pl.ds(pl.multiple_of(begin + first, 128), step)
@@ -104,9 +117,12 @@
             act = half + half * jnp.tanh(half)
             up_grad = (grad_v[:, cut].astype(jnp.float32) * act).astype(jnp.bfloat16)
             hidden = (act * up_v[:, cut].astype(jnp.float32)).astype(jnp.bfloat16)
-            part = paired(up_grad, hidden, hidden_w[cut, :])
-            total = part if total is None else total + part
-        hidden_sum[...] += total
+            form = forms[first // STEP % 2]
+            part = form(up_grad, hidden, hidden_w[cut, :])
+            totals[form] = totals[form] + part if form in totals else part
+        for form, sums in zip(forms, (hidden_sum, hidden_turned)):
+            if form in totals:
+                sums[...] += totals[form]
 
     ahead = min(AHEAD, full)
     for slot, (begin, size) in enumerate(head):
@@ -116,7 +132,8 @@
     if not full:
         start_models()
     hidden_sum[...] = jnp.zeros_like(hidden_sum)
-    model_sum[...] = jnp.zeros_like(model_sum)
+    for sums in (model_sum, hidden_turned, model_turned):
+        sums[...] = jnp.zeros_like(sums)
     for slot, (begin, size) in enumerate(head):
         arrive(hidden_copies(slot, begin, size))
         advance(begin, size)
@@ -138,13 +155,19 @@
     @pl.loop(0, model_count)
     def _(piece):
         arrive(model_copies(piece))
-        cut = pl.ds(pl.multiple_of(piece * model_each, model_each), model_each)
-        model_sum[...] += paired(tokens_v[:, cut], outer_v[:, cut], model_w[cut, :])
+        half = model_each // 2 if model_each % 256 == 0 else model_each
+        begin = pl.multiple_of(piece * model_each, model_each)
+        for first, form, sums in zip(
+            range(0, model_each, half), forms, (model_sum, model_turned)
+        ):
+            cut = pl.ds(pl.multiple_of(begin + first, 128), half)
+            sums[...] += form(tokens_v[:, cut], outer_v[:, cut], model_w[cut, :])
 
     low = lanes_of((rows, WIDE)) < RANK
-    turned = pltpu.roll(hidden_sum[...], RANK, 1)
-    out[:, :WIDE] = jnp.where(low, model_sum[...], turned)
-    out[:, WIDE:] = jnp.where(low, turned, model_sum[...])
+    turned = pltpu.roll(hidden_sum[...] + hidden_turned[...].T, RANK, 1)
+    straight = model_sum[...] + model_turned[...].T
+    out[:, :WIDE] = jnp.where(low, straight, turned)
+    out[:, WIDE:] = jnp.where(low, turned, straight)
 
 
 def project(gate_pre, up_pre, hidden_grad, proj_hidden, tokens_in, out_grad, proj_model):
@@ -168,6 +191,8 @@
             pltpu.VMEM((model_width, WIDE), held),
             pltpu.VMEM((rows, WIDE), jnp.float32),
             pltpu.VMEM((rows, WIDE), jnp.float32),
+            pltpu.VMEM((WIDE, rows), jnp.float32),
+            pltpu.VMEM((WIDE, rows), jnp.float32),
             pltpu.SemaphoreType.DMA((hidden_slots, 4)),
             pltpu.SemaphoreType.DMA((model_width // math.gcd(model_width, MODEL_EACH), 3)),
         ],

time: 25.8 us -> 25.8 us (level)
  no operation moved by 1% of the time
where the time goes in v19:
time: 25.8 us; the launch traced here: 25.7 us
  starting transfers between devices  13.3 us (52%)
  Pallas kernels  10.5 us (41%)
  waiting for transfers between devices  1.83 us (7%)
    ppermute x1, starting transfers between devices, summed_over_groups(): received = lax.ppermute(value, 'mp', pairs)  12.8 us
    pallas_call x1, Pallas kernels, project(): pl.pallas_call(project_kernel, out_shape=jax.ShapeDtypeStruct((rows, 2 *...  7.71 us
    pallas_call x1, Pallas kernels, whiten(): pl.pallas_call(functools.partial(whiten_kernel, factor, rows_each), out_s...  2.25 us
    ppermute x1, waiting for transfers between devices, shards(): parts.append(lax.ppermute(part, 'mp', pairs))  0.99 us
    ppermute x1, waiting for transfers between devices, summed_over_groups(): received = lax.ppermute(value, 'mp', pairs)  0.84 us
    pallas_call x1, Pallas kernels, gram_of(): pl.pallas_call(functools.partial(gram_kernel, rows_each, len(parts)), out...  0.58 us
    ppermute x1, starting transfers between devices, shards(): parts.append(lax.ppermute(part, 'mp', pairs))  0.52 us
  transfers between devices with their start and end apart: 2, of which 2 were waited for; matrix products, arithmetic and copies ran while one was open for 0% of the time, Pallas kernels for 0%

profile of v19, /device:TPU:0, one launch (start us, length us, event | category | flops | bytes accessed | tf_op | source)
XLA Modules:
  0.0 25.7 jit_solution(17537876213542758150)
XLA Ops:
  0.0 7.7 %project.1.refs_1_ = f32[128,256]{1,0:T(8,128)S(1)} custom-call(bf16[128,14336]{1,0:T(8,128)(2,1)} %gate.1, bf16[128,14336]{1,0:T(8,128)(2,1)} %up.1, bf16[128,14336]{1,0:T(8,128)(2,1)} %grad.1, bf16[14336,128]{1,0:T(8,128)(2,1)} %proj_hidden.1, bf16[128,4096]{1,0:T(8,128)(2,1)} %tokens.1, bf16[128,4096]{1,0:T(8,128)(2,1)} %outer.1, bf16[4096,128]{1,0:T(8,128)(2,1)} %proj_model.1), custom_call_target="tpu_custom_call" | custom-call | tf_op jit(solution)/shard_map/project/pallas_call | solution.py:179
  7.7 0.5 %collective-permute-start.4 = (f32[128,256]{1,0:T(8,128)S(1)}, f32[128,256]{1,0:T(8,128)S(1)}, u32[]{:S(2)}, u32[]{:S(2)}) collective-permute-start(f32[128,256]{1,0:T(8,128)S(1)} %project.1.refs_1_), channel_id=1, source_target_pairs={{0,1},{1,0},{2,3},{3,2},{4,5},{5,4},{6,7},{7,6},{8,9},{9,8},{10,11... | collective-permute-start | bytes 393224 | tf_op jit(solution)/shard_map/ppermute | solution.py:397
  8.2 1.0 %collective-permute-done.4.refs_2_ = f32[128,256]{1,0:T(8,128)S(1)} collective-permute-done((f32[128,256]{1,0:T(8,128)S(1)}, f32[128,256]{1,0:T(8,128)S(1)}, u32[]{:S(2)}, u32[]{:S(2)}) %collective-permute-start.4) | collective-permute-done | bytes 131104 | tf_op jit(solution)/shard_map/ppermute | solution.py:397
  9.2 0.6 %gram.1 = (f32[1,64,128]{2,1,0:T(8,128)S(1)}, f32[32,128]{1,0:T(8,128)S(1)}) custom-call(s32[1]{0:T(128)} %bitcast.refs_0_, f32[128,256]{1,0:T(8,128)S(1)} %project.1.refs_1_, f32[128,256]{1,0:T(8,128)S(1)} %collective-permute-done.4.refs_2_), custom_call_target="tpu_custom_call" | custom-call | tf_op jit(solution)/shard_map/gram/pallas_call | solution.py:239
  9.8 12.8 %collective-permute-start.5 = (f32[32,128]{1,0:T(8,128)S(1)}, f32[32,128]{1,0:T(8,128)S(1)}, u32[]{:S(2)}, u32[]{:S(2)}) collective-permute-start(f32[32,128]{1,0:T(8,128)S(1)} %get-tuple-element.14), channel_id=1, source_target_pairs={{0,1},{1,0},{2,3},{3,2},{4,5},{5,4},{6,7},{7,6},{8,9},{9,8},{10,11... | collective-permute-start | bytes 49160 | tf_op jit(solution)/shard_map/ppermute | solution.py:381
  22.6 0.8 %collective-permute-done.5 = f32[32,128]{1,0:T(8,128)S(1)} collective-permute-done((f32[32,128]{1,0:T(8,128)S(1)}, f32[32,128]{1,0:T(8,128)S(1)}, u32[]{:S(2)}, u32[]{:S(2)}) %collective-permute-start.5) | collective-permute-done | bytes 16416 | tf_op jit(solution)/shard_map/ppermute | solution.py:381
  23.4 2.2 %whiten.1 = f32[1,64,64]{2,1,0:T(8,128)} custom-call(f32[1,64,128]{2,1,0:T(8,128)S(1)} %get-tuple-element.12.rows_ref, f32[32,128]{1,0:T(8,128)S(1)} %broadcast_select_fusion.gram_ref), custom_call_target="tpu_custom_call" | custom-call | tf_op jit(solution)/shard_map/whiten/pallas_call | solution.py:356
  (2 shorter events, 0.0 us)
Async XLA Ops:
  7.7 1.5 %collective-permute-start.4 = (f32[128,256]{1,0:T(8,128)S(1)}, f32[128,256]{1,0:T(8,128)S(1)}, u32[]{:S(2)}, u32[]{:S(2)}) collective-permute-start(f32[128,256]{1,0:T(8,128)S(1)} %project.1.refs_1_), channel_id=1, source_target_pairs={{0,1},{1,0},{2,3},{3,2},{4,5},{5,4},{6,7},{7,6},{8,9},{9,8},{10,11... | collective-permute-start | bytes 393224 | tf_op jit(solution)/shard_map/ppermute | solution.py:397
  9.8 13.6 %collective-permute-start.5 = (f32[32,128]{1,0:T(8,128)S(1)}, f32[32,128]{1,0:T(8,128)S(1)}, u32[]{:S(2)}, u32[]{:S(2)}) collective-permute-start(f32[32,128]{1,0:T(8,128)S(1)} %get-tuple-element.14), channel_id=1, source_target_pairs={{0,1},{1,0},{2,3},{3,2},{4,5},{5,4},{6,7},{7,6},{8,9},{9,8},{10,11... | collective-permute-start | bytes 49160 | tf_op jit(solution)/shard_map/ppermute | solution.py:381

commit v20 on v17

--- a/solution.py
+++ b/solution.py
@@ -11,11 +11,12 @@
 RANK = 64
 LEN = 128
 WIDE = 2 * RANK
-EACH = 2048
+EACH = 4096
+BODY = 2048
 HEAD = 512
-MODEL_EACH = 1024
+MODEL_EACH = 2048
 STEP = 256
-AHEAD = 6
+AHEAD = 4
 
 highest = lax.Precision.HIGHEST
 whole_vmem = pl.BlockSpec(memory_space=pltpu.VMEM)
@@ -28,7 +29,7 @@
     head = width - full * EACH
     ends = [0, min(HEAD, head)]
     while ends[-1] < head:
-        ends.append(min(ends[-1] + EACH // 2, head))
+        ends.append(min(ends[-1] + BODY // 2, head))
     return [(begin, end - begin) for begin, end in zip(ends, ends[1:])], full
 
 
@@ -133,7 +134,9 @@
         def _():
             start_models()
 
-        advance(head_width + piece * EACH, EACH)
+        @pl.loop(0, EACH // BODY)
+        def _(part):
+            advance(head_width + piece * EACH + part * BODY, BODY)
 
     @pl.loop(0, model_count)
     def _(piece):

time: 25.8 us -> 25.9 us (level)
  no operation moved by 1% of the time
where the time goes in v20:
time: 25.9 us; the launch traced here: 25.7 us
  starting transfers between devices  13.3 us (51%)
  Pallas kernels  10.6 us (41%)
  waiting for transfers between devices  1.83 us (7%)
    ppermute x1, starting transfers between devices, summed_over_groups(): received = lax.ppermute(value, 'mp', pairs)  12.8 us
    pallas_call x1, Pallas kernels, project(): pl.pallas_call(project_kernel, out_shape=jax.ShapeDtypeStruct((rows, 2 *...  7.78 us
    pallas_call x1, Pallas kernels, whiten(): pl.pallas_call(functools.partial(whiten_kernel, factor, rows_each), out_s...  2.25 us
    ppermute x1, waiting for transfers between devices, shards(): parts.append(lax.ppermute(part, 'mp', pairs))  0.99 us
    ppermute x1, waiting for transfers between devices, summed_over_groups(): received = lax.ppermute(value, 'mp', pairs)  0.84 us
    pallas_call x1, Pallas kernels, gram_of(): pl.pallas_call(functools.partial(gram_kernel, rows_each, len(parts)), out...  0.58 us
  transfers between devices with their start and end apart: 2, of which 2 were waited for; matrix products, arithmetic and copies ran while one was open for 0% of the time, Pallas kernels for 0%

profile of v20, /device:TPU:0, one launch (start us, length us, event | category | flops | bytes accessed | tf_op | source)
XLA Modules:
  0.0 25.7 jit_solution(5841768631870885894)
XLA Ops:
  0.0 7.8 %project.1.refs_1_ = f32[128,256]{1,0:T(8,128)S(1)} custom-call(bf16[128,14336]{1,0:T(8,128)(2,1)} %gate.1, bf16[128,14336]{1,0:T(8,128)(2,1)} %up.1, bf16[128,14336]{1,0:T(8,128)(2,1)} %grad.1, bf16[14336,128]{1,0:T(8,128)(2,1)} %proj_hidden.1, bf16[128,4096]{1,0:T(8,128)(2,1)} %tokens.1, bf16[128,4096]{1,0:T(8,128)(2,1)} %outer.1, bf16[4096,128]{1,0:T(8,128)(2,1)} %proj_model.1), custom_call_target="tpu_custom_call" | custom-call | tf_op jit(solution)/shard_map/project/pallas_call | solution.py:159
  7.8 0.5 %collective-permute-start.4 = (f32[128,256]{1,0:T(8,128)S(1)}, f32[128,256]{1,0:T(8,128)S(1)}, u32[]{:S(2)}, u32[]{:S(2)}) collective-permute-start(f32[128,256]{1,0:T(8,128)S(1)} %project.1.refs_1_), channel_id=1, source_target_pairs={{0,1},{1,0},{2,3},{3,2},{4,5},{5,4},{6,7},{7,6},{8,9},{9,8},{10,11... | collective-permute-start | bytes 393224 | tf_op jit(solution)/shard_map/ppermute | solution.py:375
  8.3 1.0 %collective-permute-done.4.refs_2_ = f32[128,256]{1,0:T(8,128)S(1)} collective-permute-done((f32[128,256]{1,0:T(8,128)S(1)}, f32[128,256]{1,0:T(8,128)S(1)}, u32[]{:S(2)}, u32[]{:S(2)}) %collective-permute-start.4) | collective-permute-done | bytes 131104 | tf_op jit(solution)/shard_map/ppermute | solution.py:375
  9.3 0.6 %gram.1 = (f32[1,64,128]{2,1,0:T(8,128)S(1)}, f32[32,128]{1,0:T(8,128)S(1)}) custom-call(s32[1]{0:T(128)} %bitcast.refs_0_, f32[128,256]{1,0:T(8,128)S(1)} %project.1.refs_1_, f32[128,256]{1,0:T(8,128)S(1)} %collective-permute-done.4.refs_2_), custom_call_target="tpu_custom_call" | custom-call | tf_op jit(solution)/shard_map/gram/pallas_call | solution.py:217
  9.9 12.8 %collective-permute-start.5 = (f32[32,128]{1,0:T(8,128)S(1)}, f32[32,128]{1,0:T(8,128)S(1)}, u32[]{:S(2)}, u32[]{:S(2)}) collective-permute-start(f32[32,128]{1,0:T(8,128)S(1)} %get-tuple-element.14), channel_id=1, source_target_pairs={{0,1},{1,0},{2,3},{3,2},{4,5},{5,4},{6,7},{7,6},{8,9},{9,8},{10,11... | collective-permute-start | bytes 49160 | tf_op jit(solution)/shard_map/ppermute | solution.py:359
  22.6 0.8 %collective-permute-done.5 = f32[32,128]{1,0:T(8,128)S(1)} collective-permute-done((f32[32,128]{1,0:T(8,128)S(1)}, f32[32,128]{1,0:T(8,128)S(1)}, u32[]{:S(2)}, u32[]{:S(2)}) %collective-permute-start.5) | collective-permute-done | bytes 16416 | tf_op jit(solution)/shard_map/ppermute | solution.py:359
  23.5 2.2 %whiten.1 = f32[1,64,64]{2,1,0:T(8,128)} custom-call(f32[1,64,128]{2,1,0:T(8,128)S(1)} %get-tuple-element.12.rows_ref, f32[32,128]{1,0:T(8,128)S(1)} %broadcast_select_fusion.gram_ref), custom_call_target="tpu_custom_call" | custom-call | tf_op jit(solution)/shard_map/whiten/pallas_call | solution.py:334
  (2 shorter events, 0.0 us)
Async XLA Ops:
  7.8 1.5 %collective-permute-start.4 = (f32[128,256]{1,0:T(8,128)S(1)}, f32[128,256]{1,0:T(8,128)S(1)}, u32[]{:S(2)}, u32[]{:S(2)}) collective-permute-start(f32[128,256]{1,0:T(8,128)S(1)} %project.1.refs_1_), channel_id=1, source_target_pairs={{0,1},{1,0},{2,3},{3,2},{4,5},{5,4},{6,7},{7,6},{8,9},{9,8},{10,11... | collective-permute-start | bytes 393224 | tf_op jit(solution)/shard_map/ppermute | solution.py:375
  9.9 13.6 %collective-permute-start.5 = (f32[32,128]{1,0:T(8,128)S(1)}, f32[32,128]{1,0:T(8,128)S(1)}, u32[]{:S(2)}, u32[]{:S(2)}) collective-permute-start(f32[32,128]{1,0:T(8,128)S(1)} %get-tuple-element.14), channel_id=1, source_target_pairs={{0,1},{1,0},{2,3},{3,2},{4,5},{5,4},{6,7},{7,6},{8,9},{9,8},{10,11... | collective-permute-start | bytes 49160 | tf_op jit(solution)/shard_map/ppermute | solution.py:359

commit v21 on v17

--- a/solution.py
+++ b/solution.py
@@ -248,72 +248,63 @@
             (k, m): down(first_slot + m, k) for k in range(height) for m in range(k, height)
         }
         rows = [down(first_slot + height, k) for k in range(height)]
-        ahead = None
-        if held + 1 < blocks:
-            ahead = [across(state[held + 1], base + k) for k in range(height)]
-        factors = {}
-        solved = [None] * height
+        nearby = range(held + 1, min(held + 3, blocks))
+        moving = [rows] + [
+            [across(state[other], base + k) for k in range(height)] for other in nearby
+        ]
+        block = jnp.zeros_like(own)
         for k in range(0, height, 2):
             first, cross, second = corner[k, k], corner[k, k + 1], corner[k + 1, k + 1]
-            determinant = first * second - cross * cross
-            inverse = pl.reciprocal(determinant, approx=True)
-            solved[k] = (second * rows[k] - cross * rows[k + 1]) * inverse
-            solved[k + 1] = (first * rows[k + 1] - cross * rows[k]) * inverse
-            for m in range(k + 2, height):
-                left, right = corner[k, m], corner[k + 1, m]
-                upper = second * left - cross * right
-                lower = first * right - cross * left
+            inverse = pl.reciprocal(first, approx=True)
+            other_inverse = first * pl.reciprocal(first * second - cross * cross, approx=True)
+            ratio = cross * inverse
+            for several in moving:
+                several[k + 1] = several[k + 1] - ratio * several[k]
+            later = range(k + 2, height)
+            upper = {m: corner[k, m] for m in later}
+            lower = {m: corner[k + 1, m] - ratio * corner[k, m] for m in later}
+            for m in later:
                 for n in range(m, height):
-                    taken = upper * corner[k, n] + lower * corner[k + 1, n]
-                    corner[m, n] = corner[m, n] - taken * inverse
-                factors[k, m], factors[k + 1, m] = upper * inverse, lower * inverse
-                for several in (rows, ahead):
-                    if several is not None:
-                        several[m] = several[m] - (
-                            factors[k, m] * several[k] + factors[k + 1, m] * several[k + 1]
-                        )
-        if ahead is not None:
-            taken = [ahead[k] * solved[k] for k in range(height)]
-            while len(taken) > 1:
-                taken = [left + right for left, right in zip(taken[::2], taken[1::2])]
-            state[held + 1] = state[held + 1] - taken[0]
-        if held + 2 < blocks:
-            back = list(solved)
-            for m in reversed(range(2, height)):
-                for k in range(m - m % 2):
-                    back[k] = back[k] - factors[k, m] * back[m]
-            near = state[held + 2]
-            taken = [across(near, base + k) * back[k] for k in range(height)]
-            while len(taken) > 1:
-                taken = [left + right for left, right in zip(taken[::2], taken[1::2])]
-            state[held + 2] = near - taken[0]
+                    corner[m, n] = (
+                        corner[m, n]
+                        - (upper[m] * upper[n]) * inverse
+                        - (lower[m] * lower[n]) * other_inverse
+                    )
+                for several in moving:
+                    several[m] = several[m] - (
+                        (upper[m] * inverse) * several[k]
+                        + (lower[m] * other_inverse) * several[k + 1]
+                    )
+            for which, other in enumerate(nearby):
+                columns = moving[1 + which]
+                state[other] = state[other] - (
+                    columns[k] * (inverse * rows[k])
+                    + columns[k + 1] * (other_inverse * rows[k + 1])
+                )
+            for m, pivot in ((k, inverse), (k + 1, other_inverse)):
+                block = jnp.where(sub == m, rows[m] * (pivot * lax.rsqrt(pivot)), block)
+        done.append(block)
         if held + 3 < blocks:
-            packed = back[0]
-            for k in range(1, height):
-                packed = jnp.where(sub == k, back[k], packed)
-            weights = [jnp.zeros_like(own)] * (2 * blocks)
-            weights[blocks + held] = packed
-            later = jnp.concatenate(state[held + 3 :], axis=0)
-            later = later - jnp.dot(
-                later,
-                jnp.concatenate(weights, axis=0),
+            far = (held + 3) * height
+            update = jnp.dot(
+                block.T[RANK + far :, :],
+                block,
                 precision=highest,
                 preferred_element_type=jnp.float32,
             )
             for other in range(held + 3, blocks):
-                at = (other - held - 3) * height
-                state[other] = later[at : at + height]
-        block = jnp.zeros_like(own)
-        for k in range(0, height, 2):
-            first, cross, second = corner[k, k], corner[k, k + 1], corner[k + 1, k + 1]
-            ratio = cross * pl.reciprocal(first, approx=True)
-            final = second - cross * ratio
-            block = jnp.where(sub == k, rows[k] * lax.rsqrt(first), block)
-            block = jnp.where(
-                sub == k + 1, (rows[k + 1] - ratio * rows[k]) * lax.rsqrt(final), block
-            )
-        done.append(block)
+                at = other * height - far
+                state[other] = state[other] - update[at : at + height]
     return done
+
+
+def scaled(joined):
+    lane = lanes_of(joined.shape)
+    row = lax.broadcasted_iota(jnp.int32, joined.shape, 0)
+    diagonal = jnp.where(lane == row + RANK, joined, 0.0)
+    down = lax.rsqrt(jnp.sum(diagonal, axis=1, keepdims=True))
+    along = lax.rsqrt(jnp.sum(diagonal, axis=0, keepdims=True))
+    return joined * down * jnp.where(lane < RANK, 1.0, along)
 
 
 def whiten_kernel(factor, rows_each, rows_ref, gram_ref, out_ref, spread):
@@ -321,7 +312,7 @@
     gram = jnp.concatenate([pltpu.roll(packed, RANK, 1), packed], axis=0)
     low = lanes_of((RANK, WIDE)) < RANK
     for example in range(rows_ref.shape[0]):
-        joined = jnp.where(low, rows_ref[example], gram)
+        joined = scaled(jnp.where(low, rows_ref[example], gram))
         done = eliminated([joined[at : at + 8] for at in range(0, RANK, 8)], spread)
         solved = (jnp.concatenate(done, axis=0) * factor).T
         out_ref[example] = solved[:rows_each, :]

time: 25.8 us -> 26.1 us (1.012)
  Pallas kernels: 10.5 us -> 10.9 us
    pallas_call x1, Pallas kernels: 2.25 us -> 2.62 us  [whiten(): pl.pallas_call(functools.partial(whiten_kernel, factor, rows_each), out_s...]
where the time goes in v21:
time: 26.1 us; the launch traced here: 26 us
  starting transfers between devices  13.3 us (51%)
  Pallas kernels  10.9 us (42%)
  waiting for transfers between devices  1.83 us (7%)
    ppermute x1, starting transfers between devices, summed_over_groups(): received = lax.ppermute(value, 'mp', pairs)  12.8 us
    pallas_call x1, Pallas kernels, project(): pl.pallas_call(project_kernel, out_shape=jax.ShapeDtypeStruct((rows, 2 *...  7.68 us
    pallas_call x1, Pallas kernels, whiten(): pl.pallas_call(functools.partial(whiten_kernel, factor, rows_each), out_s...  2.62 us
    ppermute x1, waiting for transfers between devices, shards(): parts.append(lax.ppermute(part, 'mp', pairs))  0.99 us
    ppermute x1, waiting for transfers between devices, summed_over_groups(): received = lax.ppermute(value, 'mp', pairs)  0.84 us
    pallas_call x1, Pallas kernels, gram_of(): pl.pallas_call(functools.partial(gram_kernel, rows_each, len(parts)), out...  0.58 us
  transfers between devices with their start and end apart: 2, of which 2 were waited for; matrix products, arithmetic and copies ran while one was open for 0% of the time, Pallas kernels for 0%

profile of v21, /device:TPU:0, one launch (start us, length us, event | category | flops | bytes accessed | tf_op | source)
XLA Modules:
  0.0 26.0 jit_solution(10701710101376649698)
XLA Ops:
  0.0 7.7 %project.1.refs_1_ = f32[128,256]{1,0:T(8,128)S(1)} custom-call(bf16[128,14336]{1,0:T(8,128)(2,1)} %gate.1, bf16[128,14336]{1,0:T(8,128)(2,1)} %up.1, bf16[128,14336]{1,0:T(8,128)(2,1)} %grad.1, bf16[14336,128]{1,0:T(8,128)(2,1)} %proj_hidden.1, bf16[128,4096]{1,0:T(8,128)(2,1)} %tokens.1, bf16[128,4096]{1,0:T(8,128)(2,1)} %outer.1, bf16[4096,128]{1,0:T(8,128)(2,1)} %proj_model.1), custom_call_target="tpu_custom_call" | custom-call | tf_op jit(solution)/shard_map/project/pallas_call | solution.py:156
  7.7 0.5 %collective-permute-start.4 = (f32[128,256]{1,0:T(8,128)S(1)}, f32[128,256]{1,0:T(8,128)S(1)}, u32[]{:S(2)}, u32[]{:S(2)}) collective-permute-start(f32[128,256]{1,0:T(8,128)S(1)} %project.1.refs_1_), channel_id=1, source_target_pairs={{0,1},{1,0},{2,3},{3,2},{4,5},{5,4},{6,7},{7,6},{8,9},{9,8},{10,11... | collective-permute-start | bytes 393224 | tf_op jit(solution)/shard_map/ppermute | solution.py:363
  8.2 1.0 %collective-permute-done.4.refs_2_ = f32[128,256]{1,0:T(8,128)S(1)} collective-permute-done((f32[128,256]{1,0:T(8,128)S(1)}, f32[128,256]{1,0:T(8,128)S(1)}, u32[]{:S(2)}, u32[]{:S(2)}) %collective-permute-start.4) | collective-permute-done | bytes 131104 | tf_op jit(solution)/shard_map/ppermute | solution.py:363
  9.2 0.6 %gram.1 = (f32[1,64,128]{2,1,0:T(8,128)S(1)}, f32[32,128]{1,0:T(8,128)S(1)}) custom-call(s32[1]{0:T(128)} %bitcast.refs_0_, f32[128,256]{1,0:T(8,128)S(1)} %project.1.refs_1_, f32[128,256]{1,0:T(8,128)S(1)} %collective-permute-done.4.refs_2_), custom_call_target="tpu_custom_call" | custom-call | tf_op jit(solution)/shard_map/gram/pallas_call | solution.py:214
  9.8 12.8 %collective-permute-start.5 = (f32[32,128]{1,0:T(8,128)S(1)}, f32[32,128]{1,0:T(8,128)S(1)}, u32[]{:S(2)}, u32[]{:S(2)}) collective-permute-start(f32[32,128]{1,0:T(8,128)S(1)} %get-tuple-element.14), channel_id=1, source_target_pairs={{0,1},{1,0},{2,3},{3,2},{4,5},{5,4},{6,7},{7,6},{8,9},{9,8},{10,11... | collective-permute-start | bytes 49160 | tf_op jit(solution)/shard_map/ppermute | solution.py:347
  22.5 0.8 %collective-permute-done.5 = f32[32,128]{1,0:T(8,128)S(1)} collective-permute-done((f32[32,128]{1,0:T(8,128)S(1)}, f32[32,128]{1,0:T(8,128)S(1)}, u32[]{:S(2)}, u32[]{:S(2)}) %collective-permute-start.5) | collective-permute-done | bytes 16416 | tf_op jit(solution)/shard_map/ppermute | solution.py:347
  23.4 2.6 %whiten.1 = f32[1,64,64]{2,1,0:T(8,128)} custom-call(f32[1,64,128]{2,1,0:T(8,128)S(1)} %get-tuple-element.12.rows_ref, f32[32,128]{1,0:T(8,128)S(1)} %broadcast_select_fusion.gram_ref), custom_call_target="tpu_custom_call" | custom-call | tf_op jit(solution)/shard_map/whiten/pallas_call | solution.py:322
  (2 shorter events, 0.0 us)
Async XLA Ops:
  7.7 1.5 %collective-permute-start.4 = (f32[128,256]{1,0:T(8,128)S(1)}, f32[128,256]{1,0:T(8,128)S(1)}, u32[]{:S(2)}, u32[]{:S(2)}) collective-permute-start(f32[128,256]{1,0:T(8,128)S(1)} %project.1.refs_1_), channel_id=1, source_target_pairs={{0,1},{1,0},{2,3},{3,2},{4,5},{5,4},{6,7},{7,6},{8,9},{9,8},{10,11... | collective-permute-start | bytes 393224 | tf_op jit(solution)/shard_map/ppermute | solution.py:363
  9.8 13.6 %collective-permute-start.5 = (f32[32,128]{1,0:T(8,128)S(1)}, f32[32,128]{1,0:T(8,128)S(1)}, u32[]{:S(2)}, u32[]{:S(2)}) collective-permute-start(f32[32,128]{1,0:T(8,128)S(1)} %get-tuple-element.14), channel_id=1, source_target_pairs={{0,1},{1,0},{2,3},{3,2},{4,5},{5,4},{6,7},{7,6},{8,9},{9,8},{10,11... | collective-permute-start | bytes 49160 | tf_op jit(solution)/shard_map/ppermute | solution.py:347

commit v22 on v21

--- a/solution.py
+++ b/solution.py
@@ -248,11 +248,11 @@
             (k, m): down(first_slot + m, k) for k in range(height) for m in range(k, height)
         }
         rows = [down(first_slot + height, k) for k in range(height)]
-        nearby = range(held + 1, min(held + 3, blocks))
+        nearby = range(held + 1, min(held + 2, blocks))
         moving = [rows] + [
             [across(state[other], base + k) for k in range(height)] for other in nearby
         ]
-        block = jnp.zeros_like(own)
+        block = packed = divided = jnp.zeros_like(own)
         for k in range(0, height, 2):
             first, cross, second = corner[k, k], corner[k, k + 1], corner[k + 1, k + 1]
             inverse = pl.reciprocal(first, approx=True)
@@ -283,16 +283,18 @@
                 )
             for m, pivot in ((k, inverse), (k + 1, other_inverse)):
                 block = jnp.where(sub == m, rows[m] * (pivot * lax.rsqrt(pivot)), block)
+                packed = jnp.where(sub == m, rows[m], packed)
+                divided = jnp.where(sub == m, rows[m] * pivot, divided)
         done.append(block)
-        if held + 3 < blocks:
-            far = (held + 3) * height
+        if held + 2 < blocks:
+            far = (held + 2) * height
             update = jnp.dot(
-                block.T[RANK + far :, :],
-                block,
+                packed.T[RANK + far :, :],
+                divided,
                 precision=highest,
                 preferred_element_type=jnp.float32,
             )
-            for other in range(held + 3, blocks):
+            for other in range(held + 2, blocks):
                 at = other * height - far
                 state[other] = state[other] - update[at : at + height]
     return done

time: 26.1 us -> 26.3 us (level)
  no operation moved by 1% of the time
where the time goes in v22:
time: 26.3 us; the launch traced here: 26.2 us
  starting transfers between devices  13.3 us (51%)
  Pallas kernels  11.1 us (42%)
  waiting for transfers between devices  1.83 us (7%)
    ppermute x1, starting transfers between devices, summed_over_groups(): received = lax.ppermute(value, 'mp', pairs)  12.8 us
    pallas_call x1, Pallas kernels, project(): pl.pallas_call(project_kernel, out_shape=jax.ShapeDtypeStruct((rows, 2 *...  7.68 us
    pallas_call x1, Pallas kernels, whiten(): pl.pallas_call(functools.partial(whiten_kernel, factor, rows_each), out_s...  2.82 us
    ppermute x1, waiting for transfers between devices, shards(): parts.append(lax.ppermute(part, 'mp', pairs))  0.99 us
    ppermute x1, waiting for transfers between devices, summed_over_groups(): received = lax.ppermute(value, 'mp', pairs)  0.84 us
    pallas_call x1, Pallas kernels, gram_of(): pl.pallas_call(functools.partial(gram_kernel, rows_each, len(parts)), out...  0.58 us
  transfers between devices with their start and end apart: 2, of which 2 were waited for; matrix products, arithmetic and copies ran while one was open for 0% of the time, Pallas kernels for 0%

profile of v22, /device:TPU:0, one launch (start us, length us, event | category | flops | bytes accessed | tf_op | source)
XLA Modules:
  0.0 26.2 jit_solution(13503689789751120304)
XLA Ops:
  0.0 7.7 %project.1.refs_1_ = f32[128,256]{1,0:T(8,128)S(1)} custom-call(bf16[128,14336]{1,0:T(8,128)(2,1)} %gate.1, bf16[128,14336]{1,0:T(8,128)(2,1)} %up.1, bf16[128,14336]{1,0:T(8,128)(2,1)} %grad.1, bf16[14336,128]{1,0:T(8,128)(2,1)} %proj_hidden.1, bf16[128,4096]{1,0:T(8,128)(2,1)} %tokens.1, bf16[128,4096]{1,0:T(8,128)(2,1)} %outer.1, bf16[4096,128]{1,0:T(8,128)(2,1)} %proj_model.1), custom_call_target="tpu_custom_call" | custom-call | tf_op jit(solution)/shard_map/project/pallas_call | solution.py:156
  7.7 0.5 %collective-permute-start.4 = (f32[128,256]{1,0:T(8,128)S(1)}, f32[128,256]{1,0:T(8,128)S(1)}, u32[]{:S(2)}, u32[]{:S(2)}) collective-permute-start(f32[128,256]{1,0:T(8,128)S(1)} %project.1.refs_1_), channel_id=1, source_target_pairs={{0,1},{1,0},{2,3},{3,2},{4,5},{5,4},{6,7},{7,6},{8,9},{9,8},{10,11... | collective-permute-start | bytes 393224 | tf_op jit(solution)/shard_map/ppermute | solution.py:365
  8.2 1.0 %collective-permute-done.4.refs_2_ = f32[128,256]{1,0:T(8,128)S(1)} collective-permute-done((f32[128,256]{1,0:T(8,128)S(1)}, f32[128,256]{1,0:T(8,128)S(1)}, u32[]{:S(2)}, u32[]{:S(2)}) %collective-permute-start.4) | collective-permute-done | bytes 131104 | tf_op jit(solution)/shard_map/ppermute | solution.py:365
  9.2 0.6 %gram.1 = (f32[1,64,128]{2,1,0:T(8,128)S(1)}, f32[32,128]{1,0:T(8,128)S(1)}) custom-call(s32[1]{0:T(128)} %bitcast.refs_0_, f32[128,256]{1,0:T(8,128)S(1)} %project.1.refs_1_, f32[128,256]{1,0:T(8,128)S(1)} %collective-permute-done.4.refs_2_), custom_call_target="tpu_custom_call" | custom-call | tf_op jit(solution)/shard_map/gram/pallas_call | solution.py:214
  9.8 12.8 %collective-permute-start.5 = (f32[32,128]{1,0:T(8,128)S(1)}, f32[32,128]{1,0:T(8,128)S(1)}, u32[]{:S(2)}, u32[]{:S(2)}) collective-permute-start(f32[32,128]{1,0:T(8,128)S(1)} %get-tuple-element.14), channel_id=1, source_target_pairs={{0,1},{1,0},{2,3},{3,2},{4,5},{5,4},{6,7},{7,6},{8,9},{9,8},{10,11... | collective-permute-start | bytes 49160 | tf_op jit(solution)/shard_map/ppermute | solution.py:349
  22.5 0.8 %collective-permute-done.5 = f32[32,128]{1,0:T(8,128)S(1)} collective-permute-done((f32[32,128]{1,0:T(8,128)S(1)}, f32[32,128]{1,0:T(8,128)S(1)}, u32[]{:S(2)}, u32[]{:S(2)}) %collective-permute-start.5) | collective-permute-done | bytes 16416 | tf_op jit(solution)/shard_map/ppermute | solution.py:349
  23.4 2.8 %whiten.1 = f32[1,64,64]{2,1,0:T(8,128)} custom-call(f32[1,64,128]{2,1,0:T(8,128)S(1)} %get-tuple-element.12.rows_ref, f32[32,128]{1,0:T(8,128)S(1)} %broadcast_select_fusion.gram_ref), custom_call_target="tpu_custom_call" | custom-call | tf_op jit(solution)/shard_map/whiten/pallas_call | solution.py:324
  (2 shorter events, 0.0 us)
Async XLA Ops:
  7.7 1.5 %collective-permute-start.4 = (f32[128,256]{1,0:T(8,128)S(1)}, f32[128,256]{1,0:T(8,128)S(1)}, u32[]{:S(2)}, u32[]{:S(2)}) collective-permute-start(f32[128,256]{1,0:T(8,128)S(1)} %project.1.refs_1_), channel_id=1, source_target_pairs={{0,1},{1,0},{2,3},{3,2},{4,5},{5,4},{6,7},{7,6},{8,9},{9,8},{10,11... | collective-permute-start | bytes 393224 | tf_op jit(solution)/shard_map/ppermute | solution.py:365
  9.8 13.6 %collective-permute-start.5 = (f32[32,128]{1,0:T(8,128)S(1)}, f32[32,128]{1,0:T(8,128)S(1)}, u32[]{:S(2)}, u32[]{:S(2)}) collective-permute-start(f32[32,128]{1,0:T(8,128)S(1)} %get-tuple-element.14), channel_id=1, source_target_pairs={{0,1},{1,0},{2,3},{3,2},{4,5},{5,4},{6,7},{7,6},{8,9},{9,8},{10,11... | collective-permute-start | bytes 49160 | tf_op jit(solution)/shard_map/ppermute | solution.py:349

commit v23 on v22

--- a/solution.py
+++ b/solution.py
@@ -248,7 +248,7 @@
             (k, m): down(first_slot + m, k) for k in range(height) for m in range(k, height)
         }
         rows = [down(first_slot + height, k) for k in range(height)]
-        nearby = range(held + 1, min(held + 2, blocks))
+        nearby = range(held + 1, min(held + 4, blocks))
         moving = [rows] + [
             [across(state[other], base + k) for k in range(height)] for other in nearby
         ]
@@ -286,15 +286,15 @@
                 packed = jnp.where(sub == m, rows[m], packed)
                 divided = jnp.where(sub == m, rows[m] * pivot, divided)
         done.append(block)
-        if held + 2 < blocks:
-            far = (held + 2) * height
+        if held + 4 < blocks:
+            far = (held + 4) * height
             update = jnp.dot(
                 packed.T[RANK + far :, :],
                 divided,
                 precision=highest,
                 preferred_element_type=jnp.float32,
             )
-            for other in range(held + 2, blocks):
+            for other in range(held + 4, blocks):
                 at = other * height - far
                 state[other] = state[other] - update[at : at + height]
     return done

time: 26.3 us -> 25.9 us (0.985)
  Pallas kernels: 11.1 us -> 10.6 us
    pallas_call x1, Pallas kernels: 2.82 us -> 2.35 us  [whiten(): pl.pallas_call(functools.partial(whiten_kernel, factor, rows_each), out_s...]
where the time goes in v23:
time: 25.9 us; the launch traced here: 25.7 us
  starting transfers between devices  13.3 us (51%)
  Pallas kernels  10.6 us (41%)
  waiting for transfers between devices  1.83 us (7%)
    ppermute x1, starting transfers between devices, summed_over_groups(): received = lax.ppermute(value, 'mp', pairs)  12.8 us
    pallas_call x1, Pallas kernels, project(): pl.pallas_call(project_kernel, out_shape=jax.ShapeDtypeStruct((rows, 2 *...  7.68 us
    pallas_call x1, Pallas kernels, whiten(): pl.pallas_call(functools.partial(whiten_kernel, factor, rows_each), out_s...  2.35 us
    ppermute x1, waiting for transfers between devices, shards(): parts.append(lax.ppermute(part, 'mp', pairs))  0.99 us
    ppermute x1, waiting for transfers between devices, summed_over_groups(): received = lax.ppermute(value, 'mp', pairs)  0.84 us
    pallas_call x1, Pallas kernels, gram_of(): pl.pallas_call(functools.partial(gram_kernel, rows_each, len(parts)), out...  0.58 us
  transfers between devices with their start and end apart: 2, of which 2 were waited for; matrix products, arithmetic and copies ran while one was open for 0% of the time, Pallas kernels for 0%

profile of v23, /device:TPU:0, one launch (start us, length us, event | category | flops | bytes accessed | tf_op | source)
XLA Modules:
  0.0 25.7 jit_solution(10292702785238404926)
XLA Ops:
  0.0 7.7 %project.1.refs_1_ = f32[128,256]{1,0:T(8,128)S(1)} custom-call(bf16[128,14336]{1,0:T(8,128)(2,1)} %gate.1, bf16[128,14336]{1,0:T(8,128)(2,1)} %up.1, bf16[128,14336]{1,0:T(8,128)(2,1)} %grad.1, bf16[14336,128]{1,0:T(8,128)(2,1)} %proj_hidden.1, bf16[128,4096]{1,0:T(8,128)(2,1)} %tokens.1, bf16[128,4096]{1,0:T(8,128)(2,1)} %outer.1, bf16[4096,128]{1,0:T(8,128)(2,1)} %proj_model.1), custom_call_target="tpu_custom_call" | custom-call | tf_op jit(solution)/shard_map/project/pallas_call | solution.py:156
  7.7 0.5 %collective-permute-start.4 = (f32[128,256]{1,0:T(8,128)S(1)}, f32[128,256]{1,0:T(8,128)S(1)}, u32[]{:S(2)}, u32[]{:S(2)}) collective-permute-start(f32[128,256]{1,0:T(8,128)S(1)} %project.1.refs_1_), channel_id=1, source_target_pairs={{0,1},{1,0},{2,3},{3,2},{4,5},{5,4},{6,7},{7,6},{8,9},{9,8},{10,11... | collective-permute-start | bytes 393224 | tf_op jit(solution)/shard_map/ppermute | solution.py:365
  8.2 1.0 %collective-permute-done.4.refs_2_ = f32[128,256]{1,0:T(8,128)S(1)} collective-permute-done((f32[128,256]{1,0:T(8,128)S(1)}, f32[128,256]{1,0:T(8,128)S(1)}, u32[]{:S(2)}, u32[]{:S(2)}) %collective-permute-start.4) | collective-permute-done | bytes 131104 | tf_op jit(solution)/shard_map/ppermute | solution.py:365
  9.2 0.6 %gram.1 = (f32[1,64,128]{2,1,0:T(8,128)S(1)}, f32[32,128]{1,0:T(8,128)S(1)}) custom-call(s32[1]{0:T(128)} %bitcast.refs_0_, f32[128,256]{1,0:T(8,128)S(1)} %project.1.refs_1_, f32[128,256]{1,0:T(8,128)S(1)} %collective-permute-done.4.refs_2_), custom_call_target="tpu_custom_call" | custom-call | tf_op jit(solution)/shard_map/gram/pallas_call | solution.py:214
  9.8 12.8 %collective-permute-start.5 = (f32[32,128]{1,0:T(8,128)S(1)}, f32[32,128]{1,0:T(8,128)S(1)}, u32[]{:S(2)}, u32[]{:S(2)}) collective-permute-start(f32[32,128]{1,0:T(8,128)S(1)} %get-tuple-element.14), channel_id=1, source_target_pairs={{0,1},{1,0},{2,3},{3,2},{4,5},{5,4},{6,7},{7,6},{8,9},{9,8},{10,11... | collective-permute-start | bytes 49160 | tf_op jit(solution)/shard_map/ppermute | solution.py:349
  22.5 0.8 %collective-permute-done.5 = f32[32,128]{1,0:T(8,128)S(1)} collective-permute-done((f32[32,128]{1,0:T(8,128)S(1)}, f32[32,128]{1,0:T(8,128)S(1)}, u32[]{:S(2)}, u32[]{:S(2)}) %collective-permute-start.5) | collective-permute-done | bytes 16416 | tf_op jit(solution)/shard_map/ppermute | solution.py:349
  23.4 2.4 %whiten.1 = f32[1,64,64]{2,1,0:T(8,128)} custom-call(f32[1,64,128]{2,1,0:T(8,128)S(1)} %get-tuple-element.12.rows_ref, f32[32,128]{1,0:T(8,128)S(1)} %broadcast_select_fusion.gram_ref), custom_call_target="tpu_custom_call" | custom-call | tf_op jit(solution)/shard_map/whiten/pallas_call | solution.py:324
  (2 shorter events, 0.0 us)
Async XLA Ops:
  7.7 1.5 %collective-permute-start.4 = (f32[128,256]{1,0:T(8,128)S(1)}, f32[128,256]{1,0:T(8,128)S(1)}, u32[]{:S(2)}, u32[]{:S(2)}) collective-permute-start(f32[128,256]{1,0:T(8,128)S(1)} %project.1.refs_1_), channel_id=1, source_target_pairs={{0,1},{1,0},{2,3},{3,2},{4,5},{5,4},{6,7},{7,6},{8,9},{9,8},{10,11... | collective-permute-start | bytes 393224 | tf_op jit(solution)/shard_map/ppermute | solution.py:365
  9.8 13.6 %collective-permute-start.5 = (f32[32,128]{1,0:T(8,128)S(1)}, f32[32,128]{1,0:T(8,128)S(1)}, u32[]{:S(2)}, u32[]{:S(2)}) collective-permute-start(f32[32,128]{1,0:T(8,128)S(1)} %get-tuple-element.14), channel_id=1, source_target_pairs={{0,1},{1,0},{2,3},{3,2},{4,5},{5,4},{6,7},{7,6},{8,9},{9,8},{10,11... | collective-permute-start | bytes 49160 | tf_op jit(solution)/shard_map/ppermute | solution.py:349

commit v24 on v23

--- a/solution.py
+++ b/solution.py
@@ -248,7 +248,7 @@
             (k, m): down(first_slot + m, k) for k in range(height) for m in range(k, height)
         }
         rows = [down(first_slot + height, k) for k in range(height)]
-        nearby = range(held + 1, min(held + 4, blocks))
+        nearby = range(held + 1, min(held + 5, blocks))
         moving = [rows] + [
             [across(state[other], base + k) for k in range(height)] for other in nearby
         ]
@@ -286,15 +286,15 @@
                 packed = jnp.where(sub == m, rows[m], packed)
                 divided = jnp.where(sub == m, rows[m] * pivot, divided)
         done.append(block)
-        if held + 4 < blocks:
-            far = (held + 4) * height
+        if held + 5 < blocks:
+            far = (held + 5) * height
             update = jnp.dot(
                 packed.T[RANK + far :, :],
                 divided,
                 precision=highest,
                 preferred_element_type=jnp.float32,
             )
-            for other in range(held + 4, blocks):
+            for other in range(held + 5, blocks):
                 at = other * height - far
                 state[other] = state[other] - update[at : at + height]
     return done

time: 25.9 us -> 25.9 us (level)
  no operation moved by 1% of the time
where the time goes in v24:
time: 25.9 us; the launch traced here: 25.8 us
  starting transfers between devices  13.3 us (51%)
  Pallas kernels  10.7 us (41%)
  waiting for transfers between devices  1.83 us (7%)
    ppermute x1, starting transfers between devices, summed_over_groups(): received = lax.ppermute(value, 'mp', pairs)  12.8 us
    pallas_call x1, Pallas kernels, project(): pl.pallas_call(project_kernel, out_shape=jax.ShapeDtypeStruct((rows, 2 *...  7.68 us
    pallas_call x1, Pallas kernels, whiten(): pl.pallas_call(functools.partial(whiten_kernel, factor, rows_each), out_s...  2.41 us
    ppermute x1, waiting for transfers between devices, shards(): parts.append(lax.ppermute(part, 'mp', pairs))  0.99 us
    ppermute x1, waiting for transfers between devices, summed_over_groups(): received = lax.ppermute(value, 'mp', pairs)  0.84 us
    pallas_call x1, Pallas kernels, gram_of(): pl.pallas_call(functools.partial(gram_kernel, rows_each, len(parts)), out...  0.58 us
  transfers between devices with their start and end apart: 2, of which 2 were waited for; matrix products, arithmetic and copies ran while one was open for 0% of the time, Pallas kernels for 0%

profile of v24, /device:TPU:0, one launch (start us, length us, event | category | flops | bytes accessed | tf_op | source)
XLA Modules:
  0.0 25.8 jit_solution(7419627259879141640)
XLA Ops:
  0.0 7.7 %project.1.refs_1_ = f32[128,256]{1,0:T(8,128)S(1)} custom-call(bf16[128,14336]{1,0:T(8,128)(2,1)} %gate.1, bf16[128,14336]{1,0:T(8,128)(2,1)} %up.1, bf16[128,14336]{1,0:T(8,128)(2,1)} %grad.1, bf16[14336,128]{1,0:T(8,128)(2,1)} %proj_hidden.1, bf16[128,4096]{1,0:T(8,128)(2,1)} %tokens.1, bf16[128,4096]{1,0:T(8,128)(2,1)} %outer.1, bf16[4096,128]{1,0:T(8,128)(2,1)} %proj_model.1), custom_call_target="tpu_custom_call" | custom-call | tf_op jit(solution)/shard_map/project/pallas_call | solution.py:156
  7.7 0.5 %collective-permute-start.4 = (f32[128,256]{1,0:T(8,128)S(1)}, f32[128,256]{1,0:T(8,128)S(1)}, u32[]{:S(2)}, u32[]{:S(2)}) collective-permute-start(f32[128,256]{1,0:T(8,128)S(1)} %project.1.refs_1_), channel_id=1, source_target_pairs={{0,1},{1,0},{2,3},{3,2},{4,5},{5,4},{6,7},{7,6},{8,9},{9,8},{10,11... | collective-permute-start | bytes 393224 | tf_op jit(solution)/shard_map/ppermute | solution.py:365
  8.2 1.0 %collective-permute-done.4.refs_2_ = f32[128,256]{1,0:T(8,128)S(1)} collective-permute-done((f32[128,256]{1,0:T(8,128)S(1)}, f32[128,256]{1,0:T(8,128)S(1)}, u32[]{:S(2)}, u32[]{:S(2)}) %collective-permute-start.4) | collective-permute-done | bytes 131104 | tf_op jit(solution)/shard_map/ppermute | solution.py:365
  9.2 0.6 %gram.1 = (f32[1,64,128]{2,1,0:T(8,128)S(1)}, f32[32,128]{1,0:T(8,128)S(1)}) custom-call(s32[1]{0:T(128)} %bitcast.refs_0_, f32[128,256]{1,0:T(8,128)S(1)} %project.1.refs_1_, f32[128,256]{1,0:T(8,128)S(1)} %collective-permute-done.4.refs_2_), custom_call_target="tpu_custom_call" | custom-call | tf_op jit(solution)/shard_map/gram/pallas_call | solution.py:214
  9.8 12.8 %collective-permute-start.5 = (f32[32,128]{1,0:T(8,128)S(1)}, f32[32,128]{1,0:T(8,128)S(1)}, u32[]{:S(2)}, u32[]{:S(2)}) collective-permute-start(f32[32,128]{1,0:T(8,128)S(1)} %get-tuple-element.14), channel_id=1, source_target_pairs={{0,1},{1,0},{2,3},{3,2},{4,5},{5,4},{6,7},{7,6},{8,9},{9,8},{10,11... | collective-permute-start | bytes 49160 | tf_op jit(solution)/shard_map/ppermute | solution.py:349
  22.5 0.8 %collective-permute-done.5 = f32[32,128]{1,0:T(8,128)S(1)} collective-permute-done((f32[32,128]{1,0:T(8,128)S(1)}, f32[32,128]{1,0:T(8,128)S(1)}, u32[]{:S(2)}, u32[]{:S(2)}) %collective-permute-start.5) | collective-permute-done | bytes 16416 | tf_op jit(solution)/shard_map/ppermute | solution.py:349
  23.4 2.4 %whiten.1 = f32[1,64,64]{2,1,0:T(8,128)} custom-call(f32[1,64,128]{2,1,0:T(8,128)S(1)} %get-tuple-element.12.rows_ref, f32[32,128]{1,0:T(8,128)S(1)} %broadcast_select_fusion.gram_ref), custom_call_target="tpu_custom_call" | custom-call | tf_op jit(solution)/shard_map/whiten/pallas_call | solution.py:324
  (2 shorter events, 0.0 us)
Async XLA Ops:
  7.7 1.5 %collective-permute-start.4 = (f32[128,256]{1,0:T(8,128)S(1)}, f32[128,256]{1,0:T(8,128)S(1)}, u32[]{:S(2)}, u32[]{:S(2)}) collective-permute-start(f32[128,256]{1,0:T(8,128)S(1)} %project.1.refs_1_), channel_id=1, source_target_pairs={{0,1},{1,0},{2,3},{3,2},{4,5},{5,4},{6,7},{7,6},{8,9},{9,8},{10,11... | collective-permute-start | bytes 393224 | tf_op jit(solution)/shard_map/ppermute | solution.py:365
  9.8 13.6 %collective-permute-start.5 = (f32[32,128]{1,0:T(8,128)S(1)}, f32[32,128]{1,0:T(8,128)S(1)}, u32[]{:S(2)}, u32[]{:S(2)}) collective-permute-start(f32[32,128]{1,0:T(8,128)S(1)} %get-tuple-element.14), channel_id=1, source_target_pairs={{0,1},{1,0},{2,3},{3,2},{4,5},{5,4},{6,7},{7,6},{8,9},{9,8},{10,11... | collective-permute-start | bytes 49160 | tf_op jit(solution)/shard_map/ppermute | solution.py:349

commit v25 on v23

--- a/solution.py
+++ b/solution.py
@@ -242,8 +242,8 @@
         own = state[held]
         first_slot = (held % 2) * (height + 1)
         for k in range(height):
-            spread[first_slot + k] = across(own, base + k)
-        spread[first_slot + height] = own
+            spread[first_slot + k, :height] = across(own, base + k)
+        spread[first_slot + height, :height] = own
         corner = {
             (k, m): down(first_slot + m, k) for k in range(height) for m in range(k, height)
         }
@@ -326,7 +326,7 @@
         out_shape=jax.ShapeDtypeStruct((rows.shape[0], rows_each, RANK), jnp.float32),
         in_specs=[whole_vmem] * 2,
         out_specs=whole_vmem,
-        scratch_shapes=[pltpu.VMEM((18, 8, WIDE), jnp.float32)],
+        scratch_shapes=[pltpu.VMEM((18, 16, WIDE), jnp.float32)],
         compiler_params=small,
         name="whiten",
     )(rows, gram)

time: 25.9 us -> 25.9 us (level)
  no operation moved by 1% of the time
where the time goes in v25:
time: 25.9 us; the launch traced here: 25.7 us
  starting transfers between devices  13.3 us (51%)
  Pallas kernels  10.6 us (41%)
  waiting for transfers between devices  1.83 us (7%)
    ppermute x1, starting transfers between devices, summed_over_groups(): received = lax.ppermute(value, 'mp', pairs)  12.8 us
    pallas_call x1, Pallas kernels, project(): pl.pallas_call(project_kernel, out_shape=jax.ShapeDtypeStruct((rows, 2 *...  7.68 us
    pallas_call x1, Pallas kernels, whiten(): pl.pallas_call(functools.partial(whiten_kernel, factor, rows_each), out_s...  2.35 us
    ppermute x1, waiting for transfers between devices, shards(): parts.append(lax.ppermute(part, 'mp', pairs))  0.99 us
    ppermute x1, waiting for transfers between devices, summed_over_groups(): received = lax.ppermute(value, 'mp', pairs)  0.84 us
    pallas_call x1, Pallas kernels, gram_of(): pl.pallas_call(functools.partial(gram_kernel, rows_each, len(parts)), out...  0.58 us
  transfers between devices with their start and end apart: 2, of which 2 were waited for; matrix products, arithmetic and copies ran while one was open for 0% of the time, Pallas kernels for 0%

profile of v25, /device:TPU:0, one launch (start us, length us, event | category | flops | bytes accessed | tf_op | source)
XLA Modules:
  0.0 25.7 jit_solution(5301674888671935390)
XLA Ops:
  0.0 7.7 %project.1.refs_1_ = f32[128,256]{1,0:T(8,128)S(1)} custom-call(bf16[128,14336]{1,0:T(8,128)(2,1)} %gate.1, bf16[128,14336]{1,0:T(8,128)(2,1)} %up.1, bf16[128,14336]{1,0:T(8,128)(2,1)} %grad.1, bf16[14336,128]{1,0:T(8,128)(2,1)} %proj_hidden.1, bf16[128,4096]{1,0:T(8,128)(2,1)} %tokens.1, bf16[128,4096]{1,0:T(8,128)(2,1)} %outer.1, bf16[4096,128]{1,0:T(8,128)(2,1)} %proj_model.1), custom_call_target="tpu_custom_call" | custom-call | tf_op jit(solution)/shard_map/project/pallas_call | solution.py:156
  7.7 0.5 %collective-permute-start.4 = (f32[128,256]{1,0:T(8,128)S(1)}, f32[128,256]{1,0:T(8,128)S(1)}, u32[]{:S(2)}, u32[]{:S(2)}) collective-permute-start(f32[128,256]{1,0:T(8,128)S(1)} %project.1.refs_1_), channel_id=1, source_target_pairs={{0,1},{1,0},{2,3},{3,2},{4,5},{5,4},{6,7},{7,6},{8,9},{9,8},{10,11... | collective-permute-start | bytes 393224 | tf_op jit(solution)/shard_map/ppermute | solution.py:365
  8.2 1.0 %collective-permute-done.4.refs_2_ = f32[128,256]{1,0:T(8,128)S(1)} collective-permute-done((f32[128,256]{1,0:T(8,128)S(1)}, f32[128,256]{1,0:T(8,128)S(1)}, u32[]{:S(2)}, u32[]{:S(2)}) %collective-permute-start.4) | collective-permute-done | bytes 131104 | tf_op jit(solution)/shard_map/ppermute | solution.py:365
  9.2 0.6 %gram.1 = (f32[1,64,128]{2,1,0:T(8,128)S(1)}, f32[32,128]{1,0:T(8,128)S(1)}) custom-call(s32[1]{0:T(128)} %bitcast.refs_0_, f32[128,256]{1,0:T(8,128)S(1)} %project.1.refs_1_, f32[128,256]{1,0:T(8,128)S(1)} %collective-permute-done.4.refs_2_), custom_call_target="tpu_custom_call" | custom-call | tf_op jit(solution)/shard_map/gram/pallas_call | solution.py:214
  9.8 12.8 %collective-permute-start.5 = (f32[32,128]{1,0:T(8,128)S(1)}, f32[32,128]{1,0:T(8,128)S(1)}, u32[]{:S(2)}, u32[]{:S(2)}) collective-permute-start(f32[32,128]{1,0:T(8,128)S(1)} %get-tuple-element.14), channel_id=1, source_target_pairs={{0,1},{1,0},{2,3},{3,2},{4,5},{5,4},{6,7},{7,6},{8,9},{9,8},{10,11... | collective-permute-start | bytes 49160 | tf_op jit(solution)/shard_map/ppermute | solution.py:349
  22.5 0.8 %collective-permute-done.5 = f32[32,128]{1,0:T(8,128)S(1)} collective-permute-done((f32[32,128]{1,0:T(8,128)S(1)}, f32[32,128]{1,0:T(8,128)S(1)}, u32[]{:S(2)}, u32[]{:S(2)}) %collective-permute-start.5) | collective-permute-done | bytes 16416 | tf_op jit(solution)/shard_map/ppermute | solution.py:349
  23.4 2.4 %whiten.1 = f32[1,64,64]{2,1,0:T(8,128)} custom-call(f32[1,64,128]{2,1,0:T(8,128)S(1)} %get-tuple-element.12.rows_ref, f32[32,128]{1,0:T(8,128)S(1)} %broadcast_select_fusion.gram_ref), custom_call_target="tpu_custom_call" | custom-call | tf_op jit(solution)/shard_map/whiten/pallas_call | solution.py:324
  (2 shorter events, 0.0 us)
Async XLA Ops:
  7.7 1.5 %collective-permute-start.4 = (f32[128,256]{1,0:T(8,128)S(1)}, f32[128,256]{1,0:T(8,128)S(1)}, u32[]{:S(2)}, u32[]{:S(2)}) collective-permute-start(f32[128,256]{1,0:T(8,128)S(1)} %project.1.refs_1_), channel_id=1, source_target_pairs={{0,1},{1,0},{2,3},{3,2},{4,5},{5,4},{6,7},{7,6},{8,9},{9,8},{10,11... | collective-permute-start | bytes 393224 | tf_op jit(solution)/shard_map/ppermute | solution.py:365
  9.8 13.6 %collective-permute-start.5 = (f32[32,128]{1,0:T(8,128)S(1)}, f32[32,128]{1,0:T(8,128)S(1)}, u32[]{:S(2)}, u32[]{:S(2)}) collective-permute-start(f32[32,128]{1,0:T(8,128)S(1)} %get-tuple-element.14), channel_id=1, source_target_pairs={{0,1},{1,0},{2,3},{3,2},{4,5},{5,4},{6,7},{7,6},{8,9},{9,8},{10,11... | collective-permute-start | bytes 49160 | tf_op jit(solution)/shard_map/ppermute | solution.py:349
